TPU v7x, 32 devices: a whole 2x2x4 slice. The times are simulated.
32 devices in a mesh: rep: 8 (over z, x), tp: 4 (over y, core).
Axes of the slice: x: 2, y: 2, z: 4, core: 2. Of those that a mesh axis runs over, the one named last changes fastest.
Arguments:
- tokens: bfloat16 [64, 256, 3584], P('rep', 'tp'), may hold values from -6 to 6
- seg_replica: int32 [32, 1], replicated, may hold values from 0 to 7; in each aligned block of 32 rows (0 to 31, 32 to 63, ...) at most 8 rows name the same one
- doc_of_segment: int32 [32], replicated, may hold values from 0 to 15, never falling along the last dimension, each value on 1 to 4 neighbouring positions
- doc_owner: int32 [16, 1], replicated, may hold values from 0 to 7; in each aligned block of 16 rows (0 to 15, 16 to 31, ...) at most 4 rows name the same one
- enc_gain: float32 [3584], replicated, may hold values from 0.5 to 1.5
- enc_query: bfloat16 [3584, 512], P(None, 'tp'), may hold values from -3.5 to 3.5
- enc_keyvalue: bfloat16 [3584, 2, 128], P(None, None, 'tp'), may hold values from -1 to 1
- enc_output: bfloat16 [512, 3584], P('tp'), may hold values from -0.25 to 0.25
- doc_proj: bfloat16 [3584, 256], P('tp'), may hold values from -0.09375 to 0.09375
- doc_gain: float32 [256], replicated, may hold values from 0.5 to 1.5
- doc_qkv: bfloat16 [256, 3, 256], P(None, None, 'tp'), may hold values from -4 to 4
Outputs:
- doc_context: bfloat16 [32, 4, 256], P('rep', None, 'tp')
Inputs may be any that keep to these rules, and one draw needn't show every extreme that they name: `seg_replica`: no replica is assigned more than 8 segments, one replica exactly 8, every replica at least one. `doc_of_segment`: Non-decreasing; every document has 1 to 4 consecutive segments, some document exactly 4. `doc_owner`: no replica owns more than 4 documents, one exactly 4, every replica at least one.
All inputs are finite; a program needn't handle non-finite values.
Results may differ from a plain program's by a relative error of at most 0.014.
Values may be sent and summed in bfloat16 or wider, within the bound.
No kernel may reach another device: no remote copies, remote signals or barrier semaphores. Data moves between devices by JAX's collectives and lax.ppermute only.
A program may use at most 64 MiB of HBM per device.

v0:
```python
import jax
import jax.numpy as jnp
from jax import lax
from jax.sharding import PartitionSpec as P

CAP = 8
DOC_MOST = 4
OWN_DOCS = 4


def swapped(block, axis, apart):
    count = lax.axis_size(axis)
    route = []
    for low in range(count):
        high = low | 1 << apart
        if high != low and high < count:
            route += [(low, high), (high, low)]
    return lax.ppermute(block, axis, route)


def slot_table(seg_replica):
    replica_of = seg_replica[:, 0]
    order = jnp.arange(replica_of.shape[0], dtype=jnp.int32)
    earlier = (replica_of[None, :] == replica_of[:, None]) & (order[None, :] < order[:, None])
    return replica_of * CAP + jnp.sum(earlier.astype(jnp.int32), axis=1)


def owner_rows(doc_of_segment, doc_owner):
    owner_of = doc_owner[:, 0]
    doc_ids = jnp.arange(owner_of.shape[0], dtype=jnp.int32)
    earlier = (owner_of[None, :] == owner_of[:, None]) & (doc_ids[None, :] < doc_ids[:, None])
    doc_rank = jnp.sum(earlier.astype(jnp.int32), axis=1)
    start_of = jnp.sum((doc_of_segment[None, :] < doc_ids[:, None]).astype(jnp.int32), axis=1)
    matches = doc_of_segment[:, None] == doc_ids[None, :]
    seg_owner = jnp.sum(jnp.where(matches, owner_of[None, :], 0), axis=1)
    seg_rank = jnp.sum(jnp.where(matches, doc_rank[None, :], 0), axis=1)
    seg_start = jnp.sum(jnp.where(matches, start_of[None, :], 0), axis=1)
    position = jnp.arange(doc_of_segment.shape[0], dtype=jnp.int32) - seg_start
    return seg_owner * (OWN_DOCS * DOC_MOST) + seg_rank * DOC_MOST + position


def sorted_concatenation(own_part, other_part, lower_first):
    forward_encoder = jnp.concatenate([own_part, other_part], axis=2)
    backward = jnp.concatenate([other_part, own_part], axis=2)
    return jnp.where(lower_first, forward_encoder, backward)


def local(
    tokens,
    seg_replica,
    doc_of_segment,
    doc_owner,
    enc_gain,
    enc_query,
    enc_keyvalue,
    enc_output,
    doc_proj,
    doc_gain,
    doc_qkv,
):
    rep_index = lax.axis_index("rep")
    tp_index = lax.axis_index("tp")
    global_slot = slot_table(seg_replica)
    raw_float = tokens.astype(jnp.float32)
    normed = (
        raw_float
        * lax.rsqrt(jnp.mean(raw_float * raw_float, axis=-1, keepdims=True) + 1e-06)
        * enc_gain
    ).astype(jnp.bfloat16)
    head_dim = enc_query.shape[1]
    kv_width = enc_keyvalue.shape[2]
    joined_weights = jnp.concatenate(
        [enc_query, enc_keyvalue.reshape(enc_keyvalue.shape[0], 2 * kv_width)], axis=1
    )
    projected = jnp.einsum(
        "spd,dc->spc",
        lax.all_gather(normed, "tp", axis=1, tiled=True),
        joined_weights,
        preferred_element_type=jnp.float32,
    ).astype(jnp.bfloat16)
    queries = projected[:, :, :head_dim]
    seg_slots = projected.shape[0]
    length = projected.shape[1]
    kv_local = projected[:, :, head_dim:].reshape(seg_slots, length, 1, 2 * kv_width)
    partner = swapped(kv_local, "tp", 0)
    kv_two = sorted_concatenation(kv_local, partner, tp_index % 2 == 0)
    far_pair = swapped(kv_two, "tp", 1)
    kv_four = sorted_concatenation(kv_two, far_pair, tp_index // 2 % 2 == 0)
    kv_four = kv_four.reshape(seg_slots, length, 4, 2, kv_width)
    key_rows = kv_four[:, :, :, 0, :].reshape(seg_slots, length, head_dim)
    value_rows = kv_four[:, :, :, 1, :].reshape(seg_slots, length, head_dim)
    scores = jnp.einsum(
        "sqe,ske->sqk", queries, key_rows, preferred_element_type=jnp.float32
    ) * head_dim ** (-0.5)
    attn_weights = jax.nn.softmax(scores, axis=-1).astype(jnp.bfloat16)
    context = jnp.einsum(
        "sqk,ske->sqe", attn_weights, value_rows, preferred_element_type=jnp.float32
    ).astype(jnp.bfloat16)
    context_mean = jnp.mean(context.astype(jnp.float32), axis=1)
    own_sum = jnp.sum(raw_float, axis=1) / length
    partial_pool = own_sum + jnp.dot(
        context_mean, enc_output.astype(jnp.float32), precision=lax.Precision.HIGHEST
    )
    pooled = lax.psum_scatter(partial_pool, "tp", scatter_dimension=1, tiled=True).astype(
        jnp.bfloat16
    )
    everywhere = lax.all_gather(pooled, "rep", axis=0, tiled=True)
    by_segment = everywhere[global_slot]
    row_of = owner_rows(doc_of_segment, doc_owner)
    owned_rows = OWN_DOCS * DOC_MOST
    wanted = rep_index * owned_rows + jnp.arange(owned_rows, dtype=jnp.int32)
    matches = row_of[None, :] == wanted[:, None]
    selected = jnp.dot(
        matches.astype(jnp.bfloat16), by_segment, preferred_element_type=jnp.float32
    ).astype(jnp.bfloat16)
    filled = jnp.sum(matches.astype(jnp.float32), axis=1)
    doc_partial = jnp.dot(selected, doc_proj, preferred_element_type=jnp.float32)
    doc_first = lax.psum(doc_partial, "tp")
    doc_normed = (
        doc_first
        * lax.rsqrt(jnp.mean(doc_first * doc_first, axis=-1, keepdims=True) + 1e-06)
        * doc_gain
    ).astype(jnp.bfloat16)
    doc_head = doc_qkv.shape[2]
    document_projected_rows = jnp.einsum(
        "rc,cte->tre", doc_normed, doc_qkv, preferred_element_type=jnp.float32
    ).astype(jnp.bfloat16)
    document_projected_rows = document_projected_rows.reshape(3, OWN_DOCS, DOC_MOST, doc_head)
    doc_scores = jnp.einsum(
        "xjf,xlf->xjl",
        document_projected_rows[0],
        document_projected_rows[1],
        preferred_element_type=jnp.float32,
    ) * doc_head ** (-0.5)
    filled_rows = filled.reshape(OWN_DOCS, DOC_MOST)
    diagonal_mask = jnp.eye(DOC_MOST, dtype=bool)
    allowed = (filled_rows[:, None, :] > 0.5) | diagonal_mask[None, :, :]
    doc_scores = jnp.where(allowed, doc_scores, -1e30)
    document_weight_matrix = jax.nn.softmax(doc_scores, axis=-1).astype(jnp.bfloat16)
    doc_context = jnp.einsum(
        "lyw,lwn->lyn",
        document_weight_matrix,
        document_projected_rows[2],
        preferred_element_type=jnp.float32,
    )
    return (doc_context * filled_rows[:, :, None]).astype(jnp.bfloat16)


def solution(mesh):
    in_specs = (
        P("rep", "tp", None),
        P(),
        P(),
        P(),
        P(),
        P(None, "tp"),
        P(None, None, "tp"),
        P("tp", None),
        P("tp", None),
        P(),
        P(None, None, "tp"),
    )
    out_specs = P("rep", None, "tp")
    return jax.shard_map(local, mesh=mesh, in_specs=in_specs, out_specs=out_specs, check_vma=False)
```

profile of v0, /device:TPU:0, one launch (start us, length us, event | category | flops | bytes accessed | tf_op | source)
XLA Modules:
  0.0 215.1 jit_solution(13629368546128226890)
XLA Ops:
  6.5 3.9 %fusion.2 = (f32[8,64]{1,0:T(8,128)S(1)}, f32[8,3584]{1,0:T(8,128)S(1)}) fusion(bf16[8,64,3584]{2,1,0:T(8,128)(2,1)} %param.11), kind=kLoop, calls=%fused_computation.6 | loop fusion | flops 7310848 | bytes 3786752 | tf_op jit(solution)/shard_map/reduce_sum | solution.py:67
  10.5 3.0 %fusion.4 = bf16[8,64,3584]{2,1,0:T(8,128)(2,1)} fusion(bf16[8,64,3584]{2,1,0:T(8,128)(2,1)S(1)} %copy-done.1, f32[3584]{0:T(1024)S(1)} %copy-done.6, f32[8,64]{1,0:T(8,128)S(1)} %add_rsqrt_fusion), kind=kLoop, calls=%fused_computation.8 | loop fusion | flops 7340032 | bytes 7356416 | tf_op jit(solution)/shard_map/convert_element_type | solution.py:69
  13.6 1.1 copy-done.2
  14.6 0.5 copy.26
  15.8 94.6 %all-gather.2.cloned.1.call-done = bf16[8,256,3584]{2,1,0:T(8,128)(2,1)} async-done(((bf16[8,64,3584]{2,1,0:T(8,128)(2,1)}), bf16[8,256,3584]{2,1,0:T(8,128)(2,1)}) %all-gather.2.cloned.1.call-update) | async-done | bytes 14680080 | tf_op jit(solution)/shard_map/all_gather | solution.py:77
  110.4 10.0 %convolution_convert_fusion = bf16[8,256,192]{1,2,0:T(8,128)(2,1)S(1)} fusion(bf16[8,256,3584]{2,1,0:T(8,128)(2,1)} %all-gather.2.cloned.1.call-done, bf16[3584,64]{0,1:T(8,128)(2,1)S(1)} %bitcast.52, bf16[3584,128]{0,1:T(8,128)(2,1)S(1)} %copy.26), kind=kOutput, calls=%fused_computation.14 | convolution fusion | flops 2821718016 | bytes 16842752 | tf_op jit(solution)/shard_map/spd,dc->spc/dot_general | solution.py:75
  120.5 0.8 copy-done.4
  121.3 0.3 collective-permute-start
  121.6 1.3 collective-permute-done
  122.9 0.4 collective-permute-start.1
  123.3 0.2 fusion.26
  123.7 13.4 %collective-permute-done.1 = bf16[8,256,2,64]{1,3,0,2:T(8,128)(2,1)S(1)} collective-permute-done((bf16[8,256,2,64]{1,3,0,2:T(8,128)(2,1)S(1)}, bf16[8,256,2,64]{1,3,0,2:T(8,128)(2,1)S(1)}, u32[]{:S(2)}, u32[]{:S(2)}) %collective-permute-start.1) | collective-permute-done | bytes 524320 | tf_op jit(solution)/shard_map/ppermute | solution.py:18
  137.1 0.4 maximum_select_fusion
  137.6 1.0 copy-done.5
  138.6 2.2 %fusion.48 = (f32[8,256]{1,0:T(8,128)S(1)}, f32[8,256,256]{1,2,0:T(8,128)}) fusion(bf16[8,256,128]{1,2,0:T(8,128)(2,1)S(1)} %bitcast.44, bf16[8,256,192]{1,2,0:T(8,128)(2,1)S(1)} %copy-done.5), kind=kOutput, calls=%fused_computation.82 | convolution fusion | flops 135790848 | bytes 3153920 | tf_op jit(solution)/shard_map/sub | solution.py:95
  140.8 2.5 %fusion.9 = f32[8,128]{1,0:T(8,128)S(1)} fusion(bf16[8,256,128]{1,2,0:T(8,128)(2,1)S(1)} %bitcast.43, f32[8,256,256]{1,2,0:T(8,128)} %get-tuple-element.20, f32[8,256]{1,0:T(8,128)S(1)} %get-tuple-element.19), kind=kOutput, calls=%fused_computation.20 | convolution fusion | flops 136051712 | bytes 2633728 | tf_op jit(solution)/shard_map/sqk,ske->sqe/dot_general | solution.py:96
  143.3 1.1 convolution_add_fusion
  144.6 19.6 %reduce-scatter.2.cloned.1.call-done = f32[8,896]{1,0:T(8,128)} async-done(((f32[8,3584]{1,0:T(8,128)}), f32[8,896]{1,0:T(8,128)}) %reduce-scatter.2.cloned.1.call-update) | async-done | bytes 28688 | tf_op jit(solution)/shard_map/reduce_scatter | solution.py:104
  164.2 0.8 convert_element_type.62
  164.9 30.6 %all_gather.7 = bf16[64,896]{1,0:T(8,128)(2,1)S(1)} all-gather(bf16[8,896]{1,0:T(8,128)(2,1)S(1)} %convert_element_type.62), channel_id=1, replica_groups=mesh['rep'=8,'tp'=4] {'rep'}, dimensions={0}, use_global_device_ids=true | all-gather | bytes 129024 | tf_op jit(solution)/shard_map/all_gather | solution.py:107
  195.6 0.6 gather_fusion
  196.2 0.3 fusion.10
  196.5 10.3 %psum.7 = f32[16,256]{1,0:T(8,128)S(1)} all-reduce(f32[16,256]{1,0:T(8,128)S(1)} %fusion.10), channel_id=1, replica_groups=mesh['rep'=8,'tp'=4] {'tp'}, use_global_device_ids=true, to_apply=%region_13.14 | all-reduce | flops 4096 | bytes 32768 | tf_op jit(solution)/shard_map/psum | solution.py:118
  207.4 0.8 fusion.15
  (50 shorter events, 1.8 us)
Async XLA Ops:
  6.5 136.8 %copy-start = (bf16[128,3584]{1,0:T(8,128)(2,1)S(1)}, bf16[128,3584]{1,0:T(8,128)(2,1)}, u32[]{:S(2)}) copy-start(bf16[128,3584]{1,0:T(8,128)(2,1)} %param.18) | copy-start | bytes 2752516
  6.5 3.9 %copy-start.6 = (f32[3584]{0:T(1024)S(1)}, f32[3584]{0:T(1024)}, u32[]{:S(2)}) copy-start(f32[3584]{0:T(1024)} %param.15) | copy-start | bytes 43012
  6.5 103.8 %all-gather.2.cloned.1.call-start = ((), (), s32[]{:S(2)}) async-start(), calls=%async_computation.1 | async-start | bytes 18350080 | tf_op jit(solution)/shard_map/all_gather | solution.py:77
  6.5 3.9 %copy-start.1 = (bf16[8,64,3584]{2,1,0:T(8,128)(2,1)S(1)}, bf16[8,64,3584]{2,1,0:T(8,128)(2,1)}, u32[]{:S(2)}) copy-start(bf16[8,64,3584]{2,1,0:T(8,128)(2,1)} %param.11) | copy-start | bytes 11010052
  13.5 1.2 copy-start.2
  13.5 1.7 copy-start.8
  13.5 1.8 copy-start.12
  13.5 2.0 copy-start.7
  13.5 96.9 %copy-start.9 = (bf16[3584,2,32]{0,2,1:T(8,128)(2,1)S(1)}, bf16[3584,2,32]{0,2,1:T(8,128)(2,1)}, u32[]{:S(2)}) copy-start(bf16[3584,2,32]{0,2,1:T(8,128)(2,1)} %param.17) | copy-start | bytes 1376260
  13.5 150.7 %reduce-scatter.2.cloned.1.call-start = ((), (), s32[]{:S(2)}) async-start(), calls=%async_computation.2 | async-start | bytes 143360 | tf_op jit(solution)/shard_map/reduce_scatter | solution.py:104
  120.4 0.9 copy-start.4
  121.3 1.5 collective-permute-start
  122.9 14.2 %collective-permute-start.1 = (bf16[8,256,2,64]{1,3,0,2:T(8,128)(2,1)S(1)}, bf16[8,256,2,64]{1,3,0,2:T(8,128)(2,1)S(1)}, u32[]{:S(2)}, u32[]{:S(2)}) collective-permute-start(bf16[8,256,2,64]{1,3,0,2:T(8,128)(2,1)S(1)} %maximum_select_fusion.1), channel_id=1, source_target_pairs={{0,2},{2,0},{1,3},{3,1},{4,6},{6,4},{5,7},{7,5},{8,10},{10,8},{9,1... | collective-permute-start | bytes 1572872 | tf_op jit(solution)/shard_map/ppermute | solution.py:18
  137.5 1.1 copy-start.5
  140.8 55.4 %copy-start.3 = (bf16[896,256]{1,0:T(8,128)(2,1)S(1)}, bf16[896,256]{1,0:T(8,128)(2,1)}, u32[]{:S(2)}) copy-start(bf16[896,256]{1,0:T(8,128)(2,1)} %param.19) | copy-start | bytes 1376260
  143.3 63.6 %copy-start.10 = (bf16[256,3,64]{0,2,1:T(8,128)(2,1)S(1)}, bf16[256,3,64]{0,2,1:T(8,128)(2,1)}, u32[]{:S(2)}) copy-start(bf16[256,3,64]{0,2,1:T(8,128)(2,1)} %param.21) | copy-start | bytes 294916
  143.3 63.6 %copy-start.11 = (f32[256]{0:T(256)S(1)}, f32[256]{0:T(256)}, u32[]{:S(2)}) copy-start(f32[256]{0:T(256)} %param.20) | copy-start | bytes 3076
Sparse Core Ops, SparseCore 0:
  13.6 96.7 all-gather.1
  144.6 19.5 reduce-scatter.1
where the time goes:
time: 215 us
  waiting for transfers between devices  129 us (60%)
  blocking collectives  40.9 us (19%)
  matrix products  17.4 us (8%)
  between operations  13.6 us (6%)
  other arithmetic  9.17 us (4%)
  local copies, waits for them, and re-layouts  4.34 us (2%)
    all_gather x1, waiting for transfers between devices, local(): lax.all_gather(normed, 'tp', axis=1, tiled=True)  94.6 us
    all_gather x1, blocking collectives, local(): everywhere = lax.all_gather(pooled, 'rep', axis=0, tiled=True)  30.6 us
    reduce_scatter x1, waiting for transfers between devices, local(): lax.psum_scatter(partial_pool, 'tp', scatter_dimension=1, tiled=True)  19.6 us
    ppermute x2, waiting for transfers between devices, swapped(): return lax.ppermute(block, axis, route)  14.7 us
    psum x1, blocking collectives, local(): doc_first = lax.psum(doc_partial, 'tp')  10.3 us
    dot_general x1, matrix products, local(): jnp.einsum('spd,dc->spc', lax.all_gather(normed, 'tp', axis=1, tiled=True...  10 us
  transfers between devices with their start and end apart: 4, of which 4 were waited for; matrix products, arithmetic and copies ran while one was open for 1% of the time, Pallas kernels for 0%

commit v1 on v0

v1 whole, which is shorter than its diff:
```python
import functools

import jax
import jax.numpy as jnp
from jax import lax
from jax.experimental import pallas as pl
from jax.experimental.pallas import tpu as pltpu
from jax.sharding import PartitionSpec as P

CAP = 8
DOC_MOST = 4
OWN_DOCS = 4
F32 = jnp.float32
BF16 = jnp.bfloat16
HIGH = lax.Precision.HIGHEST


def flipped(block, axis, mask):
    count = lax.axis_size(axis)
    return lax.ppermute(block, axis, [(i, i ^ mask) for i in range(count)])


def masks_of(count):
    masks = [0]
    bit = count // 2
    while bit:
        masks = masks + [m | bit for m in masks]
        bit //= 2
    return masks


def tp_blocks(block, count):
    blocks = [block]
    bit = count // 2
    while bit:
        blocks = blocks + [flipped(b, "tp", bit) for b in blocks]
        bit //= 2
    return blocks


def slot_table(seg_replica):
    replica_of = seg_replica[:, 0]
    order = jnp.arange(replica_of.shape[0], dtype=jnp.int32)
    earlier = (replica_of[None, :] == replica_of[:, None]) & (order[None, :] < order[:, None])
    return replica_of, jnp.sum(earlier.astype(jnp.int32), axis=1)


def owner_rows(doc_of_segment, doc_owner):
    owner_of = doc_owner[:, 0]
    doc_ids = jnp.arange(owner_of.shape[0], dtype=jnp.int32)
    earlier = (owner_of[None, :] == owner_of[:, None]) & (doc_ids[None, :] < doc_ids[:, None])
    doc_rank = jnp.sum(earlier.astype(jnp.int32), axis=1)
    start_of = jnp.sum((doc_of_segment[None, :] < doc_ids[:, None]).astype(jnp.int32), axis=1)
    matches = doc_of_segment[:, None] == doc_ids[None, :]
    seg_owner = jnp.sum(jnp.where(matches, owner_of[None, :], 0), axis=1)
    seg_rank = jnp.sum(jnp.where(matches, doc_rank[None, :], 0), axis=1)
    seg_start = jnp.sum(jnp.where(matches, start_of[None, :], 0), axis=1)
    position = jnp.arange(doc_of_segment.shape[0], dtype=jnp.int32) - seg_start
    return seg_owner * (OWN_DOCS * DOC_MOST) + seg_rank * DOC_MOST + position


def attention_kernel(group, head_dim, length, q_ref, kv_ref, w2_ref, xp_ref, out_ref, ctx_ref):
    slots, tokens, width = q_ref.shape
    heads = width // head_dim
    kv_heads = heads // group
    for s in range(slots):
        q = q_ref[s]
        for g in range(kv_heads):
            rows = jnp.concatenate(
                [q[:, h * head_dim:(h + 1) * head_dim] for h in range(g * group, (g + 1) * group)], axis=0
            )
            keys = kv_ref[:, s, :, g * 2 * head_dim:(g * 2 + 1) * head_dim].reshape(-1, head_dim)
            values = kv_ref[:, s, :, (g * 2 + 1) * head_dim:(g * 2 + 2) * head_dim].reshape(-1, head_dim)
            scores = lax.dot_general(
                rows, keys, (((1,), (1,)), ((), ())), preferred_element_type=F32
            ) * head_dim ** (-0.5)
            e = jnp.exp(scores - jnp.max(scores, axis=1, keepdims=True))
            probs = e * (1.0 / jnp.sum(e, axis=1, keepdims=True))
            weight = jnp.sum(probs.reshape(group, tokens, -1), axis=1)
            context = jnp.dot(weight, values.astype(F32), preferred_element_type=F32, precision=HIGH)
            for j in range(group):
                h = g * group + j
                ctx_ref[s:s + 1, h * head_dim:(h + 1) * head_dim] = context[j:j + 1] * (1.0 / length)
    out_ref[...] = xp_ref[...] + jnp.dot(
        ctx_ref[...], w2_ref[...].astype(F32), preferred_element_type=F32, precision=HIGH
    )


def document_kernel(rows_ref, sel_ref, allow_ref, fill_ref, gain_ref, qkv_ref, out_ref):
    docs, most, head = out_ref.shape
    first = jnp.dot(sel_ref[...], rows_ref[...], preferred_element_type=F32, precision=HIGH)
    scale = lax.rsqrt(jnp.mean(first * first, axis=-1, keepdims=True) + 1e-06)
    normed = (first * scale * gain_ref[...]).astype(BF16)
    q, k, v = (
        jnp.dot(normed, qkv_ref[i], preferred_element_type=F32).astype(BF16) for i in range(3)
    )
    scores = lax.dot_general(
        q, k, (((1,), (1,)), ((), ())), preferred_element_type=F32
    ) * head ** (-0.5)
    scores = jnp.where(allow_ref[...] > 0.5, scores, -1e30)
    e = jnp.exp(scores - jnp.max(scores, axis=1, keepdims=True))
    probs = (e / jnp.sum(e, axis=1, keepdims=True)).astype(BF16)
    context = jnp.dot(probs, v, preferred_element_type=F32) * fill_ref[...]
    for d in range(docs):
        out_ref[d] = context[d * most:(d + 1) * most].astype(BF16)


def local(
    tokens,
    seg_replica,
    doc_of_segment,
    doc_owner,
    enc_gain,
    enc_query,
    enc_keyvalue,
    enc_output,
    doc_proj,
    doc_gain,
    doc_qkv,
):
    n_rep, n_tp = lax.axis_size("rep"), lax.axis_size("tp")
    rep_index = lax.axis_index("rep")
    tp_index = lax.axis_index("tp")
    slots, own_tokens, width = tokens.shape
    length = own_tokens * n_tp
    head_dim = enc_query.shape[1]
    kv_width = enc_keyvalue.shape[2]
    group = head_dim // kv_width
    block = doc_proj.shape[0]
    doc_width = doc_proj.shape[1]
    masks = masks_of(n_tp)

    kv_weights = enc_keyvalue.reshape(width, 2 * kv_width)
    kv_all = jnp.concatenate(tp_blocks(kv_weights, n_tp), axis=1)
    q_blocks = tp_blocks(enc_query, n_tp)

    raw = tokens.astype(F32)
    normed = (
        raw * lax.rsqrt(jnp.mean(raw * raw, axis=-1, keepdims=True) + 1e-06) * enc_gain
    ).astype(BF16).reshape(slots * own_tokens, width)

    kv = jnp.dot(normed, kv_all, preferred_element_type=F32).astype(BF16)
    column = jnp.arange(2 * kv_width * n_tp, dtype=jnp.int32)
    mask_of = jnp.array(masks, jnp.int32)[column // (2 * kv_width)]
    inner = column % (2 * kv_width)
    target = (
        (mask_of // group) * (2 * head_dim)
        + (inner // kv_width) * head_dim
        + ((tp_index ^ mask_of) % group) * kv_width
        + inner % kv_width
    )
    place = (target[:, None] == column[None, :]).astype(BF16)
    kv = jnp.dot(kv, place, preferred_element_type=F32).astype(BF16)
    kv = kv.reshape(slots, own_tokens, kv.shape[1])
    kv_tokens = jnp.stack(tp_blocks(kv, n_tp), axis=0)

    half = doc_width // 2
    parity = rep_index % 2
    proj_half = lax.dynamic_slice_in_dim(doc_proj, parity * half, half, axis=1)
    proj_blocks = tp_blocks(proj_half, n_tp)
    w2_half = jnp.zeros((head_dim, half), F32)
    for mask, part in zip(masks, proj_blocks):
        piece = lax.dynamic_slice_in_dim(enc_output, (tp_index ^ mask) * block, block, axis=1)
        w2_half = w2_half + jnp.dot(piece, part, preferred_element_type=F32)
    w2_half = w2_half.astype(BF16)
    w2_other = flipped(w2_half, "rep", 1)
    w2_own = jnp.concatenate(
        [jnp.where(parity == 0, w2_half, w2_other), jnp.where(parity == 0, w2_other, w2_half)], axis=1
    )
    w2 = jnp.concatenate(tp_blocks(w2_own, n_tp), axis=0)

    sums = jnp.sum(raw, axis=1) * (1.0 / length)
    mine = sums.reshape(slots, n_tp, block)
    bit = n_tp // 2
    while bit:
        low = lax.dynamic_slice_in_dim(mine, (tp_index // bit % 2) * bit, bit, axis=1)
        far = lax.dynamic_slice_in_dim(mine, (1 - tp_index // bit % 2) * bit, bit, axis=1)
        mine = low + flipped(far, "tp", bit)
        bit //= 2
    mean_part = jnp.dot(mine.reshape(slots, block), doc_proj.astype(F32), precision=HIGH)

    queries = jnp.concatenate(
        [jnp.dot(normed, w, preferred_element_type=F32).astype(BF16) for w in q_blocks], axis=1
    ).reshape(slots, own_tokens, head_dim * n_tp)

    part = pl.pallas_call(
        functools.partial(attention_kernel, group, head_dim, length),
        out_shape=jax.ShapeDtypeStruct((slots, doc_width), F32),
        scratch_shapes=[pltpu.VMEM((slots, head_dim * n_tp), F32)],
        compiler_params=pltpu.CompilerParams(vmem_limit_bytes=40 * 2**20),
    )(queries, kv_tokens, w2, mean_part)

    bit = 1
    while bit < n_tp:
        part = part + flipped(part, "tp", bit)
        bit *= 2
    bit = 1
    while bit < n_rep:
        part = jnp.concatenate([part, flipped(part, "rep", bit)], axis=0)
        bit *= 2

    replica_of, rank = slot_table(seg_replica)
    row_of = owner_rows(doc_of_segment, doc_owner)
    owned = OWN_DOCS * DOC_MOST
    wanted = rep_index * owned + jnp.arange(owned, dtype=jnp.int32)
    matches = (row_of[None, :] == wanted[:, None]).astype(F32)
    at_slot = (replica_of ^ rep_index) * CAP + rank
    holds = (at_slot[:, None] == jnp.arange(n_rep * CAP, dtype=jnp.int32)[None, :]).astype(F32)
    select = jnp.dot(matches, holds)
    filled = jnp.sum(matches, axis=1)
    row = jnp.arange(owned, dtype=jnp.int32)
    same_doc = row[:, None] // DOC_MOST == row[None, :] // DOC_MOST
    allowed = same_doc & ((filled[None, :] > 0.5) | (row[:, None] == row[None, :]))

    return pl.pallas_call(
        document_kernel,
        out_shape=jax.ShapeDtypeStruct((OWN_DOCS, DOC_MOST, doc_qkv.shape[2]), BF16),
    )(
        part,
        select,
        allowed.astype(F32),
        filled[:, None],
        doc_gain[None, :],
        jnp.transpose(doc_qkv, (1, 0, 2)),
    )


def solution(mesh):
    in_specs = (
        P("rep", "tp", None),
        P(),
        P(),
        P(),
        P(),
        P(None, "tp"),
        P(None, None, "tp"),
        P("tp", None),
        P("tp", None),
        P(),
        P(None, None, "tp"),
    )
    out_specs = P("rep", None, "tp")
    return jax.shard_map(local, mesh=mesh, in_specs=in_specs, out_specs=out_specs, check_vma=False)
```

time: 215 us -> 96.1 us (0.45)
  waiting for transfers between devices: 129 us -> 34.2 us
  blocking collectives: 40.9 us -> 0 us
  starting transfers between devices: 0.68 us -> 21.1 us
  between operations: 13.6 us -> 0.42 us
  Pallas kernels: 0 us -> 6.66 us
    all_gather x1 -> x0, waiting for transfers between devices: 94.6 us -> none  [local(): lax.all_gather(normed, 'tp', axis=1, tiled=True)]
    all_gather x1 -> x0, blocking collectives: 30.6 us -> none  [local(): everywhere = lax.all_gather(pooled, 'rep', axis=0, tiled=True)]
    ppermute x2 -> x23, starting transfers between devices: 0.64 us -> 21.1 us  [flipped(): return lax.ppermute(block, axis, [(i, i ^ mask) for i in range(count)])]
    reduce_scatter x1 -> x0, waiting for transfers between devices: 19.6 us -> none  [local(): lax.psum_scatter(partial_pool, 'tp', scatter_dimension=1, tiled=True)]
    ppermute x2 -> x23, waiting for transfers between devices: 14.7 us -> 34.2 us  [flipped(): return lax.ppermute(block, axis, [(i, i ^ mask) for i in range(count)])]
    psum x1 -> x0, blocking collectives: 10.3 us -> none  [local(): doc_first = lax.psum(doc_partial, 'tp')]
    pallas_call x0 -> x2, Pallas kernels: none -> 6.66 us  [the longest x1 4.24 us: local(): pl.pallas_call(functools.partial(attention_kernel, group, head_dim, lengt...]
    dot_general x7 -> x11, matrix products: 15 us -> 18 us  [the longest x4 10.5 us: local(): jnp.dot(normed, w, preferred_element_type=F32).astype(BF16)]
  transfers between devices with their start and end apart: 4 -> 23, of which waited for: 4 -> 7; matrix products, arithmetic and copies ran while one was open for 1% -> 29% of each run, Pallas kernels for 0% -> 0%
where the time goes in v1:
time: 96.1 us; the launch traced here: 95.7 us
  waiting for transfers between devices  34.2 us (36%)
  starting transfers between devices  21.1 us (22%)
  matrix products  18 us (19%)
  other arithmetic  10.2 us (11%)
  Pallas kernels  6.66 us (7%)
  local copies, waits for them, and re-layouts  5.12 us (5%)
    ppermute x23, waiting for transfers between devices, flipped(): return lax.ppermute(block, axis, [(i, i ^ mask) for i in range(count)])  34.2 us
    ppermute x23, starting transfers between devices, flipped(): return lax.ppermute(block, axis, [(i, i ^ mask) for i in range(count)])  21.1 us
    dot_general x4, matrix products, local(): jnp.dot(normed, w, preferred_element_type=F32).astype(BF16)  10.5 us
    pallas_call x1, Pallas kernels, local(): pl.pallas_call(functools.partial(attention_kernel, group, head_dim, lengt...  4.24 us
    dot_general x1, matrix products, local(): kv = jnp.dot(kv, place, preferred_element_type=F32).astype(BF16)  3.87 us
    reduce_sum x1, other arithmetic, local(): sums = jnp.sum(raw, axis=1) * (1.0 / length)  3.72 us
    convert_element_type x1, other arithmetic, local(): normed = (raw * lax.rsqrt(jnp.mean(raw * raw, axis=-1, keepdims=True) + 1...  3.21 us
    unnamed x27, local copies, waits for them, and re-layouts  2.63 us
  transfers between devices with their start and end apart: 23, of which 7 were waited for; matrix products, arithmetic and copies ran while one was open for 29% of the time, Pallas kernels for 0%

profile of v1, /device:TPU:0, one launch (start us, length us, event | category | flops | bytes accessed | tf_op | source)
XLA Modules:
  0.0 95.7 jit_solution(14656405074207694661)
XLA Ops:
  0.0 3.0 %collective-permute-start.3 = (bf16[3584,64]{0,1:T(8,128)(2,1)}, bf16[3584,64]{0,1:T(8,128)(2,1)}, u32[]{:S(2)}, u32[]{:S(2)}) collective-permute-start(bf16[3584,64]{0,1:T(8,128)(2,1)} %bitcast.61), channel_id=1, source_target_pairs={{0,2},{1,3},{2,0},{3,1},{4,6},{5,7},{6,4},{7,5},{8,10},{9,11},{10,... | collective-permute-start | bytes 1376264 | tf_op jit(solution)/shard_map/ppermute | solution.py:20
  4.1 1.9 %collective-permute-start.9 = (bf16[896,128]{1,0:T(8,128)(2,1)S(1)}, bf16[896,128]{1,0:T(8,128)(2,1)}, u32[]{:S(2)}, u32[]{:S(2)}) collective-permute-start(bf16[896,128]{1,0:T(8,128)(2,1)S(1)} %constant_dynamic-slice_fusion.2), channel_id=1, source_target_pairs={{0,2},{1,3},{2,0},{3,1},{4,6},{5,7},{6,4},{7,5},{8,10},{9,11},{10,... | collective-permute-start | bytes 688136 | tf_op jit(solution)/shard_map/ppermute | solution.py:20
  6.0 3.7 %convert_reduce_fusion = (f32[8,3584]{1,0:T(8,128)S(1)}, f32[8,64]{1,0:T(8,128)S(1)}) fusion(bf16[8,64,3584]{2,1,0:T(8,128)(2,1)} %param.12), kind=kLoop, calls=%fused_computation | loop fusion | flops 7310848 | bytes 3786752 | tf_op jit(solution)/shard_map/reduce_sum | solution.py:172
  10.7 3.2 %fusion.2 = bf16[8,64,3584]{2,1,0:T(8,128)(2,1)S(1)} fusion(bf16[8,64,3584]{2,1,0:T(8,128)(2,1)} %param.12, f32[3584]{0:T(1024)S(1)} %copy-done.9, f32[8,64]{1,0:T(8,128)S(1)} %add_rsqrt_fusion), kind=kLoop, calls=%fused_computation.5 | loop fusion | flops 7340032 | bytes 7356416 | tf_op jit(solution)/shard_map/convert_element_type | solution.py:140
  14.0 1.8 %copy-done.1 = bf16[8,64,3584]{2,1,0:T(8,128)(2,1)} copy-done((bf16[8,64,3584]{2,1,0:T(8,128)(2,1)}, bf16[8,64,3584]{2,1,0:T(8,128)(2,1)S(1)}, u32[]{:S(2)}) %copy-start.1) | copy-done | bytes 3670040
  15.7 2.0 %convolution_convert_fusion.4 = bf16[512,128]{0,1:T(8,128)(2,1)} fusion(bf16[512,3584]{1,0:T(8,128)(2,1)S(1)} %bitcast.40, bf16[3584,128]{1,0:T(8,128)(2,1)S(1)} %copy-done.4), kind=kOutput, calls=%fused_computation.19 | convolution fusion | flops 469827584 | bytes 4718592 | tf_op jit(solution)/shard_map/dot_general | solution.py:183
  18.6 21.0 %collective-permute-done.16 = f32[8,2,896]{2,0,1:T(8,128)} collective-permute-done((f32[8,2,896]{2,0,1:T(8,128)}, f32[8,2,896]{2,0,1:T(8,128)}, u32[]{:S(2)}, u32[]{:S(2)}) %collective-permute-start.16) | collective-permute-done | bytes 57376 | tf_op jit(solution)/shard_map/ppermute | solution.py:20
  42.7 1.8 %collective-permute-start.12 = (bf16[128,128]{1,0:T(8,128)(2,1)S(1)}, bf16[128,128]{1,0:T(8,128)(2,1)S(1)}, u32[]{:S(2)}, u32[]{:S(2)}) collective-permute-start(bf16[128,128]{1,0:T(8,128)(2,1)S(1)} %fusion.16), channel_id=1, source_target_pairs={{0,4},{4,0},{8,12},{12,8},{16,20},{20,16},{24,28},{28,24},{1,5},{5... | collective-permute-start | bytes 98312 | tf_op jit(solution)/shard_map/ppermute | solution.py:20
  46.7 1.8 %collective-permute-start.13 = (bf16[128,256]{1,0:T(8,128)(2,1)S(1)}, bf16[128,256]{1,0:T(8,128)(2,1)S(1)}, u32[]{:S(2)}, u32[]{:S(2)}) collective-permute-start(bf16[128,256]{1,0:T(8,128)(2,1)S(1)} %pad_maximum_fusion.3), channel_id=1, source_target_pairs={{0,2},{1,3},{2,0},{3,1},{4,6},{5,7},{6,4},{7,5},{8,10},{9,11},{10,... | collective-permute-start | bytes 196616 | tf_op jit(solution)/shard_map/ppermute | solution.py:20
  48.5 2.5 %collective-permute-done.13 = bf16[128,256]{1,0:T(8,128)(2,1)S(1)} collective-permute-done((bf16[128,256]{1,0:T(8,128)(2,1)S(1)}, bf16[128,256]{1,0:T(8,128)(2,1)S(1)}, u32[]{:S(2)}, u32[]{:S(2)}) %collective-permute-start.13) | collective-permute-done | bytes 65568 | tf_op jit(solution)/shard_map/ppermute | solution.py:20
  52.8 3.9 %convolution_convert_fusion = bf16[512,256]{1,0:T(8,128)(2,1)S(1)} fusion(bf16[512,3584]{1,0:T(8,128)(2,1)} %bitcast.41, bf16[3584,64]{0,1:T(8,128)(2,1)} %collective-permute-done.5, bf16[3584,64]{0,1:T(8,128)(2,1)} %collective-permute-done.4, bf16[3584,64]{0,1:T(8,128)(2,1)} %collective-permute-done.3, bf16[3584,64]{0,1:T(8,128)(2,1)} %bitcast.63, ...), kind=kOutput, calls=%fused_computation.15 | convolution fusion | flops 1014300672 | bytes 5768192 | tf_op jit(solution)/shard_map/dot_general | solution.py:153
  56.7 1.8 %collective-permute-start.6 = (bf16[8,64,256]{2,1,0:T(8,128)(2,1)S(1)}, bf16[8,64,256]{2,1,0:T(8,128)(2,1)S(1)}, u32[]{:S(2)}, u32[]{:S(2)}) collective-permute-start(bf16[8,64,256]{2,1,0:T(8,128)(2,1)S(1)} %bitcast.48), channel_id=1, source_target_pairs={{0,2},{1,3},{2,0},{3,1},{4,6},{5,7},{6,4},{7,5},{8,10},{9,11},{10,... | collective-permute-start | bytes 786440 | tf_op jit(solution)/shard_map/ppermute | solution.py:20
  58.7 3.4 %convolution_convert_fusion.3 = bf16[512,128]{0,1:T(8,128)(2,1)S(1)} fusion(bf16[512,3584]{1,0:T(8,128)(2,1)} %bitcast.42, bf16[3584,128]{1,0:T(8,128)(2,1)S(1)} %collective-permute-done), kind=kOutput, calls=%fused_computation.18 | convolution fusion | flops 469827584 | bytes 4718592 | tf_op jit(solution)/shard_map/dot_general | solution.py:183
  62.1 3.4 %collective-permute-done.6 = bf16[8,64,256]{2,1,0:T(8,128)(2,1)S(1)} collective-permute-done((bf16[8,64,256]{2,1,0:T(8,128)(2,1)S(1)}, bf16[8,64,256]{2,1,0:T(8,128)(2,1)S(1)}, u32[]{:S(2)}, u32[]{:S(2)}) %collective-permute-start.6) | collective-permute-done | bytes 262176 | tf_op jit(solution)/shard_map/ppermute | solution.py:20
  65.4 2.5 %convolution_convert_fusion.2 = bf16[512,128]{0,1:T(8,128)(2,1)S(1)} fusion(bf16[512,3584]{1,0:T(8,128)(2,1)S(1)} %bitcast.43, bf16[3584,128]{1,0:T(8,128)(2,1)} %collective-permute-done.1), kind=kOutput, calls=%fused_computation.17 | convolution fusion | flops 469827584 | bytes 4718592 | tf_op jit(solution)/shard_map/dot_general | solution.py:183
  68.2 2.6 %convolution_convert_fusion.1 = bf16[512,128]{0,1:T(8,128)(2,1)S(1)} fusion(bf16[512,3584]{1,0:T(8,128)(2,1)S(1)} %bitcast.44, bf16[3584,128]{1,0:T(8,128)(2,1)} %collective-permute-done.2), kind=kOutput, calls=%fused_computation.16 | convolution fusion | flops 469827584 | bytes 4718592 | tf_op jit(solution)/shard_map/dot_general | solution.py:183
  71.0 4.2 %shard_map.118 = f32[8,256]{1,0:T(8,128)S(1)} custom-call(bf16[8,64,512]{2,1,0:T(8,128)(2,1)S(1)} %bitcast.39, bf16[4,8,64,256]{3,2,1,0:T(8,128)(2,1)S(1)} %pad_maximum_fusion.kv_ref, bf16[512,256]{1,0:T(8,128)(2,1)S(1)} %pad_maximum_fusion.2.w2_ref, f32[8,256]{1,0:T(8,128)S(1)} %fusion.23.xp_ref), custom_call_target="tpu_custom_call" | custom-call | tf_op jit(solution)/shard_map/pallas_call | solution.py:186
  76.6 1.7 %collective-permute-start.19 = (f32[8,256]{1,0:T(8,128)S(1)}, f32[8,256]{1,0:T(8,128)S(1)}, u32[]{:S(2)}, u32[]{:S(2)}) collective-permute-start(f32[8,256]{1,0:T(8,128)S(1)} %add.224), channel_id=1, source_target_pairs={{0,2},{1,3},{2,0},{3,1},{4,6},{5,7},{6,4},{7,5},{8,10},{9,11},{10,... | collective-permute-start | bytes 24584 | tf_op jit(solution)/shard_map/ppermute | solution.py:20
  78.5 1.7 %collective-permute-done.19 = f32[8,256]{1,0:T(8,128)S(1)} collective-permute-done((f32[8,256]{1,0:T(8,128)S(1)}, f32[8,256]{1,0:T(8,128)S(1)}, u32[]{:S(2)}, u32[]{:S(2)}) %collective-permute-start.19) | collective-permute-done | bytes 8224 | tf_op jit(solution)/shard_map/ppermute | solution.py:20
  82.0 1.9 %collective-permute-done.20 = f32[8,256]{1,0:T(8,128)S(1)} collective-permute-done((f32[8,256]{1,0:T(8,128)S(1)}, f32[8,256]{1,0:T(8,128)S(1)}, u32[]{:S(2)}, u32[]{:S(2)}) %collective-permute-start.20) | collective-permute-done | bytes 8224 | tf_op jit(solution)/shard_map/ppermute | solution.py:20
  83.9 1.8 %collective-permute-start.21 = (f32[16,256]{1,0:T(8,128)S(1)}, f32[16,256]{1,0:T(8,128)S(1)}, u32[]{:S(2)}, u32[]{:S(2)}) collective-permute-start(f32[16,256]{1,0:T(8,128)S(1)} %pad_maximum_fusion.6), channel_id=1, source_target_pairs={{0,8},{4,12},{8,0},{12,4},{16,24},{20,28},{24,16},{28,20},{1,9},{5... | collective-permute-start | bytes 49160 | tf_op jit(solution)/shard_map/ppermute | solution.py:20
  85.7 1.9 %collective-permute-done.21 = f32[16,256]{1,0:T(8,128)S(1)} collective-permute-done((f32[16,256]{1,0:T(8,128)S(1)}, f32[16,256]{1,0:T(8,128)S(1)}, u32[]{:S(2)}, u32[]{:S(2)}) %collective-permute-start.21) | collective-permute-done | bytes 16416 | tf_op jit(solution)/shard_map/ppermute | solution.py:20
  87.7 2.8 %collective-permute-start.22 = (f32[32,256]{1,0:T(8,128)S(1)}, f32[32,256]{1,0:T(8,128)S(1)}, u32[]{:S(2)}, u32[]{:S(2)}) collective-permute-start(f32[32,256]{1,0:T(8,128)S(1)} %pad_maximum_fusion.5), channel_id=1, source_target_pairs={{0,16},{4,20},{8,24},{12,28},{16,0},{20,4},{24,8},{28,12},{1,17},{... | collective-permute-start | bytes 98312 | tf_op jit(solution)/shard_map/ppermute | solution.py:20
  93.3 2.4 %shard_map.119 = bf16[4,4,64]{2,1,0:T(4,128)(2,1)} custom-call(f32[64,256]{1,0:T(8,128)} %pad_maximum_fusion.4.rows_ref, f32[16,64]{1,0:T(8,128)} %fusion.28.sel_ref, f32[16,16]{1,0:T(8,128)} %fusion.35.allow_ref, f32[16,1]{1,0:T(8,128)} %copy.33.fill_ref, f32[1,256]{1,0:T(1,128)} %bitcast.56, bf16[3,256,64]{2,1,0:T(8,128)(2,1)} %bitcast.45), custom_call_target="tpu_custom_call" | custom-call | tf_op jit(solution)/shard_map/pallas_call | solution.py:215
  (96 shorter events, 16.5 us)
Async XLA Ops:
  0.0 44.5 %collective-permute-start.3 = (bf16[3584,64]{0,1:T(8,128)(2,1)}, bf16[3584,64]{0,1:T(8,128)(2,1)}, u32[]{:S(2)}, u32[]{:S(2)}) collective-permute-start(bf16[3584,64]{0,1:T(8,128)(2,1)} %bitcast.61), channel_id=1, source_target_pairs={{0,2},{1,3},{2,0},{3,1},{4,6},{5,7},{6,4},{7,5},{8,10},{9,11},{10,... | collective-permute-start | bytes 1376264 | tf_op jit(solution)/shard_map/ppermute | solution.py:20
  3.0 49.8 %collective-permute-start.4 = (bf16[3584,64]{0,1:T(8,128)(2,1)}, bf16[3584,64]{0,1:T(8,128)(2,1)}, u32[]{:S(2)}, u32[]{:S(2)}) collective-permute-start(bf16[3584,64]{0,1:T(8,128)(2,1)} %bitcast.62), channel_id=1, source_target_pairs={{0,1},{1,0},{2,3},{3,2},{4,5},{5,4},{6,7},{7,6},{8,9},{9,8},{10,11... | collective-permute-start | bytes 1376264 | tf_op jit(solution)/shard_map/ppermute | solution.py:20
  3.0 49.7 %collective-permute-start = (bf16[3584,128]{1,0:T(8,128)(2,1)}, bf16[3584,128]{1,0:T(8,128)(2,1)S(1)}, u32[]{:S(2)}, u32[]{:S(2)}) collective-permute-start(bf16[3584,128]{1,0:T(8,128)(2,1)} %param.17), channel_id=1, source_target_pairs={{0,2},{1,3},{2,0},{3,1},{4,6},{5,7},{6,4},{7,5},{8,10},{9,11},{10,... | collective-permute-start | bytes 2752520 | tf_op jit(solution)/shard_map/ppermute | solution.py:20
  4.1 36.4 %collective-permute-start.9 = (bf16[896,128]{1,0:T(8,128)(2,1)S(1)}, bf16[896,128]{1,0:T(8,128)(2,1)}, u32[]{:S(2)}, u32[]{:S(2)}) collective-permute-start(bf16[896,128]{1,0:T(8,128)(2,1)S(1)} %constant_dynamic-slice_fusion.2), channel_id=1, source_target_pairs={{0,2},{1,3},{2,0},{3,1},{4,6},{5,7},{6,4},{7,5},{8,10},{9,11},{10,... | collective-permute-start | bytes 688136 | tf_op jit(solution)/shard_map/ppermute | solution.py:20
  10.4 29.2 %collective-permute-start.16 = (f32[8,2,896]{2,0,1:T(8,128)}, f32[8,2,896]{2,0,1:T(8,128)}, u32[]{:S(2)}, u32[]{:S(2)}) collective-permute-start(f32[8,2,896]{2,0,1:T(8,128)} %constant_dynamic-slice_fusion.1), channel_id=1, source_target_pairs={{0,2},{1,3},{2,0},{3,1},{4,6},{5,7},{6,4},{7,5},{8,10},{9,11},{10,... | collective-permute-start | bytes 172040 | tf_op jit(solution)/shard_map/ppermute | solution.py:20
  15.7 35.3 %copy-start.3 = (bf16[896,256]{1,0:T(8,128)(2,1)S(1)}, bf16[896,256]{1,0:T(8,128)(2,1)}, u32[]{:S(2)}) copy-start(bf16[896,256]{1,0:T(8,128)(2,1)} %param.20) | copy-start | bytes 1376260
  39.6 2.6 %collective-permute-start.10 = (bf16[896,128]{1,0:T(8,128)(2,1)S(1)}, bf16[896,128]{1,0:T(8,128)(2,1)S(1)}, u32[]{:S(2)}, u32[]{:S(2)}) collective-permute-start(bf16[896,128]{1,0:T(8,128)(2,1)S(1)} %constant_dynamic-slice_fusion.2), channel_id=1, source_target_pairs={{0,1},{1,0},{2,3},{3,2},{4,5},{5,4},{6,7},{7,6},{8,9},{9,8},{10,11... | collective-permute-start | bytes 688136 | tf_op jit(solution)/shard_map/ppermute | solution.py:20
  40.5 2.0 %collective-permute-start.11 = (bf16[896,128]{1,0:T(8,128)(2,1)}, bf16[896,128]{1,0:T(8,128)(2,1)S(1)}, u32[]{:S(2)}, u32[]{:S(2)}) collective-permute-start(bf16[896,128]{1,0:T(8,128)(2,1)} %collective-permute-done.9), channel_id=1, source_target_pairs={{0,1},{1,0},{2,3},{3,2},{4,5},{5,4},{6,7},{7,6},{8,9},{9,8},{10,11... | collective-permute-start | bytes 688136 | tf_op jit(solution)/shard_map/ppermute | solution.py:20
  42.7 4.0 %collective-permute-start.12 = (bf16[128,128]{1,0:T(8,128)(2,1)S(1)}, bf16[128,128]{1,0:T(8,128)(2,1)S(1)}, u32[]{:S(2)}, u32[]{:S(2)}) collective-permute-start(bf16[128,128]{1,0:T(8,128)(2,1)S(1)} %fusion.16), channel_id=1, source_target_pairs={{0,4},{4,0},{8,12},{12,8},{16,20},{20,16},{24,28},{28,24},{1,5},{5... | collective-permute-start | bytes 98312 | tf_op jit(solution)/shard_map/ppermute | solution.py:20
  44.5 4.0 %collective-permute-start.17 = (f32[8,1,896]{2,0,1:T(8,128)S(1)}, f32[8,1,896]{2,0,1:T(8,128)S(1)}, u32[]{:S(2)}, u32[]{:S(2)}) collective-permute-start(f32[8,1,896]{2,0,1:T(8,128)S(1)} %constant_dynamic-slice_fusion), channel_id=1, source_target_pairs={{0,1},{1,0},{2,3},{3,2},{4,5},{5,4},{6,7},{7,6},{8,9},{9,8},{10,11... | collective-permute-start | bytes 86024 | tf_op jit(solution)/shard_map/ppermute | solution.py:20
  44.5 8.3 %collective-permute-start.5 = (bf16[3584,64]{0,1:T(8,128)(2,1)}, bf16[3584,64]{0,1:T(8,128)(2,1)}, u32[]{:S(2)}, u32[]{:S(2)}) collective-permute-start(bf16[3584,64]{0,1:T(8,128)(2,1)} %collective-permute-done.3), channel_id=1, source_target_pairs={{0,1},{1,0},{2,3},{3,2},{4,5},{5,4},{6,7},{7,6},{8,9},{9,8},{10,11... | collective-permute-start | bytes 1376264 | tf_op jit(solution)/shard_map/ppermute | solution.py:20
  46.7 4.3 %collective-permute-start.13 = (bf16[128,256]{1,0:T(8,128)(2,1)S(1)}, bf16[128,256]{1,0:T(8,128)(2,1)S(1)}, u32[]{:S(2)}, u32[]{:S(2)}) collective-permute-start(bf16[128,256]{1,0:T(8,128)(2,1)S(1)} %pad_maximum_fusion.3), channel_id=1, source_target_pairs={{0,2},{1,3},{2,0},{3,1},{4,6},{5,7},{6,4},{7,5},{8,10},{9,11},{10,... | collective-permute-start | bytes 196616 | tf_op jit(solution)/shard_map/ppermute | solution.py:20
  48.5 3.6 %collective-permute-start.14 = (bf16[128,256]{1,0:T(8,128)(2,1)S(1)}, bf16[128,256]{1,0:T(8,128)(2,1)S(1)}, u32[]{:S(2)}, u32[]{:S(2)}) collective-permute-start(bf16[128,256]{1,0:T(8,128)(2,1)S(1)} %pad_maximum_fusion.3), channel_id=1, source_target_pairs={{0,1},{1,0},{2,3},{3,2},{4,5},{5,4},{6,7},{7,6},{8,9},{9,8},{10,11... | collective-permute-start | bytes 196616 | tf_op jit(solution)/shard_map/ppermute | solution.py:20
  51.0 1.6 %collective-permute-start.15 = (bf16[128,256]{1,0:T(8,128)(2,1)S(1)}, bf16[128,256]{1,0:T(8,128)(2,1)S(1)}, u32[]{:S(2)}, u32[]{:S(2)}) collective-permute-start(bf16[128,256]{1,0:T(8,128)(2,1)S(1)} %collective-permute-done.13), channel_id=1, source_target_pairs={{0,1},{1,0},{2,3},{3,2},{4,5},{5,4},{6,7},{7,6},{8,9},{9,8},{10,11... | collective-permute-start | bytes 196616 | tf_op jit(solution)/shard_map/ppermute | solution.py:20
  52.1 13.3 %collective-permute-start.1 = (bf16[3584,128]{1,0:T(8,128)(2,1)S(1)}, bf16[3584,128]{1,0:T(8,128)(2,1)}, u32[]{:S(2)}, u32[]{:S(2)}) collective-permute-start(bf16[3584,128]{1,0:T(8,128)(2,1)S(1)} %copy-done.4), channel_id=1, source_target_pairs={{0,1},{1,0},{2,3},{3,2},{4,5},{5,4},{6,7},{7,6},{8,9},{9,8},{10,11... | collective-permute-start | bytes 2752520 | tf_op jit(solution)/shard_map/ppermute | solution.py:20
  52.7 15.5 %collective-permute-start.2 = (bf16[3584,128]{1,0:T(8,128)(2,1)S(1)}, bf16[3584,128]{1,0:T(8,128)(2,1)}, u32[]{:S(2)}, u32[]{:S(2)}) collective-permute-start(bf16[3584,128]{1,0:T(8,128)(2,1)S(1)} %collective-permute-done), channel_id=1, source_target_pairs={{0,1},{1,0},{2,3},{3,2},{4,5},{5,4},{6,7},{7,6},{8,9},{9,8},{10,11... | collective-permute-start | bytes 2752520 | tf_op jit(solution)/shard_map/ppermute | solution.py:20
  56.7 8.8 %collective-permute-start.6 = (bf16[8,64,256]{2,1,0:T(8,128)(2,1)S(1)}, bf16[8,64,256]{2,1,0:T(8,128)(2,1)S(1)}, u32[]{:S(2)}, u32[]{:S(2)}) collective-permute-start(bf16[8,64,256]{2,1,0:T(8,128)(2,1)S(1)} %bitcast.48), channel_id=1, source_target_pairs={{0,2},{1,3},{2,0},{3,1},{4,6},{5,7},{6,4},{7,5},{8,10},{9,11},{10,... | collective-permute-start | bytes 786440 | tf_op jit(solution)/shard_map/ppermute | solution.py:20
  58.5 9.5 %collective-permute-start.7 = (bf16[8,64,256]{2,1,0:T(8,128)(2,1)S(1)}, bf16[8,64,256]{2,1,0:T(8,128)(2,1)S(1)}, u32[]{:S(2)}, u32[]{:S(2)}) collective-permute-start(bf16[8,64,256]{2,1,0:T(8,128)(2,1)S(1)} %bitcast.49), channel_id=1, source_target_pairs={{0,1},{1,0},{2,3},{3,2},{4,5},{5,4},{6,7},{7,6},{8,9},{9,8},{10,11... | collective-permute-start | bytes 786440 | tf_op jit(solution)/shard_map/ppermute | solution.py:20
  65.4 2.6 %collective-permute-start.8 = (bf16[8,64,256]{2,1,0:T(8,128)(2,1)S(1)}, bf16[8,64,256]{2,1,0:T(8,128)(2,1)S(1)}, u32[]{:S(2)}, u32[]{:S(2)}) collective-permute-start(bf16[8,64,256]{2,1,0:T(8,128)(2,1)S(1)} %collective-permute-done.6), channel_id=1, source_target_pairs={{0,1},{1,0},{2,3},{3,2},{4,5},{5,4},{6,7},{7,6},{8,9},{9,8},{10,11... | collective-permute-start | bytes 786440 | tf_op jit(solution)/shard_map/ppermute | solution.py:20
  75.3 1.4 %collective-permute-start.18 = (f32[8,256]{1,0:T(8,128)S(1)}, f32[8,256]{1,0:T(8,128)S(1)}, u32[]{:S(2)}, u32[]{:S(2)}) collective-permute-start(f32[8,256]{1,0:T(8,128)S(1)} %shard_map.118), channel_id=1, source_target_pairs={{0,1},{1,0},{2,3},{3,2},{4,5},{5,4},{6,7},{7,6},{8,9},{9,8},{10,11... | collective-permute-start | bytes 24584 | tf_op jit(solution)/shard_map/ppermute | solution.py:20
  76.6 3.7 %collective-permute-start.19 = (f32[8,256]{1,0:T(8,128)S(1)}, f32[8,256]{1,0:T(8,128)S(1)}, u32[]{:S(2)}, u32[]{:S(2)}) collective-permute-start(f32[8,256]{1,0:T(8,128)S(1)} %add.224), channel_id=1, source_target_pairs={{0,2},{1,3},{2,0},{3,1},{4,6},{5,7},{6,4},{7,5},{8,10},{9,11},{10,... | collective-permute-start | bytes 24584 | tf_op jit(solution)/shard_map/ppermute | solution.py:20
  80.3 3.7 %collective-permute-start.20 = (f32[8,256]{1,0:T(8,128)S(1)}, f32[8,256]{1,0:T(8,128)S(1)}, u32[]{:S(2)}, u32[]{:S(2)}) collective-permute-start(f32[8,256]{1,0:T(8,128)S(1)} %add.225), channel_id=1, source_target_pairs={{0,4},{4,0},{8,12},{12,8},{16,20},{20,16},{24,28},{28,24},{1,5},{5... | collective-permute-start | bytes 24584 | tf_op jit(solution)/shard_map/ppermute | solution.py:20
  83.9 3.7 %collective-permute-start.21 = (f32[16,256]{1,0:T(8,128)S(1)}, f32[16,256]{1,0:T(8,128)S(1)}, u32[]{:S(2)}, u32[]{:S(2)}) collective-permute-start(f32[16,256]{1,0:T(8,128)S(1)} %pad_maximum_fusion.6), channel_id=1, source_target_pairs={{0,8},{4,12},{8,0},{12,4},{16,24},{20,28},{24,16},{28,20},{1,9},{5... | collective-permute-start | bytes 49160 | tf_op jit(solution)/shard_map/ppermute | solution.py:20
  87.7 5.0 %collective-permute-start.22 = (f32[32,256]{1,0:T(8,128)S(1)}, f32[32,256]{1,0:T(8,128)S(1)}, u32[]{:S(2)}, u32[]{:S(2)}) collective-permute-start(f32[32,256]{1,0:T(8,128)S(1)} %pad_maximum_fusion.5), channel_id=1, source_target_pairs={{0,16},{4,20},{8,24},{12,28},{16,0},{20,4},{24,8},{28,12},{1,17},{... | collective-permute-start | bytes 98312 | tf_op jit(solution)/shard_map/ppermute | solution.py:20
  (12 other events, 88.7 us)

commit v2 on v1

v2 whole, which is shorter than its diff:
```python
import functools

import jax
import jax.numpy as jnp
from jax import lax
from jax.experimental import pallas as pl
from jax.experimental.pallas import tpu as pltpu
from jax.sharding import PartitionSpec as P

CAP = 8
DOC_MOST = 4
OWN_DOCS = 4
F32 = jnp.float32
BF16 = jnp.bfloat16
HIGH = lax.Precision.HIGHEST
NT = (((1,), (1,)), ((), ()))


def flipped(block, axis, mask):
    count = lax.axis_size(axis)
    return lax.ppermute(block, axis, [(i, i ^ mask) for i in range(count)])


def after(value, earlier):
    return lax.optimization_barrier((value, earlier))[0]


def cut(array, at, size, axis):
    return lax.dynamic_slice_in_dim(array, at * size, size, axis=axis)


def ordered(own, other, bit, axis):
    first = jnp.where(bit == 0, own, other)
    second = jnp.where(bit == 0, other, own)
    return jnp.concatenate([first, second], axis=axis)


def slot_table(seg_replica):
    replica_of = seg_replica[:, 0]
    order = jnp.arange(replica_of.shape[0], dtype=jnp.int32)
    earlier = (replica_of[None, :] == replica_of[:, None]) & (order[None, :] < order[:, None])
    return replica_of, jnp.sum(earlier.astype(jnp.int32), axis=1)


def owner_rows(doc_of_segment, doc_owner):
    owner_of = doc_owner[:, 0]
    doc_ids = jnp.arange(owner_of.shape[0], dtype=jnp.int32)
    earlier = (owner_of[None, :] == owner_of[:, None]) & (doc_ids[None, :] < doc_ids[:, None])
    doc_rank = jnp.sum(earlier.astype(jnp.int32), axis=1)
    start_of = jnp.sum((doc_of_segment[None, :] < doc_ids[:, None]).astype(jnp.int32), axis=1)
    matches = doc_of_segment[:, None] == doc_ids[None, :]
    seg_owner = jnp.sum(jnp.where(matches, owner_of[None, :], 0), axis=1)
    seg_rank = jnp.sum(jnp.where(matches, doc_rank[None, :], 0), axis=1)
    seg_start = jnp.sum(jnp.where(matches, start_of[None, :], 0), axis=1)
    position = jnp.arange(doc_of_segment.shape[0], dtype=jnp.int32) - seg_start
    return seg_owner * (OWN_DOCS * DOC_MOST) + seg_rank * DOC_MOST + position


def norm_kernel(tokens_ref, gain_ref, normed_ref, sum_ref):
    x = tokens_ref[0].astype(F32)
    scale = lax.rsqrt(jnp.mean(x * x, axis=-1, keepdims=True) + 1e-06)
    normed_ref[0] = (x * scale * gain_ref[...]).astype(BF16)
    sum_ref[0] = jnp.sum(x, axis=0, keepdims=True)


def normalized(tokens, gain):
    slots, count, width = tokens.shape
    return pl.pallas_call(
        norm_kernel,
        grid=(slots,),
        in_specs=[
            pl.BlockSpec((1, count, width), lambda i: (i, 0, 0)),
            pl.BlockSpec((1, width), lambda i: (0, 0)),
        ],
        out_specs=[
            pl.BlockSpec((1, count, width), lambda i: (i, 0, 0)),
            pl.BlockSpec((1, 1, width), lambda i: (i, 0, 0)),
        ],
        out_shape=[
            jax.ShapeDtypeStruct((slots, count, width), BF16),
            jax.ShapeDtypeStruct((slots, 1, width), F32),
        ],
        cost_estimate=pl.CostEstimate(
            flops=8 * tokens.size, bytes_accessed=4 * tokens.size, transcendentals=0
        ),
    )(tokens, gain)


def attention_kernel(masks, group, slots, length, *refs):
    n = len(masks)
    q_refs, near_refs, far_refs, w2_refs = (refs[i * n:(i + 1) * n] for i in range(4))
    place_ref, xp_ref, out_ref, ctx_ref = refs[4 * n:]
    rows, head_dim = q_refs[0].shape
    tokens = rows // (2 * slots)
    groups = sorted({m // group for m in masks})
    for s in range(slots):
        spans = [slice((c * slots + s) * tokens, (c * slots + s + 1) * tokens) for c in range(2)]
        kv = jnp.concatenate(
            [
                jnp.dot(
                    jnp.concatenate([near[spans[c], :], far[spans[1 - c], :]], axis=1),
                    place_ref[p],
                    preferred_element_type=F32,
                ).astype(BF16)
                for p, (near, far) in enumerate(zip(near_refs, far_refs))
                for c in range(2)
            ],
            axis=0,
        )
        for g in groups:
            heads = [p for p in range(n) if masks[p] // group == g]
            q = jnp.concatenate([q_refs[p][span, :] for p in heads for span in spans], axis=0)
            keys = kv[:, g * 2 * head_dim:(g * 2 + 1) * head_dim]
            values = kv[:, (g * 2 + 1) * head_dim:(g * 2 + 2) * head_dim]
            scores = lax.dot_general(q, keys, NT, preferred_element_type=F32) * head_dim ** (-0.5)
            e = jnp.exp(scores - jnp.max(scores, axis=1, keepdims=True))
            probs = e * (1.0 / jnp.sum(e, axis=1, keepdims=True))
            weight = jnp.sum(probs.reshape(len(heads), 2 * tokens, -1), axis=1)
            context = jnp.dot(weight, values.astype(F32), preferred_element_type=F32, precision=HIGH)
            for j, p in enumerate(heads):
                ctx_ref[p, s:s + 1, :] = context[j:j + 1] * (1.0 / length)
    total = xp_ref[...]
    for p in range(n):
        total += lax.dot_general(
            ctx_ref[p], w2_refs[p][...].astype(F32), NT, preferred_element_type=F32, precision=HIGH
        )
    out_ref[...] = total


def document_kernel(rows_ref, sel_ref, allow_ref, fill_ref, gain_ref, qkv_ref, out_ref):
    docs, most, head = out_ref.shape
    first = jnp.dot(sel_ref[...], rows_ref[...], preferred_element_type=F32, precision=HIGH)
    scale = lax.rsqrt(jnp.mean(first * first, axis=-1, keepdims=True) + 1e-06)
    normed = (first * scale * gain_ref[...]).astype(BF16)
    q, k, v = (
        lax.dot_general(normed, qkv_ref[i], NT, preferred_element_type=F32).astype(BF16) for i in range(3)
    )
    scores = lax.dot_general(q, k, NT, preferred_element_type=F32) * head ** (-0.5)
    scores = jnp.where(allow_ref[...] > 0.5, scores, -1e30)
    e = jnp.exp(scores - jnp.max(scores, axis=1, keepdims=True))
    probs = (e / jnp.sum(e, axis=1, keepdims=True)).astype(BF16)
    context = jnp.dot(probs, v, preferred_element_type=F32) * fill_ref[...]
    for d in range(docs):
        out_ref[d] = context[d * most:(d + 1) * most].astype(BF16)


def local(
    tokens,
    seg_replica,
    doc_of_segment,
    doc_owner,
    enc_gain,
    enc_query,
    enc_keyvalue,
    enc_output,
    doc_proj,
    doc_gain,
    doc_qkv,
):
    n_rep, n_tp = lax.axis_size("rep"), lax.axis_size("tp")
    rep_index = lax.axis_index("rep")
    tp_index = lax.axis_index("tp")
    x_bit, z_bit = rep_index % 2, rep_index // 2 % 2
    slots, own_tokens, width = tokens.shape
    length = own_tokens * n_tp
    head_dim = enc_query.shape[1]
    kv_width = enc_keyvalue.shape[2]
    group = head_dim // kv_width
    block, doc_width = doc_proj.shape
    masks = list(range(0, n_tp, 2))

    tokens_far = flipped(tokens, "tp", 1)

    kv_rows = jnp.transpose(enc_keyvalue, (1, 2, 0))
    part_kv = kv_width // 2
    part_doc = doc_width // 4
    proj_rows = part_doc * block // width
    proj = cut(doc_proj, z_bit * 2 + x_bit, part_doc, 1).T
    proj = jnp.concatenate(
        [proj[i * proj_rows:(i + 1) * proj_rows] for i in range(width // block)], axis=1
    )
    opening = jnp.concatenate(
        [cut(kv_rows[0], x_bit, part_kv, 0), cut(kv_rows[1], z_bit, part_kv, 0), proj], axis=0
    )
    received = [flipped(opening, "tp", m) for m in masks[1:]]

    part_q = width // 4
    q_half = jnp.concatenate(
        [cut(enc_query[:2 * part_q], x_bit, part_q, 0), cut(enc_query[2 * part_q:], z_bit, part_q, 0)], axis=0
    )
    q_half = after(q_half, received[0])
    q_received = [flipped(q_half, "tp", m) for m in masks[1:]]

    near, sums = normalized(tokens, enc_gain[None, :])

    kv_parts = [kv_rows.reshape(2 * kv_width, width)]
    for r in received:
        kv_parts += [
            r[:part_kv],
            flipped(r[:part_kv], "rep", 1),
            r[part_kv:2 * part_kv],
            flipped(r[part_kv:2 * part_kv], "rep", 2),
        ]
    kv_weights = jnp.concatenate(kv_parts, axis=0)

    far, sums_far = normalized(tokens_far, enc_gain[None, :])
    rows = slots * own_tokens
    normed = jnp.concatenate([near.reshape(rows, width), far.reshape(rows, width)], axis=0)

    proj_near = [proj] + [r[2 * part_kv:] for r in received]
    proj_far = flipped(jnp.concatenate(proj_near, axis=0), "tp", 1)
    proj_all = proj_near + [proj_far[i * proj_rows:(i + 1) * proj_rows] for i in range(len(masks))]
    origin = masks + [m + 1 for m in masks]
    proj_all = jnp.concatenate(
        [
            jnp.concatenate([p[:, i * block:(i + 1) * block] for i in range(width // block)], axis=0)
            for p in proj_all
        ],
        axis=1,
    )
    output_all = jnp.concatenate([cut(enc_output, tp_index ^ m, block, 1) for m in origin], axis=1)
    w2 = lax.dot_general(proj_all, output_all, NT, preferred_element_type=F32).astype(BF16)
    w2 = ordered(w2, flipped(w2, "rep", 1), x_bit, 0)
    w2 = ordered(w2, flipped(w2, "rep", 2), z_bit, 0)

    kv = lax.dot_general(normed, kv_weights, NT, preferred_element_type=F32).astype(BF16)
    lanes = kv.shape[1]
    mean = ((sums + sums_far) * (1.0 / length)).reshape(slots, n_tp // 2, 2, block)
    mean = lax.dynamic_index_in_dim(mean, tp_index % 2, 2, keepdims=False)

    def mean_of(m):
        return lax.dynamic_index_in_dim(mean, (tp_index ^ m) // 2, 1, keepdims=False)

    kv_near, w2_near, mean_here = [kv], [w2], mean_of(0)
    for m in masks[1:]:
        there = mean_of(m)
        high = there.astype(BF16)
        low = (there - high.astype(F32)).astype(BF16)
        both = jnp.stack([high, low], axis=0)
        pad = -both.size % (lanes * 8)
        both_rows = jnp.pad(both.reshape(-1), (0, pad)).reshape(-1, lanes)
        w2_rows = w2.reshape(-1, lanes)
        packed = jnp.concatenate([kv, w2_rows, both_rows], axis=0)
        packed = flipped(packed, "tp", m)
        kv_near.append(packed[:kv.shape[0]])
        w2_near.append(packed[kv.shape[0]:kv.shape[0] + w2_rows.shape[0]].reshape(w2.shape))
        both = packed[kv.shape[0] + w2_rows.shape[0]:].reshape(-1)[:both.size].reshape(both.shape)
        mean_here = mean_here + (both[0].astype(F32) + both[1].astype(F32))
    kv_far = [flipped(k, "tp", 1) for k in kv_near]
    mean_part = jnp.dot(mean_here, doc_proj.astype(F32), precision=HIGH)

    count = 2 * lanes
    column = jnp.arange(count, dtype=jnp.int32)
    core = column // lanes
    mask_of = column % lanes // (2 * kv_width) * 2
    inner = column % (2 * kv_width)
    quarter = inner // part_kv
    turn = jnp.where(quarter < 2, x_bit, z_bit)
    swapped = quarter // 2 * 2 + (quarter % 2 ^ turn)
    inner = jnp.where(mask_of == 0, inner, swapped * part_kv + inner % part_kv)
    places = []
    for m in masks:
        target = (
            (mask_of ^ m) // group * (2 * head_dim)
            + inner // kv_width * head_dim
            + (tp_index ^ m ^ mask_of ^ core) % group * kv_width
            + inner % kv_width
        )
        places.append((target[:, None] == column[None, :]).astype(BF16))
    place = jnp.stack(places, axis=0)

    early = jnp.concatenate(
        [cut(normed[:, :2 * part_q], x_bit, part_q, 1), cut(normed[:, 2 * part_q:], z_bit, part_q, 1)], axis=1
    )
    late = jnp.concatenate(
        [cut(normed[:, :2 * part_q], 1 - x_bit, part_q, 1), cut(normed[:, 2 * part_q:], 1 - z_bit, part_q, 1)],
        axis=1,
    )
    queries = [jnp.dot(normed, enc_query, preferred_element_type=F32).astype(BF16)]
    for r in q_received:
        rest = jnp.concatenate(
            [flipped(r[:part_q], "rep", 1), flipped(r[part_q:], "rep", 2)], axis=0
        )
        total = jnp.dot(early, r, preferred_element_type=F32)
        total = total + jnp.dot(late, rest, preferred_element_type=F32)
        queries.append(total.astype(BF16))

    part = pl.pallas_call(
        functools.partial(attention_kernel, masks, group, slots, length),
        out_shape=jax.ShapeDtypeStruct((slots, doc_width), F32),
        scratch_shapes=[pltpu.VMEM((len(masks), slots, head_dim), F32)],
        compiler_params=pltpu.CompilerParams(vmem_limit_bytes=40 * 2**20),
    )(*queries, *kv_near, *kv_far, *w2_near, place, mean_part)

    bit = 1
    while bit < n_tp:
        part = part + flipped(part, "tp", bit)
        bit *= 2
    bit = 1
    while bit < n_rep:
        part = jnp.concatenate([part, flipped(part, "rep", bit)], axis=0)
        bit *= 2

    replica_of, rank = slot_table(seg_replica)
    row_of = owner_rows(doc_of_segment, doc_owner)
    owned = OWN_DOCS * DOC_MOST
    wanted = rep_index * owned + jnp.arange(owned, dtype=jnp.int32)
    matches = (row_of[None, :] == wanted[:, None]).astype(F32)
    at_slot = (replica_of ^ rep_index) * CAP + rank
    holds = (at_slot[:, None] == jnp.arange(n_rep * CAP, dtype=jnp.int32)[None, :]).astype(F32)
    select = jnp.dot(matches, holds)
    filled = jnp.sum(matches, axis=1)
    row = jnp.arange(owned, dtype=jnp.int32)
    same_doc = row[:, None] // DOC_MOST == row[None, :] // DOC_MOST
    allowed = same_doc & ((filled[None, :] > 0.5) | (row[:, None] == row[None, :]))

    return pl.pallas_call(
        document_kernel,
        out_shape=jax.ShapeDtypeStruct((OWN_DOCS, DOC_MOST, doc_qkv.shape[2]), BF16),
    )(
        part,
        select,
        allowed.astype(F32),
        filled[:, None],
        doc_gain[None, :],
        jnp.transpose(doc_qkv, (1, 2, 0)),
    )


def solution(mesh):
    in_specs = (
        P("rep", "tp", None),
        P(),
        P(),
        P(),
        P(),
        P(None, "tp"),
        P(None, None, "tp"),
        P("tp", None),
        P("tp", None),
        P(),
        P(None, None, "tp"),
    )
    out_specs = P("rep", None, "tp")
    return jax.shard_map(local, mesh=mesh, in_specs=in_specs, out_specs=out_specs, check_vma=False)
```

time: 96.1 us -> 98.3 us (1.023)
  Pallas kernels: 6.66 us -> 22.2 us
  waiting for transfers between devices: 34.2 us -> 21.2 us
  local copies, waits for them, and re-layouts: 5.12 us -> 14.1 us
  matrix products: 18 us -> 12.2 us
  starting transfers between devices: 21.1 us -> 16.8 us
    pallas_call x1 -> x3, Pallas kernels: 4.24 us -> 19.8 us  [the longest x2 14 us: normalized(): pl.pallas_call(norm_kernel, grid=(slots,), in_specs=[pl.BlockSpec((1, cou...]
    ppermute x23 -> x18, waiting for transfers between devices: 34.2 us -> 21.2 us  [flipped(): return lax.ppermute(block, axis, [(i, i ^ mask) for i in range(count)])]
    dot_general x10 -> x6, matrix products: 17.2 us -> 11.4 us  [the longest x1 5.35 us: local(): jnp.dot(normed, enc_query, preferred_element_type=F32).astype(BF16)]
    ppermute x23 -> x18, starting transfers between devices: 21.1 us -> 16.8 us  [flipped(): return lax.ppermute(block, axis, [(i, i ^ mask) for i in range(count)])]
    concatenate x3 -> x7, other arithmetic: 0.07 us -> 4.2 us  [the longest x1 3.34 us: local(): jnp.concatenate([near.reshape(rows, width), far.reshape(rows, width)], ax...]
    dynamic_slice x3 -> x6, local copies, waits for them, and re-layouts: 1.6 us -> 5.36 us  [the longest x5 5.3 us: cut(): return lax.dynamic_slice_in_dim(array, at * size, size, axis=axis)]
    reduce_sum x1 -> x0, other arithmetic: 3.72 us -> none  [local(): sums = jnp.sum(raw, axis=1) * (1.0 / length)]
    convert_element_type x1, other arithmetic: 3.21 us -> 0.01 us  [local(): low = (there - high.astype(F32)).astype(BF16)]
  transfers between devices with their start and end apart: 23 -> 18, of which waited for: 7 -> 11; matrix products, arithmetic and copies ran while one was open for 29% -> 34% of each run, Pallas kernels for 0% -> 14%
where the time goes in v2:
time: 98.3 us; the launch traced here: 97.6 us
  Pallas kernels  22.2 us (23%)
  waiting for transfers between devices  21.2 us (22%)
  starting transfers between devices  16.8 us (17%)
  local copies, waits for them, and re-layouts  14.1 us (14%)
  matrix products  12.2 us (12%)
  other arithmetic  10.6 us (11%)
    ppermute x18, waiting for transfers between devices, flipped(): return lax.ppermute(block, axis, [(i, i ^ mask) for i in range(count)])  21.2 us
    ppermute x18, starting transfers between devices, flipped(): return lax.ppermute(block, axis, [(i, i ^ mask) for i in range(count)])  16.8 us
    pallas_call x2, Pallas kernels, normalized(): pl.pallas_call(norm_kernel, grid=(slots,), in_specs=[pl.BlockSpec((1, cou...  14 us
    pallas_call x1, Pallas kernels, local(): pl.pallas_call(functools.partial(attention_kernel, masks, group, slots, l...  5.8 us
    dot_general x1, matrix products, local(): jnp.dot(normed, enc_query, preferred_element_type=F32).astype(BF16)  5.35 us
    dynamic_slice x5, local copies, waits for them, and re-layouts, cut(): return lax.dynamic_slice_in_dim(array, at * size, size, axis=axis)  5.3 us
    concatenate x1, other arithmetic, local(): jnp.concatenate([near.reshape(rows, width), far.reshape(rows, width)], ax...  3.34 us
    unnamed x23, local copies, waits for them, and re-layouts  3.28 us
  transfers between devices with their start and end apart: 18, of which 11 were waited for; matrix products, arithmetic and copies ran while one was open for 34% of the time, Pallas kernels for 14%

profile of v2, /device:TPU:0, one launch (start us, length us, event | category | flops | bytes accessed | tf_op | source)
XLA Modules:
  0.0 97.6 jit_solution(303025859195212097)
XLA Ops:
  3.2 3.0 %collective-permute-start.1 = (bf16[48,3584]{1,0:T(8,128)(2,1)}, bf16[48,3584]{1,0:T(8,128)(2,1)S(1)}, u32[]{:S(2)}, u32[]{:S(2)}) collective-permute-start(bf16[48,3584]{1,0:T(8,128)(2,1)} %maximum_maximum_fusion), channel_id=1, source_target_pairs={{0,2},{1,3},{2,0},{3,1},{4,6},{5,7},{6,4},{7,5},{8,10},{9,11},{10,... | collective-permute-start | bytes 1032200 | tf_op jit(solution)/shard_map/ppermute | solution.py:21
  9.5 1.3 %broadcast_in_dim.67.gain_ref = f32[1,3584]{1,0:T(1,128)} reshape(f32[3584]{0:T(1024)} %param.15) | data formatting | bytes 28672 | tf_op jit(solution)/shard_map/broadcast_in_dim | solution.py:194
  11.9 7.0 %shard_map.109 = (bf16[8,64,3584]{2,1,0:T(8,128)(2,1)}, f32[8,1,3584]{2,1,0:T(1,128)}) custom-call(bf16[8,64,3584]{2,1,0:T(8,128)(2,1)} %tokens_ref.1, f32[1,3584]{1,0:T(1,128)} %broadcast_in_dim.67.gain_ref), custom_call_target="tpu_custom_call" | custom-call | flops 14680064 | bytes 7340032 | tf_op jit(solution)/shard_map/pallas_call | solution.py:68
  19.2 1.4 %constant_dynamic-slice_fusion.5 = (bf16[128,896]{1,0:T(8,128)(2,1)S(1)}, bf16[128,896]{1,0:T(8,128)(2,1)S(1)}, bf16[128,896]{1,0:T(8,128)(2,1)S(1)}, bf16[128,896]{1,0:T(8,128)(2,1)S(1)}) fusion(bf16[128,3584]{1,0:T(8,128)(2,1)} %param.18, s32[]{:T(128)S(6)} %select_n.334, s32[]{:T(128)S(6)} %select_n.335, s32[]{:T(128)S(6)} %select_n.337, s32[]{:T(128)S(6)} %select_n.336), kind=kLoop, calls=%fused_computation.118 | loop fusion | bytes 1835024 | tf_op jit(solution)/shard_map/dynamic_slice | solution.py:29
  21.3 1.6 %collective-permute-start.6 = (bf16[16,3584]{1,0:T(8,128)(2,1)S(1)}, bf16[16,3584]{1,0:T(8,128)(2,1)S(1)}, u32[]{:S(2)}, u32[]{:S(2)}) collective-permute-start(bf16[16,3584]{1,0:T(8,128)(2,1)S(1)} %get-tuple-element.40), channel_id=1, source_target_pairs={{0,8},{4,12},{8,0},{12,4},{16,24},{20,28},{24,16},{28,20},{1,9},{5... | collective-permute-start | bytes 344072 | tf_op jit(solution)/shard_map/ppermute | solution.py:21
  22.8 1.5 %collective-permute-start.5 = (bf16[16,3584]{1,0:T(8,128)(2,1)S(1)}, bf16[16,3584]{1,0:T(8,128)(2,1)S(1)}, u32[]{:S(2)}, u32[]{:S(2)}) collective-permute-start(bf16[16,3584]{1,0:T(8,128)(2,1)S(1)} %get-tuple-element.41), channel_id=1, source_target_pairs={{0,4},{4,0},{8,12},{12,8},{16,20},{20,16},{24,28},{28,24},{1,5},{5... | collective-permute-start | bytes 344072 | tf_op jit(solution)/shard_map/ppermute | solution.py:21
  25.0 3.1 %collective-permute-done.5 = bf16[16,3584]{1,0:T(8,128)(2,1)S(1)} collective-permute-done((bf16[16,3584]{1,0:T(8,128)(2,1)S(1)}, bf16[16,3584]{1,0:T(8,128)(2,1)S(1)}, u32[]{:S(2)}, u32[]{:S(2)}) %collective-permute-start.5) | collective-permute-done | bytes 114720 | tf_op jit(solution)/shard_map/ppermute | solution.py:21
  29.2 1.6 %collective-permute-start.8 = (bf16[64,128]{1,0:T(8,128)(2,1)S(1)}, bf16[64,128]{1,0:T(8,128)(2,1)S(1)}, u32[]{:S(2)}, u32[]{:S(2)}) collective-permute-start(bf16[64,128]{1,0:T(8,128)(2,1)S(1)} %convolution_convert_fusion), channel_id=1, source_target_pairs={{0,4},{4,0},{8,12},{12,8},{16,20},{20,16},{24,28},{28,24},{1,5},{5... | collective-permute-start | bytes 49160 | tf_op jit(solution)/shard_map/ppermute | solution.py:21
  31.4 1.6 %collective-permute-done.8 = bf16[64,128]{1,0:T(8,128)(2,1)S(1)} collective-permute-done((bf16[64,128]{1,0:T(8,128)(2,1)S(1)}, bf16[64,128]{1,0:T(8,128)(2,1)S(1)}, u32[]{:S(2)}, u32[]{:S(2)}) %collective-permute-start.8) | collective-permute-done | bytes 16416 | tf_op jit(solution)/shard_map/ppermute | solution.py:21
  34.2 2.8 %collective-permute-done.9 = bf16[128,128]{1,0:T(8,128)(2,1)S(1)} collective-permute-done((bf16[128,128]{1,0:T(8,128)(2,1)S(1)}, bf16[128,128]{1,0:T(8,128)(2,1)S(1)}, u32[]{:S(2)}, u32[]{:S(2)}) %collective-permute-start.9) | collective-permute-done | bytes 32800 | tf_op jit(solution)/shard_map/ppermute | solution.py:21
  39.9 7.0 %shard_map.110 = (bf16[8,64,3584]{2,1,0:T(8,128)(2,1)}, f32[8,1,3584]{2,1,0:T(1,128)}) custom-call(bf16[8,64,3584]{2,1,0:T(8,128)(2,1)} %collective-permute-done.tokens_ref, f32[1,3584]{1,0:T(1,128)} %broadcast_in_dim.67.gain_ref), custom_call_target="tpu_custom_call" | custom-call | flops 14680064 | bytes 7340032 | tf_op jit(solution)/shard_map/pallas_call | solution.py:68
  48.4 5.3 %fusion.18.refs_0_ = bf16[1024,128]{1,0:T(8,128)(2,1)S(1)} fusion(bf16[3584,128]{1,0:T(8,128)(2,1)S(1)} %copy-done.4, bf16[512,3584]{1,0:T(8,128)(2,1)} %bitcast.39, bf16[512,3584]{1,0:T(8,128)(2,1)} %bitcast.36), kind=kOutput, calls=%fused_computation.19 | convolution fusion | flops 954335232 | bytes 8519680 | tf_op jit(solution)/shard_map/dot_general | solution.py:279
  53.8 3.3 %fusion.2 = (bf16[1024,1792]{1,0:T(8,128)(2,1)}, bf16[1024,1792]{1,0:T(8,128)(2,1)}) fusion(bf16[512,3584]{1,0:T(8,128)(2,1)S(1)} %bitcast.37, bf16[512,3584]{1,0:T(8,128)(2,1)S(1)} %bitcast.40), kind=kLoop, calls=%fused_computation.7 | loop fusion | flops 14680064 | bytes 14680064 | tf_op jit(solution)/shard_map/concatenate | solution.py:208
  57.1 2.0 %fusion.19.refs_2_ = bf16[1024,128]{1,0:T(8,128)(2,1)S(1)} fusion(bf16[128,3584]{1,0:T(8,128)(2,1)S(1)} %copy-done.5, bf16[512,3584]{1,0:T(8,128)(2,1)S(1)} %bitcast.41, bf16[512,3584]{1,0:T(8,128)(2,1)S(1)} %bitcast.38), kind=kOutput, calls=%fused_computation.20 | convolution fusion | flops 954335232 | bytes 8519680 | tf_op jit(solution)/shard_map/dot_general | solution.py:226
  59.9 3.7 %constant_dynamic-slice_fusion.11 = (bf16[1024,896]{1,0:T(8,128)(2,1)S(1)}, bf16[1024,896]{1,0:T(8,128)(2,1)S(1)}, bf16[1024,896]{1,0:T(8,128)(2,1)S(1)}, bf16[1024,896]{1,0:T(8,128)(2,1)S(1)}) fusion(bf16[1024,1792]{1,0:T(8,128)(2,1)} %get-tuple-element.19, s32[]{:T(128)S(6)} %select_n.326, s32[]{:T(128)S(6)} %select_n.331, ...), kind=kLoop, calls=%fused_computation.124 | loop fusion | bytes 14680080 | tf_op jit(solution)/shard_map/dynamic_slice | solution.py:29
  63.7 2.2 %fusion.8 = f32[1024,128]{1,0:T(8,128)S(1)} fusion(bf16[1024,896]{1,0:T(8,128)(2,1)S(1)} %get-tuple-element.23, bf16[1024,896]{1,0:T(8,128)(2,1)S(1)} %get-tuple-element.60, bf16[896,128]{1,0:T(8,128)(2,1)} %collective-permute-done.4, bf16[896,128]{1,0:T(8,128)(2,1)} %collective-permute-done.3), kind=kOutput, calls=%fused_computation.13 | convolution fusion | flops 478019584 | bytes 4653056 | tf_op jit(solution)/shard_map/dot_general | solution.py:285
  67.0 3.1 %collective-permute-done.10 = bf16[1392,128]{1,0:T(8,128)(2,1)S(1)} collective-permute-done((bf16[1392,128]{1,0:T(8,128)(2,1)S(1)}, bf16[1392,128]{1,0:T(8,128)(2,1)S(1)}, u32[]{:S(2)}, u32[]{:S(2)}) %collective-permute-start.10) | collective-permute-done | bytes 356384 | tf_op jit(solution)/shard_map/ppermute | solution.py:21
  71.7 5.8 %shard_map.111 = f32[8,256]{1,0:T(8,128)S(1)} custom-call(bf16[1024,128]{1,0:T(8,128)(2,1)S(1)} %fusion.18.refs_0_, bf16[1024,128]{1,0:T(8,128)(2,1)S(1)} %fusion.15.refs_1_, bf16[1024,128]{1,0:T(8,128)(2,1)S(1)} %fusion.19.refs_2_, bf16[1024,128]{1,0:T(8,128)(2,1)S(1)} %slice.175.refs_3_, bf16[1024,128]{1,0:T(8,128)(2,1)S(1)} %collective-permute-done.11.refs_4_, ...), custom_call_target="tpu_custom_call" | custom-call | tf_op jit(solution)/shard_map/pallas_call | solution.py:288
  79.5 3.0 %collective-permute-done.14 = f32[8,256]{1,0:T(8,128)S(1)} collective-permute-done((f32[8,256]{1,0:T(8,128)S(1)}, f32[8,256]{1,0:T(8,128)S(1)}, u32[]{:S(2)}, u32[]{:S(2)}) %collective-permute-start.14) | collective-permute-done | bytes 8224 | tf_op jit(solution)/shard_map/ppermute | solution.py:21
  83.2 2.8 %collective-permute-done.15 = f32[8,256]{1,0:T(8,128)S(1)} collective-permute-done((f32[8,256]{1,0:T(8,128)S(1)}, f32[8,256]{1,0:T(8,128)S(1)}, u32[]{:S(2)}, u32[]{:S(2)}) %collective-permute-start.15) | collective-permute-done | bytes 8224 | tf_op jit(solution)/shard_map/ppermute | solution.py:21
  86.1 1.6 %collective-permute-start.16 = (f32[16,256]{1,0:T(8,128)S(1)}, f32[16,256]{1,0:T(8,128)S(1)}, u32[]{:S(2)}, u32[]{:S(2)}) collective-permute-start(f32[16,256]{1,0:T(8,128)S(1)} %pad_maximum_fusion.15), channel_id=1, source_target_pairs={{0,8},{4,12},{8,0},{12,4},{16,24},{20,28},{24,16},{28,20},{1,9},{5... | collective-permute-start | bytes 49160 | tf_op jit(solution)/shard_map/ppermute | solution.py:21
  87.7 2.1 %collective-permute-done.16 = f32[16,256]{1,0:T(8,128)S(1)} collective-permute-done((f32[16,256]{1,0:T(8,128)S(1)}, f32[16,256]{1,0:T(8,128)S(1)}, u32[]{:S(2)}, u32[]{:S(2)}) %collective-permute-start.16) | collective-permute-done | bytes 16416 | tf_op jit(solution)/shard_map/ppermute | solution.py:21
  89.8 2.6 %collective-permute-start.17 = (f32[32,256]{1,0:T(8,128)S(1)}, f32[32,256]{1,0:T(8,128)S(1)}, u32[]{:S(2)}, u32[]{:S(2)}) collective-permute-start(f32[32,256]{1,0:T(8,128)S(1)} %pad_maximum_fusion.13), channel_id=1, source_target_pairs={{0,16},{4,20},{8,24},{12,28},{16,0},{20,4},{24,8},{28,12},{1,17},{... | collective-permute-start | bytes 98312 | tf_op jit(solution)/shard_map/ppermute | solution.py:21
  95.3 2.4 %shard_map.112 = bf16[4,4,64]{2,1,0:T(4,128)(2,1)} custom-call(f32[64,256]{1,0:T(8,128)} %pad_maximum_fusion.11.rows_ref, f32[16,64]{1,0:T(8,128)} %fusion.59.sel_ref, f32[16,16]{1,0:T(8,128)} %fusion.66.allow_ref, f32[16,1]{1,0:T(8,128)} %copy.22.fill_ref, f32[1,256]{1,0:T(1,128)} %bitcast.48, bf16[3,64,256]{2,1,0:T(8,128)(2,1)} %bitcast.46), custom_call_target="tpu_custom_call" | custom-call | tf_op jit(solution)/shard_map/pallas_call | solution.py:317
  (100 shorter events, 25.3 us)
Async XLA Ops:
  0.0 11.1 %copy-start.3 = (bf16[3584,2,32]{0,2,1:T(8,128)(2,1)S(1)}, bf16[3584,2,32]{0,2,1:T(8,128)(2,1)}, u32[]{:S(2)}) copy-start(bf16[3584,2,32]{0,2,1:T(8,128)(2,1)} %param.17) | copy-start | bytes 1376260
  0.0 11.9 %copy-start.4 = (bf16[3584,128]{1,0:T(8,128)(2,1)S(1)}, bf16[3584,128]{1,0:T(8,128)(2,1)}, u32[]{:S(2)}) copy-start(bf16[3584,128]{1,0:T(8,128)(2,1)} %param.16) | copy-start | bytes 2752516
  2.4 16.5 %copy-start.7 = (s32[16,1]{0,1:T(1,128)S(1)}, s32[16,1]{0,1:T(1,128)}, u32[]{:S(2)}) copy-start(s32[16,1]{0,1:T(1,128)} %param.14) | copy-start | bytes 196
  2.5 16.5 %copy-start.8 = (s32[32]{0:T(128)S(1)}, s32[32]{0:T(128)}, u32[]{:S(2)}) copy-start(s32[32]{0:T(128)} %param.13) | copy-start | bytes 388
  3.2 17.4 %collective-permute-start.1 = (bf16[48,3584]{1,0:T(8,128)(2,1)}, bf16[48,3584]{1,0:T(8,128)(2,1)S(1)}, u32[]{:S(2)}, u32[]{:S(2)}) collective-permute-start(bf16[48,3584]{1,0:T(8,128)(2,1)} %maximum_maximum_fusion), channel_id=1, source_target_pairs={{0,2},{1,3},{2,0},{3,1},{4,6},{5,7},{6,4},{7,5},{8,10},{9,11},{10,... | collective-permute-start | bytes 1032200 | tf_op jit(solution)/shard_map/ppermute | solution.py:21
  6.2 33.7 %collective-permute-start = (bf16[8,64,3584]{2,1,0:T(8,128)(2,1)}, bf16[8,64,3584]{2,1,0:T(8,128)(2,1)}, u32[]{:S(2)}, u32[]{:S(2)}) collective-permute-start(bf16[8,64,3584]{2,1,0:T(8,128)(2,1)} %tokens_ref.1), channel_id=1, source_target_pairs={{0,1},{1,0},{2,3},{3,2},{4,5},{5,4},{6,7},{7,6},{8,9},{9,8},{10,11... | collective-permute-start | bytes 11010056 | tf_op jit(solution)/shard_map/ppermute | solution.py:21
  21.3 12.3 %collective-permute-start.6 = (bf16[16,3584]{1,0:T(8,128)(2,1)S(1)}, bf16[16,3584]{1,0:T(8,128)(2,1)S(1)}, u32[]{:S(2)}, u32[]{:S(2)}) collective-permute-start(bf16[16,3584]{1,0:T(8,128)(2,1)S(1)} %get-tuple-element.40), channel_id=1, source_target_pairs={{0,8},{4,12},{8,0},{12,4},{16,24},{20,28},{24,16},{28,20},{1,9},{5... | collective-permute-start | bytes 344072 | tf_op jit(solution)/shard_map/ppermute | solution.py:21
  22.8 5.3 %collective-permute-start.5 = (bf16[16,3584]{1,0:T(8,128)(2,1)S(1)}, bf16[16,3584]{1,0:T(8,128)(2,1)S(1)}, u32[]{:S(2)}, u32[]{:S(2)}) collective-permute-start(bf16[16,3584]{1,0:T(8,128)(2,1)S(1)} %get-tuple-element.41), channel_id=1, source_target_pairs={{0,4},{4,0},{8,12},{12,8},{16,20},{20,16},{24,28},{28,24},{1,5},{5... | collective-permute-start | bytes 344072 | tf_op jit(solution)/shard_map/ppermute | solution.py:21
  24.4 4.4 %collective-permute-start.7 = (bf16[32,3584]{1,0:T(8,128)(2,1)S(1)}, bf16[32,3584]{1,0:T(8,128)(2,1)S(1)}, u32[]{:S(2)}, u32[]{:S(2)}) collective-permute-start(bf16[32,3584]{1,0:T(8,128)(2,1)S(1)} %pad_maximum_fusion.9), channel_id=1, source_target_pairs={{0,1},{1,0},{2,3},{3,2},{4,5},{5,4},{6,7},{7,6},{8,9},{9,8},{10,11... | collective-permute-start | bytes 688136 | tf_op jit(solution)/shard_map/ppermute | solution.py:21
  24.4 12.9 %collective-permute-start.2 = (bf16[1792,128]{1,0:T(8,128)(2,1)S(1)}, bf16[1792,128]{1,0:T(8,128)(2,1)S(1)}, u32[]{:S(2)}, u32[]{:S(2)}) collective-permute-start(bf16[1792,128]{1,0:T(8,128)(2,1)S(1)} %pad_maximum_fusion.7), channel_id=1, source_target_pairs={{0,2},{1,3},{2,0},{3,1},{4,6},{5,7},{6,4},{7,5},{8,10},{9,11},{10,... | collective-permute-start | bytes 1376264 | tf_op jit(solution)/shard_map/ppermute | solution.py:21
  29.2 17.7 %copy-start.6 = (f32[8,1,3584]{2,1,0:T(1,128)S(1)}, f32[8,1,3584]{2,1,0:T(1,128)}, u32[]{:S(2)}) copy-start(f32[8,1,3584]{2,1,0:T(1,128)} %get-tuple-element.13) | copy-start | bytes 344068
  29.2 3.8 %collective-permute-start.8 = (bf16[64,128]{1,0:T(8,128)(2,1)S(1)}, bf16[64,128]{1,0:T(8,128)(2,1)S(1)}, u32[]{:S(2)}, u32[]{:S(2)}) collective-permute-start(bf16[64,128]{1,0:T(8,128)(2,1)S(1)} %convolution_convert_fusion), channel_id=1, source_target_pairs={{0,4},{4,0},{8,12},{12,8},{16,20},{20,16},{24,28},{28,24},{1,5},{5... | collective-permute-start | bytes 49160 | tf_op jit(solution)/shard_map/ppermute | solution.py:21
  33.1 4.0 %collective-permute-start.9 = (bf16[128,128]{1,0:T(8,128)(2,1)S(1)}, bf16[128,128]{1,0:T(8,128)(2,1)S(1)}, u32[]{:S(2)}, u32[]{:S(2)}) collective-permute-start(bf16[128,128]{1,0:T(8,128)(2,1)S(1)} %pad_maximum_fusion.12), channel_id=1, source_target_pairs={{0,8},{4,12},{8,0},{12,4},{16,24},{20,28},{24,16},{28,20},{1,9},{5... | collective-permute-start | bytes 98312 | tf_op jit(solution)/shard_map/ppermute | solution.py:21
  38.2 25.5 %collective-permute-start.3 = (bf16[896,128]{1,0:T(8,128)(2,1)}, bf16[896,128]{1,0:T(8,128)(2,1)}, u32[]{:S(2)}, u32[]{:S(2)}) collective-permute-start(bf16[896,128]{1,0:T(8,128)(2,1)} %get-tuple-element.30), channel_id=1, source_target_pairs={{0,4},{4,0},{8,12},{12,8},{16,20},{20,16},{24,28},{28,24},{1,5},{5... | collective-permute-start | bytes 688136 | tf_op jit(solution)/shard_map/ppermute | solution.py:21
  39.4 24.3 %collective-permute-start.4 = (bf16[896,128]{1,0:T(8,128)(2,1)}, bf16[896,128]{1,0:T(8,128)(2,1)}, u32[]{:S(2)}, u32[]{:S(2)}) collective-permute-start(bf16[896,128]{1,0:T(8,128)(2,1)} %get-tuple-element.31), channel_id=1, source_target_pairs={{0,8},{4,12},{8,0},{12,4},{16,24},{20,28},{24,16},{28,20},{1,9},{5... | collective-permute-start | bytes 688136 | tf_op jit(solution)/shard_map/ppermute | solution.py:21
  48.3 5.4 %copy-start.1 = (bf16[8,64,3584]{2,1,0:T(8,128)(2,1)S(1)}, bf16[8,64,3584]{2,1,0:T(8,128)(2,1)}, u32[]{:S(2)}) copy-start(bf16[8,64,3584]{2,1,0:T(8,128)(2,1)} %get-tuple-element.10) | copy-start | bytes 11010052
  59.2 11.3 %collective-permute-start.11 = (bf16[1024,128]{1,0:T(8,128)(2,1)S(1)}, bf16[1024,128]{1,0:T(8,128)(2,1)S(1)}, u32[]{:S(2)}, u32[]{:S(2)}) collective-permute-start(bf16[1024,128]{1,0:T(8,128)(2,1)S(1)} %fusion.19.refs_2_), channel_id=1, source_target_pairs={{0,1},{1,0},{2,3},{3,2},{4,5},{5,4},{6,7},{7,6},{8,9},{9,8},{10,11... | collective-permute-start | bytes 786440 | tf_op jit(solution)/shard_map/ppermute | solution.py:21
  59.3 10.8 %collective-permute-start.10 = (bf16[1392,128]{1,0:T(8,128)(2,1)S(1)}, bf16[1392,128]{1,0:T(8,128)(2,1)S(1)}, u32[]{:S(2)}, u32[]{:S(2)}) collective-permute-start(bf16[1392,128]{1,0:T(8,128)(2,1)S(1)} %pad_maximum_fusion.8), channel_id=1, source_target_pairs={{0,2},{1,3},{2,0},{3,1},{4,6},{5,7},{6,4},{7,5},{8,10},{9,11},{10,... | collective-permute-start | bytes 1069064 | tf_op jit(solution)/shard_map/ppermute | solution.py:21
  70.1 1.6 %collective-permute-start.12 = (bf16[1024,128]{1,0:T(8,128)(2,1)S(1)}, bf16[1024,128]{1,0:T(8,128)(2,1)S(1)}, u32[]{:S(2)}, u32[]{:S(2)}) collective-permute-start(bf16[1024,128]{1,0:T(8,128)(2,1)S(1)} %slice.175.refs_3_), channel_id=1, source_target_pairs={{0,1},{1,0},{2,3},{3,2},{4,5},{5,4},{6,7},{7,6},{8,9},{9,8},{10,11... | collective-permute-start | bytes 786440 | tf_op jit(solution)/shard_map/ppermute | solution.py:21
  77.5 1.2 %collective-permute-start.13 = (f32[8,256]{1,0:T(8,128)S(1)}, f32[8,256]{1,0:T(8,128)S(1)}, u32[]{:S(2)}, u32[]{:S(2)}) collective-permute-start(f32[8,256]{1,0:T(8,128)S(1)} %shard_map.111), channel_id=1, source_target_pairs={{0,1},{1,0},{2,3},{3,2},{4,5},{5,4},{6,7},{7,6},{8,9},{9,8},{10,11... | collective-permute-start | bytes 24584 | tf_op jit(solution)/shard_map/ppermute | solution.py:21
  78.8 3.7 %collective-permute-start.14 = (f32[8,256]{1,0:T(8,128)S(1)}, f32[8,256]{1,0:T(8,128)S(1)}, u32[]{:S(2)}, u32[]{:S(2)}) collective-permute-start(f32[8,256]{1,0:T(8,128)S(1)} %add.372), channel_id=1, source_target_pairs={{0,2},{1,3},{2,0},{3,1},{4,6},{5,7},{6,4},{7,5},{8,10},{9,11},{10,... | collective-permute-start | bytes 24584 | tf_op jit(solution)/shard_map/ppermute | solution.py:21
  82.4 3.7 %collective-permute-start.15 = (f32[8,256]{1,0:T(8,128)S(1)}, f32[8,256]{1,0:T(8,128)S(1)}, u32[]{:S(2)}, u32[]{:S(2)}) collective-permute-start(f32[8,256]{1,0:T(8,128)S(1)} %add.373), channel_id=1, source_target_pairs={{0,4},{4,0},{8,12},{12,8},{16,20},{20,16},{24,28},{28,24},{1,5},{5... | collective-permute-start | bytes 24584 | tf_op jit(solution)/shard_map/ppermute | solution.py:21
  86.1 3.7 %collective-permute-start.16 = (f32[16,256]{1,0:T(8,128)S(1)}, f32[16,256]{1,0:T(8,128)S(1)}, u32[]{:S(2)}, u32[]{:S(2)}) collective-permute-start(f32[16,256]{1,0:T(8,128)S(1)} %pad_maximum_fusion.15), channel_id=1, source_target_pairs={{0,8},{4,12},{8,0},{12,4},{16,24},{20,28},{24,16},{28,20},{1,9},{5... | collective-permute-start | bytes 49160 | tf_op jit(solution)/shard_map/ppermute | solution.py:21
  89.8 4.8 %collective-permute-start.17 = (f32[32,256]{1,0:T(8,128)S(1)}, f32[32,256]{1,0:T(8,128)S(1)}, u32[]{:S(2)}, u32[]{:S(2)}) collective-permute-start(f32[32,256]{1,0:T(8,128)S(1)} %pad_maximum_fusion.13), channel_id=1, source_target_pairs={{0,16},{4,20},{8,24},{12,28},{16,0},{20,4},{24,8},{28,12},{1,17},{... | collective-permute-start | bytes 98312 | tf_op jit(solution)/shard_map/ppermute | solution.py:21
  (3 other events, 9.8 us)

commit v3 on v1

v3 whole, which is shorter than its diff:
```python
import functools

import jax
import jax.numpy as jnp
from jax import lax
from jax.experimental import pallas as pl
from jax.experimental.pallas import tpu as pltpu
from jax.sharding import PartitionSpec as P

CAP = 8
DOC_MOST = 4
OWN_DOCS = 4
F32 = jnp.float32
BF16 = jnp.bfloat16
HIGH = lax.Precision.HIGHEST
VMEM = 48 * 2**20
NT = (((1,), (1,)), ((), ()))


def flipped(block, axis, mask):
    count = lax.axis_size(axis)
    return lax.ppermute(block, axis, [(i, i ^ mask) for i in range(count)])


def cut(array, at, size, axis):
    return lax.dynamic_slice_in_dim(array, at * size, size, axis=axis)


def slot_table(seg_replica):
    replica_of = seg_replica[:, 0]
    order = jnp.arange(replica_of.shape[0], dtype=jnp.int32)
    earlier = (replica_of[None, :] == replica_of[:, None]) & (order[None, :] < order[:, None])
    return replica_of, jnp.sum(earlier.astype(jnp.int32), axis=1)


def owner_rows(doc_of_segment, doc_owner):
    owner_of = doc_owner[:, 0]
    doc_ids = jnp.arange(owner_of.shape[0], dtype=jnp.int32)
    earlier = (owner_of[None, :] == owner_of[:, None]) & (doc_ids[None, :] < doc_ids[:, None])
    doc_rank = jnp.sum(earlier.astype(jnp.int32), axis=1)
    start_of = jnp.sum((doc_of_segment[None, :] < doc_ids[:, None]).astype(jnp.int32), axis=1)
    matches = doc_of_segment[:, None] == doc_ids[None, :]
    seg_owner = jnp.sum(jnp.where(matches, owner_of[None, :], 0), axis=1)
    seg_rank = jnp.sum(jnp.where(matches, doc_rank[None, :], 0), axis=1)
    seg_start = jnp.sum(jnp.where(matches, start_of[None, :], 0), axis=1)
    position = jnp.arange(doc_of_segment.shape[0], dtype=jnp.int32) - seg_start
    return seg_owner * (OWN_DOCS * DOC_MOST) + seg_rank * DOC_MOST + position


def lane_step(width):
    step = 512
    while width % step:
        step //= 2
    return step


def token_kernel(tokens_ref, query_ref, q_ref, scale_ref, sum_ref):
    slots, count, width = tokens_ref.shape
    head_dim = query_ref.shape[1]
    step = lane_step(width)
    for s in range(slots):
        squares = jnp.zeros((count, 128), F32)
        for at in range(0, width, step):
            x = tokens_ref[s, :, at:at + step].astype(F32)
            sum_ref[s:s + 1, at:at + step] = jnp.sum(x, axis=0, keepdims=True)
            x = x * x
            for i in range(0, step, 128):
                squares += x[:, i:i + 128]
        mean = jnp.sum(squares, axis=1, keepdims=True) * (1.0 / width)
        scale_ref[s * count:(s + 1) * count, :] = jnp.broadcast_to(
            lax.rsqrt(mean + 1e-06), (count, head_dim)
        )
    tokens = tokens_ref[...].reshape(slots * count, width)
    q = jnp.dot(tokens, query_ref[...], preferred_element_type=F32)
    q_ref[...] = (q * scale_ref[...]).astype(BF16)


def token_parts(tokens, query):
    slots, count, width = tokens.shape
    head_dim = query.shape[1]
    rows = slots * count
    return pl.pallas_call(
        token_kernel,
        out_shape=[
            jax.ShapeDtypeStruct((rows, head_dim), BF16),
            jax.ShapeDtypeStruct((rows, head_dim), F32),
            jax.ShapeDtypeStruct((slots, width), F32),
        ],
        compiler_params=pltpu.CompilerParams(vmem_limit_bytes=VMEM),
        cost_estimate=pl.CostEstimate(
            flops=2 * rows * width * head_dim, bytes_accessed=2 * rows * width, transcendentals=0
        ),
    )(tokens, query)


def keyvalue_kernel(near_ref, far_ref, near_scale_ref, far_scale_ref, *refs):
    weight_refs, kv_ref = refs[:-1], refs[-1]
    slots, count, width = near_ref.shape
    rows = slots * count
    weights = jnp.concatenate([w[...] for w in weight_refs], axis=0)
    for c, (x_ref, scale_ref) in enumerate(((near_ref, near_scale_ref), (far_ref, far_scale_ref))):
        kv = lax.dot_general(x_ref[...].reshape(rows, width), weights, NT, preferred_element_type=F32)
        kv_ref[c * rows:(c + 1) * rows, :] = (kv * scale_ref[:, :1]).astype(BF16)


def half_query(x_ref, b_ref, c_ref, turn):
    slots, count, width = x_ref.shape
    part = b_ref.shape[0]
    rep = lax.axis_index("rep")
    at_b = pl.multiple_of((lax.rem(rep, 2) ^ turn) * part, 128)
    at_c = pl.multiple_of((2 + (lax.rem(rep // 2, 2) ^ turn)) * part, 128)
    rows = slots * count
    total = jnp.dot(
        x_ref[:, :, pl.ds(at_b, part)].reshape(rows, part), b_ref[...], preferred_element_type=F32
    )
    return total + jnp.dot(
        x_ref[:, :, pl.ds(at_c, part)].reshape(rows, part), c_ref[...], preferred_element_type=F32
    )


def early_kernel(near_ref, far_ref, b_ref, c_ref, out_ref):
    rows = out_ref.shape[0] // 2
    out_ref[:rows, :] = half_query(near_ref, b_ref, c_ref, 0)
    out_ref[rows:, :] = half_query(far_ref, b_ref, c_ref, 0)


def product_kernel(masks, output_ref, *refs):
    proj_refs, out_ref = refs[:-1], refs[-1]
    total = jnp.zeros(out_ref.shape, F32)
    for mask, proj_ref in zip(masks, proj_refs):
        total += lax.dot_general(proj_ref[...], output_ref[mask], NT, preferred_element_type=F32)
    out_ref[...] = total.astype(BF16)


def split(value):
    high = value.astype(BF16)
    return jnp.concatenate([high, (value - high.astype(F32)).astype(BF16)], axis=0)


def joined(value):
    half = value.shape[0] // 2
    return value[:half] + value[half:]


def attention_kernel(masks, group, length, *refs):
    n = len(masks)
    at = iter(range(len(refs)))

    def take(count):
        return [refs[next(at)] for _ in range(count)]

    x_refs = take(2)
    scale_refs = take(2)
    query_ref, = take(1)
    early_refs, b_refs, c_refs = take(n - 1), take(n - 1), take(n - 1)
    near_refs, far_refs = take(n), take(n)
    w2_refs = [take(2) for _ in range(n)]
    place_ref, mean_ref, proj_ref, out_ref, q_ref, kv_ref, score_ref, weight_ref, ctx_ref, w2_ref = take(10)
    slots, tokens, _ = x_refs[0].shape
    head_dim = query_ref.shape[1]
    rows = slots * tokens
    groups = sorted({m // group for m in masks})
    heads_of = [[p for p in range(n) if masks[p] // group == g] for g in groups]
    in_group = len(heads_of[0])

    rep = lax.axis_index("rep")
    quarter = lax.rem(rep, 4)
    part = w2_ref.shape[1] // 4
    for p in range(n):
        for i in range(4):
            at_row = pl.multiple_of((quarter ^ i) * part, part)
            w2_ref[p, pl.ds(at_row, part), :] = w2_refs[p][i // 2][i % 2 * part:(i % 2 + 1) * part, :]

    for p in range(n):
        for c in range(2):
            mixed = jnp.concatenate(
                [
                    near_refs[p][c * rows:(c + 1) * rows, :],
                    far_refs[p][(1 - c) * rows:(2 - c) * rows, :],
                ],
                axis=1,
            )
            kv_ref[p, c * rows:(c + 1) * rows, :] = jnp.dot(
                mixed, place_ref[p], preferred_element_type=F32
            ).astype(BF16)
    q_ref[0] = query_ref[...]
    for p in range(1, n):
        for c in range(2):
            span = slice(c * rows, (c + 1) * rows)
            q = early_refs[p - 1][span, :] + half_query(x_refs[c], b_refs[p - 1], c_refs[p - 1], 1)
            q_ref[p, span, :] = (q * scale_refs[c][...]).astype(BF16)

    def spans(s):
        return [slice(c * rows + s * tokens, c * rows + (s + 1) * tokens) for c in range(2)]

    def columns(s, first):
        return jnp.concatenate(
            [kv_ref[p, span, first:first + head_dim] for p in range(n) for span in spans(s)], axis=0
        )

    for s in range(slots):
        for g, heads in enumerate(heads_of):
            q = jnp.concatenate([q_ref[p, span, :] for p in heads for span in spans(s)], axis=0)
            keys = columns(s, g * 2 * head_dim)
            score_ref[s, g] = lax.dot_general(q, keys, NT, preferred_element_type=F32)
    for s in range(slots):
        for g in range(len(groups)):
            scores = score_ref[s, g]
            top = jnp.max(scores, axis=1, keepdims=True)
            e = jnp.exp((scores - top) * head_dim ** (-0.5))
            probs = e * (1.0 / jnp.sum(e, axis=1, keepdims=True))
            weight_ref[s, g] = jnp.sum(probs.reshape(in_group, 2 * tokens, -1), axis=1)
    for s in range(slots):
        for g, heads in enumerate(heads_of):
            values = columns(s, (g * 2 + 1) * head_dim)
            context = joined(
                jnp.dot(split(weight_ref[s, g]), values, preferred_element_type=F32)
            ) * (1.0 / length)
            for j, p in enumerate(heads):
                ctx_ref[p, s:s + 1, :] = context[j:j + 1]
    total = joined(jnp.dot(split(mean_ref[...]), proj_ref[...], preferred_element_type=F32))
    for p in range(n):
        total += joined(
            lax.dot_general(split(ctx_ref[p]), w2_ref[p], NT, preferred_element_type=F32)
        )
    out_ref[...] = total


def document_kernel(rows_ref, sel_ref, allow_ref, fill_ref, gain_ref, qkv_ref, out_ref):
    docs, most, head = out_ref.shape
    first = jnp.dot(sel_ref[...], rows_ref[...], preferred_element_type=F32, precision=HIGH)
    scale = lax.rsqrt(jnp.mean(first * first, axis=-1, keepdims=True) + 1e-06)
    normed = (first * scale * gain_ref[...]).astype(BF16)
    q, k, v = (
        lax.dot_general(normed, qkv_ref[i], NT, preferred_element_type=F32).astype(BF16) for i in range(3)
    )
    scores = lax.dot_general(q, k, NT, preferred_element_type=F32) * head ** (-0.5)
    scores = jnp.where(allow_ref[...] > 0.5, scores, -1e30)
    e = jnp.exp(scores - jnp.max(scores, axis=1, keepdims=True))
    probs = (e / jnp.sum(e, axis=1, keepdims=True)).astype(BF16)
    context = jnp.dot(probs, v, preferred_element_type=F32) * fill_ref[...]
    for d in range(docs):
        out_ref[d] = context[d * most:(d + 1) * most].astype(BF16)


def local(
    tokens,
    seg_replica,
    doc_of_segment,
    doc_owner,
    enc_gain,
    enc_query,
    enc_keyvalue,
    enc_output,
    doc_proj,
    doc_gain,
    doc_qkv,
):
    n_rep, n_tp = lax.axis_size("rep"), lax.axis_size("tp")
    rep_index = lax.axis_index("rep")
    tp_index = lax.axis_index("tp")
    x_bit, z_bit = rep_index % 2, rep_index // 2 % 2
    slots, own_tokens, width = tokens.shape
    length = own_tokens * n_tp
    head_dim = enc_query.shape[1]
    kv_width = enc_keyvalue.shape[2]
    group = head_dim // kv_width
    block, doc_width = doc_proj.shape
    masks = list(range(0, n_tp, 2))

    kv_rows = (jnp.transpose(enc_keyvalue, (1, 2, 0)).astype(F32) * enc_gain).astype(BF16)
    query = (enc_query.astype(F32) * enc_gain[:, None]).astype(BF16)
    part_kv, part_q, part_doc = kv_width // 2, width // 4, doc_width // 4
    keys_y = [flipped(cut(kv_rows[0], x_bit, part_kv, 0), "tp", m) for m in masks[1:]]
    values_y = [flipped(cut(kv_rows[1], z_bit, part_kv, 0), "tp", m) for m in masks[1:]]
    tokens_far = flipped(tokens, "tp", 1)
    proj = cut(doc_proj, z_bit * 2 + x_bit, part_doc, 1).T
    proj_near = [proj] + [flipped(proj, "tp", m) for m in masks[1:]]
    b_y = [flipped(cut(query, x_bit, part_q, 0), "tp", m) for m in masks[1:]]
    c_y = [flipped(cut(query, 2 + z_bit, part_q, 0), "tp", m) for m in masks[1:]]

    q_near, scale_near, sums_near = token_parts(tokens, query)

    weights = [kv_rows.reshape(2 * kv_width, width)]
    for k, v in zip(keys_y, values_y):
        weights += [k, flipped(k, "rep", 1), v, flipped(v, "rep", 2)]
    q_far, scale_far, sums_far = token_parts(tokens_far, query)

    rows = slots * own_tokens
    lanes = 2 * kv_width * len(masks)
    kv = pl.pallas_call(
        keyvalue_kernel,
        out_shape=jax.ShapeDtypeStruct((2 * rows, lanes), BF16),
        compiler_params=pltpu.CompilerParams(vmem_limit_bytes=VMEM),
        cost_estimate=pl.CostEstimate(
            flops=4 * rows * width * lanes, bytes_accessed=4 * rows * width, transcendentals=0
        ),
    )(tokens, tokens_far, scale_near, scale_far, *weights)
    kv_near = [kv] + [flipped(kv, "tp", m) for m in masks[1:]]
    kv_far = [flipped(k, "tp", 1) for k in kv_near]

    proj_all = proj_near + [flipped(p, "tp", 1) for p in proj_near]
    origin = masks + [m + 1 for m in masks]
    output_blocks = jnp.stack([cut(enc_output, tp_index ^ m, block, 1) for m in range(n_tp)], axis=0)
    w2 = pl.pallas_call(
        functools.partial(product_kernel, origin),
        out_shape=jax.ShapeDtypeStruct((part_doc, head_dim), BF16),
        compiler_params=pltpu.CompilerParams(vmem_limit_bytes=VMEM),
    )(output_blocks, *proj_all)
    w2 = jnp.concatenate([w2, flipped(w2, "rep", 1)], axis=0)
    w2_pair = [w2, flipped(w2, "rep", 2)]
    w2_all = w2_pair + [flipped(w, "tp", m) for m in masks[1:] for w in w2_pair]

    mean = ((sums_near + sums_far) * (1.0 / length)).reshape(slots, n_tp, block)

    def mean_of(m):
        return lax.dynamic_index_in_dim(mean, tp_index ^ m, 1, keepdims=False)

    mean_here = mean_of(0)
    for m in masks[1:]:
        mean_here = mean_here + flipped(mean_of(m), "tp", m)

    count = 2 * lanes
    column = jnp.arange(count, dtype=jnp.int32)
    core = column // lanes
    mask_of = column % lanes // (2 * kv_width) * 2
    inner = column % (2 * kv_width)
    quarter = inner // part_kv
    turn = jnp.where(quarter < 2, x_bit, z_bit)
    swapped = quarter // 2 * 2 + (quarter % 2 ^ turn)
    inner = jnp.where(mask_of == 0, inner, swapped * part_kv + inner % part_kv)
    places = []
    for m in masks:
        target = (
            (mask_of ^ m) // group * (2 * head_dim)
            + inner // kv_width * head_dim
            + (tp_index ^ m ^ mask_of ^ core) % group * kv_width
            + inner % kv_width
        )
        places.append((target[:, None] == column[None, :]).astype(BF16))
    place = jnp.stack(places, axis=0)

    early, b_rest, c_rest = [], [], []
    for q_b, q_c in zip(b_y, c_y):
        b_rest.append(flipped(q_b, "rep", 1))
        c_rest.append(flipped(q_c, "rep", 2))
        early.append(
            pl.pallas_call(
                early_kernel,
                out_shape=jax.ShapeDtypeStruct((2 * rows, head_dim), F32),
                compiler_params=pltpu.CompilerParams(vmem_limit_bytes=VMEM),
                cost_estimate=pl.CostEstimate(
                    flops=2 * rows * width * head_dim, bytes_accessed=2 * rows * width, transcendentals=0
                ),
            )(tokens, tokens_far, q_b, q_c)
        )

    n = len(masks)
    groups = n_tp // group
    part = pl.pallas_call(
        functools.partial(attention_kernel, masks, group, length),
        out_shape=jax.ShapeDtypeStruct((slots, doc_width), F32),
        scratch_shapes=[
            pltpu.VMEM((n, 2 * rows, head_dim), BF16),
            pltpu.VMEM((n, 2 * rows, 2 * lanes), BF16),
            pltpu.VMEM((slots, groups, n // groups * 2 * own_tokens, length), F32),
            pltpu.VMEM((slots, groups, n // groups, length), F32),
            pltpu.VMEM((n, slots, head_dim), F32),
            pltpu.VMEM((n, doc_width, head_dim), BF16),
        ],
        compiler_params=pltpu.CompilerParams(vmem_limit_bytes=VMEM),
    )(
        tokens,
        tokens_far,
        scale_near,
        scale_far,
        jnp.concatenate([q_near, q_far], axis=0),
        *early,
        *b_rest,
        *c_rest,
        *kv_near,
        *kv_far,
        *w2_all,
        place,
        mean_here,
        doc_proj,
    )

    bit = 1
    while bit < n_tp:
        part = part + flipped(part, "tp", bit)
        bit *= 2
    bit = 1
    while bit < n_rep:
        part = jnp.concatenate([part, flipped(part, "rep", bit)], axis=0)
        bit *= 2

    replica_of, rank = slot_table(seg_replica)
    row_of = owner_rows(doc_of_segment, doc_owner)
    owned = OWN_DOCS * DOC_MOST
    wanted = rep_index * owned + jnp.arange(owned, dtype=jnp.int32)
    matches = (row_of[None, :] == wanted[:, None]).astype(F32)
    at_slot = (replica_of ^ rep_index) * CAP + rank
    holds = (at_slot[:, None] == jnp.arange(n_rep * CAP, dtype=jnp.int32)[None, :]).astype(F32)
    select = jnp.dot(matches, holds)
    filled = jnp.sum(matches, axis=1)
    row = jnp.arange(owned, dtype=jnp.int32)
    same_doc = row[:, None] // DOC_MOST == row[None, :] // DOC_MOST
    allowed = same_doc & ((filled[None, :] > 0.5) | (row[:, None] == row[None, :]))

    return pl.pallas_call(
        document_kernel,
        out_shape=jax.ShapeDtypeStruct((OWN_DOCS, DOC_MOST, doc_qkv.shape[2]), BF16),
    )(
        part,
        select,
        allowed.astype(F32),
        filled[:, None],
        doc_gain[None, :],
        jnp.transpose(doc_qkv, (1, 2, 0)),
    )


def solution(mesh):
    in_specs = (
        P("rep", "tp", None),
        P(),
        P(),
        P(),
        P(),
        P(None, "tp"),
        P(None, None, "tp"),
        P("tp", None),
        P("tp", None),
        P(),
        P(None, None, "tp"),
    )
    out_specs = P("rep", None, "tp")
    return jax.shard_map(local, mesh=mesh, in_specs=in_specs, out_specs=out_specs, check_vma=False)
```

time: 96.1 us -> 79.5 us (0.83)
  waiting for transfers between devices: 34.2 us -> 16.9 us
  matrix products: 18 us -> 0.79 us
  Pallas kernels: 6.66 us -> 22.7 us
  other arithmetic: 10.2 us -> 4.23 us
  starting transfers between devices: 21.1 us -> 25.2 us
  local copies, waits for them, and re-layouts: 5.12 us -> 9.07 us
    ppermute x23 -> x25, waiting for transfers between devices: 34.2 us -> 16.9 us  [flipped(): return lax.ppermute(block, axis, [(i, i ^ mask) for i in range(count)])]
    dot_general x10 -> x0, matrix products: 17.2 us -> none  [the longest x4 10.5 us: local(): jnp.dot(normed, w, preferred_element_type=F32).astype(BF16)]
    pallas_call x1 -> x6, Pallas kernels: 4.24 us -> 20.3 us  [the longest x2 6.06 us: token_parts(): pl.pallas_call(token_kernel, out_shape=[jax.ShapeDtypeStruct((rows, head_...]
    ppermute x23 -> x25, starting transfers between devices: 21.1 us -> 25.2 us  [flipped(): return lax.ppermute(block, axis, [(i, i ^ mask) for i in range(count)])]
    reduce_sum x1 -> x0, other arithmetic: 3.72 us -> none  [local(): sums = jnp.sum(raw, axis=1) * (1.0 / length)]
    dynamic_slice x3 -> x4, local copies, waits for them, and re-layouts: 1.6 us -> 3.26 us  [cut(): return lax.dynamic_slice_in_dim(array, at * size, size, axis=axis)]
    convert_element_type x1 -> x3, other arithmetic: 3.21 us -> 1.73 us  [the longest x2 1.19 us: local(): (jnp.transpose(enc_keyvalue, (1, 2, 0)).astype(F32) * enc_gain).astype(BF16)]
    another operation x0 -> x1, local copies, waits for them, and re-layouts: none -> 1.37 us  [local(): jnp.stack([cut(enc_output, tp_index ^ m, block, 1) for m in range(n_tp)],...]
  transfers between devices with their start and end apart: 23 -> 25, of which waited for: 7 -> 8; matrix products, arithmetic and copies ran while one was open for 29% -> 11% of each run, Pallas kernels for 0% -> 19%
where the time goes in v3:
time: 79.5 us; the launch traced here: 79.2 us
  starting transfers between devices  25.2 us (32%)
  Pallas kernels  22.7 us (29%)
  waiting for transfers between devices  16.9 us (21%)
  local copies, waits for them, and re-layouts  9.07 us (11%)
  other arithmetic  4.23 us (5%)
    ppermute x25, starting transfers between devices, flipped(): return lax.ppermute(block, axis, [(i, i ^ mask) for i in range(count)])  25.2 us
    ppermute x25, waiting for transfers between devices, flipped(): return lax.ppermute(block, axis, [(i, i ^ mask) for i in range(count)])  16.9 us
    pallas_call x2, Pallas kernels, token_parts(): pl.pallas_call(token_kernel, out_shape=[jax.ShapeDtypeStruct((rows, head_...  6.06 us
    pallas_call x1, Pallas kernels, local(): pl.pallas_call(functools.partial(attention_kernel, masks, group, length),...  5.62 us
    pallas_call x1, Pallas kernels, local(): pl.pallas_call(keyvalue_kernel, out_shape=jax.ShapeDtypeStruct((2 * rows,...  4.09 us
    unnamed x23, local copies, waits for them, and re-layouts  3.72 us
    dynamic_slice x4, local copies, waits for them, and re-layouts, cut(): return lax.dynamic_slice_in_dim(array, at * size, size, axis=axis)  3.26 us
    pallas_call x1, Pallas kernels, local(): pl.pallas_call(early_kernel, out_shape=jax.ShapeDtypeStruct((2 * rows, he...  3.15 us
  transfers between devices with their start and end apart: 25, of which 8 were waited for; matrix products, arithmetic and copies ran while one was open for 11% of the time, Pallas kernels for 19%

profile of v3, /device:TPU:0, one launch (start us, length us, event | category | flops | bytes accessed | tf_op | source)
XLA Modules:
  0.0 79.2 jit_solution(17650681197828226555)
XLA Ops:
  1.3 3.0 %collective-permute-start.12 = (bf16[64,896]{1,0:T(8,128)(2,1)S(1)}, bf16[64,896]{1,0:T(8,128)(2,1)S(1)}, u32[]{:S(2)}, u32[]{:S(2)}) collective-permute-start(bf16[64,896]{1,0:T(8,128)(2,1)S(1)} %bitcast.34), channel_id=1, source_target_pairs={{0,2},{1,3},{2,0},{3,1},{4,6},{5,7},{6,4},{7,5},{8,10},{9,11},{10,... | collective-permute-start | bytes 344072 | tf_op jit(solution)/shard_map/ppermute | solution.py:22
  8.1 1.7 %collective-permute-start.1 = (bf16[896,128]{1,0:T(8,128)(2,1)}, bf16[896,128]{1,0:T(8,128)(2,1)S(1)}, u32[]{:S(2)}, u32[]{:S(2)}) collective-permute-start(bf16[896,128]{1,0:T(8,128)(2,1)} %get-tuple-element.25), channel_id=1, source_target_pairs={{0,2},{1,3},{2,0},{3,1},{4,6},{5,7},{6,4},{7,5},{8,10},{9,11},{10,... | collective-permute-start | bytes 688136 | tf_op jit(solution)/shard_map/ppermute | solution.py:22
  10.5 1.4 %dynamic-slice_bitcast_fusion.3 = (bf16[1,128,896]{2,1,0:T(8,128)(2,1)S(1)}, bf16[1,128,896]{2,1,0:T(8,128)(2,1)S(1)}, bf16[1,128,896]{2,1,0:T(8,128)(2,1)S(1)}, bf16[1,128,896]{2,1,0:T(8,128)(2,1)S(1)}) fusion(bf16[128,3584]{1,0:T(8,128)(2,1)} %param.18, s32[]{:T(128)S(6)} %select_n.277, s32[]{:T(128)S(6)} %select_n.278, s32[]{:T(128)S(6)} %select_n.280, ...), kind=kLoop, calls=%fused_computation.10 | loop fusion | bytes 1835024 | tf_op jit(solution)/shard_map/stack | solution.py:304
  14.7 1.7 %collective-permute-start.5 = (bf16[16,3584]{1,0:T(8,128)(2,1)}, bf16[16,3584]{1,0:T(8,128)(2,1)S(1)}, u32[]{:S(2)}, u32[]{:S(2)}) collective-permute-start(bf16[16,3584]{1,0:T(8,128)(2,1)} %dynamic-slice_bitcast_fusion.5), channel_id=1, source_target_pairs={{0,2},{1,3},{2,0},{3,1},{4,6},{5,7},{6,4},{7,5},{8,10},{9,11},{10,... | collective-permute-start | bytes 344072 | tf_op jit(solution)/shard_map/ppermute | solution.py:22
  17.4 1.4 %shard_map.113 = bf16[64,128]{1,0:T(8,128)(2,1)S(1)} custom-call(bf16[4,128,896]{2,1,0:T(8,128)(2,1)S(1)} %pad_maximum_fusion.output_ref, bf16[64,896]{1,0:T(8,128)(2,1)S(1)} %bitcast.36, bf16[64,896]{1,0:T(8,128)(2,1)S(1)} %collective-permute-done.12.refs_1_, bf16[64,896]{1,0:T(8,128)(2,1)S(1)} %copy-done.4, bf16[64,896]{1,0:T(8,128)(2,1)} %collective-permute-done.14.refs_3_), custom_call_target="tpu_custom_call" | custom-call | tf_op jit(solution)/shard_map/pallas_call | solution.py:305
  18.8 1.6 %collective-permute-start.15 = (bf16[64,128]{1,0:T(8,128)(2,1)S(1)}, bf16[64,128]{1,0:T(8,128)(2,1)S(1)}, u32[]{:S(2)}, u32[]{:S(2)}) collective-permute-start(bf16[64,128]{1,0:T(8,128)(2,1)S(1)} %shard_map.113), channel_id=1, source_target_pairs={{0,4},{4,0},{8,12},{12,8},{16,20},{20,16},{24,28},{28,24},{1,5},{5... | collective-permute-start | bytes 49160 | tf_op jit(solution)/shard_map/ppermute | solution.py:22
  20.3 2.0 %copy-done = bf16[8,64,3584]{2,1,0:T(8,128)(2,1)S(1)} copy-done((bf16[8,64,3584]{2,1,0:T(8,128)(2,1)S(1)}, bf16[8,64,3584]{2,1,0:T(8,128)(2,1)}, u32[]{:S(2)}) %copy-start) | copy-done | bytes 3670040
  22.4 2.0 %shard_map.109 = (bf16[512,128]{1,0:T(8,128)(2,1)S(1)}, f32[512,128]{1,0:T(8,128)S(1)}, f32[8,3584]{1,0:T(8,128)S(1)}) custom-call(bf16[8,64,3584]{2,1,0:T(8,128)(2,1)S(1)} %copy-done, bf16[3584,128]{1,0:T(8,128)(2,1)S(1)} %multiply_convert_fusion.query_ref), custom_call_target="tpu_custom_call" | custom-call | flops 469762048 | bytes 3670016 | tf_op jit(solution)/shard_map/pallas_call | solution.py:82
  24.4 1.6 %collective-permute-start.8 = (bf16[16,3584]{1,0:T(8,128)(2,1)S(1)}, bf16[16,3584]{1,0:T(8,128)(2,1)S(1)}, u32[]{:S(2)}, u32[]{:S(2)}) collective-permute-start(bf16[16,3584]{1,0:T(8,128)(2,1)S(1)} %collective-permute-done.7.refs_3_), channel_id=1, source_target_pairs={{0,8},{4,12},{8,0},{12,4},{16,24},{20,28},{24,16},{28,20},{1,9},{5... | collective-permute-start | bytes 344072 | tf_op jit(solution)/shard_map/ppermute | solution.py:22
  28.5 1.6 %collective-permute-start.16 = (bf16[128,128]{1,0:T(8,128)(2,1)S(1)}, bf16[128,128]{1,0:T(8,128)(2,1)S(1)}, u32[]{:S(2)}, u32[]{:S(2)}) collective-permute-start(bf16[128,128]{1,0:T(8,128)(2,1)S(1)} %pad_maximum_fusion.3.refs_12_), channel_id=1, source_target_pairs={{0,8},{4,12},{8,0},{12,4},{16,24},{20,28},{24,16},{28,20},{1,9},{5... | collective-permute-start | bytes 98312 | tf_op jit(solution)/shard_map/ppermute | solution.py:22
  30.2 4.0 %shard_map.110 = (bf16[512,128]{1,0:T(8,128)(2,1)S(1)}, f32[512,128]{1,0:T(8,128)S(1)}, f32[8,3584]{1,0:T(8,128)S(1)}) custom-call(bf16[8,64,3584]{2,1,0:T(8,128)(2,1)} %collective-permute-done.tokens_ref.far_ref.refs_1_, bf16[3584,128]{1,0:T(8,128)(2,1)S(1)} %multiply_convert_fusion.query_ref), custom_call_target="tpu_custom_call" | custom-call | flops 469762048 | bytes 3670016 | tf_op jit(solution)/shard_map/pallas_call | solution.py:82
  35.0 4.1 %shard_map.112.refs_8_ = bf16[1024,128]{1,0:T(8,128)(2,1)S(1)} custom-call(bf16[8,64,3584]{2,1,0:T(8,128)(2,1)S(1)} %copy-done.1, bf16[8,64,3584]{2,1,0:T(8,128)(2,1)} %collective-permute-done.tokens_ref.far_ref.refs_1_, f32[512,128]{1,0:T(8,128)S(1)} %get-tuple-element.11.near_scale_ref.refs_2_, f32[512,128]{1,0:T(8,128)S(1)} %get-tuple-element.12.far_scale_ref.refs_3_, ...), custom_call_target="tpu_custom_call" | custom-call | flops 939524096 | bytes 7340032 | tf_op jit(solution)/shard_map/pallas_call | solution.py:291
  39.1 1.3 %collective-permute-start.9 = (bf16[1024,128]{1,0:T(8,128)(2,1)S(1)}, bf16[1024,128]{1,0:T(8,128)(2,1)S(1)}, u32[]{:S(2)}, u32[]{:S(2)}) collective-permute-start(bf16[1024,128]{1,0:T(8,128)(2,1)S(1)} %shard_map.112.refs_8_), channel_id=1, source_target_pairs={{0,2},{1,3},{2,0},{3,1},{4,6},{5,7},{6,4},{7,5},{8,10},{9,11},{10,... | collective-permute-start | bytes 786440 | tf_op jit(solution)/shard_map/ppermute | solution.py:22
  41.5 4.4 %collective-permute-done.9.refs_9_ = bf16[1024,128]{1,0:T(8,128)(2,1)S(1)} collective-permute-done((bf16[1024,128]{1,0:T(8,128)(2,1)S(1)}, bf16[1024,128]{1,0:T(8,128)(2,1)S(1)}, u32[]{:S(2)}, u32[]{:S(2)}) %collective-permute-start.9) | collective-permute-done | bytes 262176 | tf_op jit(solution)/shard_map/ppermute | solution.py:22
  45.9 3.2 %shard_map.111.refs_5_ = f32[1024,128]{1,0:T(8,128)S(1)} custom-call(bf16[8,64,3584]{2,1,0:T(8,128)(2,1)S(1)} %copy-done.1, bf16[8,64,3584]{2,1,0:T(8,128)(2,1)} %collective-permute-done.tokens_ref.far_ref.refs_1_, bf16[896,128]{1,0:T(8,128)(2,1)S(1)} %collective-permute-done.1.b_ref, bf16[896,128]{1,0:T(8,128)(2,1)S(1)} %collective-permute-done.2.c_ref), custom_call_target="tpu_custom_call" | custom-call | flops 469762048 | bytes 3670016 | tf_op jit(solution)/shard_map/pallas_call | solution.py:348
  49.0 1.3 %collective-permute-start.18 = (bf16[128,128]{1,0:T(8,128)(2,1)S(1)}, bf16[128,128]{1,0:T(8,128)(2,1)S(1)}, u32[]{:S(2)}, u32[]{:S(2)}) collective-permute-start(bf16[128,128]{1,0:T(8,128)(2,1)S(1)} %collective-permute-done.16.refs_13_), channel_id=1, source_target_pairs={{0,2},{1,3},{2,0},{3,1},{4,6},{5,7},{6,4},{7,5},{8,10},{9,11},{10,... | collective-permute-start | bytes 98312 | tf_op jit(solution)/shard_map/ppermute | solution.py:22
  50.4 2.6 %collective-permute-done.18.refs_15_ = bf16[128,128]{1,0:T(8,128)(2,1)S(1)} collective-permute-done((bf16[128,128]{1,0:T(8,128)(2,1)S(1)}, bf16[128,128]{1,0:T(8,128)(2,1)S(1)}, u32[]{:S(2)}, u32[]{:S(2)}) %collective-permute-start.18) | collective-permute-done | bytes 32800 | tf_op jit(solution)/shard_map/ppermute | solution.py:22
  53.1 5.6 %shard_map.114 = f32[8,256]{1,0:T(8,128)S(1)} custom-call(bf16[8,64,3584]{2,1,0:T(8,128)(2,1)} %refs_0_.1, bf16[8,64,3584]{2,1,0:T(8,128)(2,1)} %collective-permute-done.tokens_ref.far_ref.refs_1_, f32[512,128]{1,0:T(8,128)S(1)} %get-tuple-element.11.near_scale_ref.refs_2_, f32[512,128]{1,0:T(8,128)S(1)} %get-tuple-element.12.far_scale_ref.refs_3_, ...), custom_call_target="tpu_custom_call" | custom-call | tf_op jit(solution)/shard_map/pallas_call | solution.py:360
  61.4 2.2 %collective-permute-done.21 = f32[8,256]{1,0:T(8,128)S(1)} collective-permute-done((f32[8,256]{1,0:T(8,128)S(1)}, f32[8,256]{1,0:T(8,128)S(1)}, u32[]{:S(2)}, u32[]{:S(2)}) %collective-permute-start.21) | collective-permute-done | bytes 8224 | tf_op jit(solution)/shard_map/ppermute | solution.py:22
  63.6 1.5 %collective-permute-start.22 = (f32[8,256]{1,0:T(8,128)S(1)}, f32[8,256]{1,0:T(8,128)S(1)}, u32[]{:S(2)}, u32[]{:S(2)}) collective-permute-start(f32[8,256]{1,0:T(8,128)S(1)} %add.336), channel_id=1, source_target_pairs={{0,4},{4,0},{8,12},{12,8},{16,20},{20,16},{24,28},{28,24},{1,5},{5... | collective-permute-start | bytes 24584 | tf_op jit(solution)/shard_map/ppermute | solution.py:22
  65.1 2.2 %collective-permute-done.22 = f32[8,256]{1,0:T(8,128)S(1)} collective-permute-done((f32[8,256]{1,0:T(8,128)S(1)}, f32[8,256]{1,0:T(8,128)S(1)}, u32[]{:S(2)}, u32[]{:S(2)}) %collective-permute-start.22) | collective-permute-done | bytes 8224 | tf_op jit(solution)/shard_map/ppermute | solution.py:22
  67.9 3.0 %collective-permute-done.23 = f32[16,256]{1,0:T(8,128)S(1)} collective-permute-done((f32[16,256]{1,0:T(8,128)S(1)}, f32[16,256]{1,0:T(8,128)S(1)}, u32[]{:S(2)}, u32[]{:S(2)}) %collective-permute-start.23) | collective-permute-done | bytes 16416 | tf_op jit(solution)/shard_map/ppermute | solution.py:22
  71.0 2.6 %collective-permute-start.24 = (f32[32,256]{1,0:T(8,128)S(1)}, f32[32,256]{1,0:T(8,128)S(1)}, u32[]{:S(2)}, u32[]{:S(2)}) collective-permute-start(f32[32,256]{1,0:T(8,128)S(1)} %pad_maximum_fusion.4), channel_id=1, source_target_pairs={{0,16},{4,20},{8,24},{12,28},{16,0},{20,4},{24,8},{28,12},{1,17},{... | collective-permute-start | bytes 98312 | tf_op jit(solution)/shard_map/ppermute | solution.py:22
  76.8 2.4 %shard_map.115 = bf16[4,4,64]{2,1,0:T(4,128)(2,1)} custom-call(f32[64,256]{1,0:T(8,128)} %pad_maximum_fusion.2.rows_ref, f32[16,64]{1,0:T(8,128)} %fusion.1.sel_ref, f32[16,16]{1,0:T(8,128)} %fusion.8.allow_ref, f32[16,1]{1,0:T(8,128)} %copy.15.fill_ref, f32[1,256]{1,0:T(1,128)} %bitcast.40, bf16[3,64,256]{2,1,0:T(8,128)(2,1)} %bitcast.39), custom_call_target="tpu_custom_call" | custom-call | tf_op jit(solution)/shard_map/pallas_call | solution.py:411
  (93 shorter events, 20.2 us)
Async XLA Ops:
  1.3 11.6 %collective-permute-start.12 = (bf16[64,896]{1,0:T(8,128)(2,1)S(1)}, bf16[64,896]{1,0:T(8,128)(2,1)S(1)}, u32[]{:S(2)}, u32[]{:S(2)}) collective-permute-start(bf16[64,896]{1,0:T(8,128)(2,1)S(1)} %bitcast.34), channel_id=1, source_target_pairs={{0,2},{1,3},{2,0},{3,1},{4,6},{5,7},{6,4},{7,5},{8,10},{9,11},{10,... | collective-permute-start | bytes 344072 | tf_op jit(solution)/shard_map/ppermute | solution.py:22
  4.3 9.0 %collective-permute-start.13 = (bf16[64,896]{1,0:T(8,128)(2,1)S(1)}, bf16[64,896]{1,0:T(8,128)(2,1)S(1)}, u32[]{:S(2)}, u32[]{:S(2)}) collective-permute-start(bf16[64,896]{1,0:T(8,128)(2,1)S(1)} %bitcast.35), channel_id=1, source_target_pairs={{0,1},{1,0},{2,3},{3,2},{4,5},{5,4},{6,7},{7,6},{8,9},{9,8},{10,11... | collective-permute-start | bytes 344072 | tf_op jit(solution)/shard_map/ppermute | solution.py:22
  6.2 12.6 %collective-permute-start.7 = (bf16[16,3584]{1,0:T(8,128)(2,1)}, bf16[16,3584]{1,0:T(8,128)(2,1)S(1)}, u32[]{:S(2)}, u32[]{:S(2)}) collective-permute-start(bf16[16,3584]{1,0:T(8,128)(2,1)} %dynamic-slice_bitcast_fusion.4), channel_id=1, source_target_pairs={{0,2},{1,3},{2,0},{3,1},{4,6},{5,7},{6,4},{7,5},{8,10},{9,11},{10,... | collective-permute-start | bytes 344072 | tf_op jit(solution)/shard_map/ppermute | solution.py:22
  6.3 22.2 %collective-permute-start = (bf16[8,64,3584]{2,1,0:T(8,128)(2,1)}, bf16[8,64,3584]{2,1,0:T(8,128)(2,1)}, u32[]{:S(2)}, u32[]{:S(2)}) collective-permute-start(bf16[8,64,3584]{2,1,0:T(8,128)(2,1)} %refs_0_.1), channel_id=1, source_target_pairs={{0,1},{1,0},{2,3},{3,2},{4,5},{5,4},{6,7},{7,6},{8,9},{9,8},{10,11... | collective-permute-start | bytes 11010056 | tf_op jit(solution)/shard_map/ppermute | solution.py:22
  8.1 17.9 %collective-permute-start.1 = (bf16[896,128]{1,0:T(8,128)(2,1)}, bf16[896,128]{1,0:T(8,128)(2,1)S(1)}, u32[]{:S(2)}, u32[]{:S(2)}) collective-permute-start(bf16[896,128]{1,0:T(8,128)(2,1)} %get-tuple-element.25), channel_id=1, source_target_pairs={{0,2},{1,3},{2,0},{3,1},{4,6},{5,7},{6,4},{7,5},{8,10},{9,11},{10,... | collective-permute-start | bytes 688136 | tf_op jit(solution)/shard_map/ppermute | solution.py:22
  12.9 14.4 %collective-permute-start.2 = (bf16[896,128]{1,0:T(8,128)(2,1)}, bf16[896,128]{1,0:T(8,128)(2,1)S(1)}, u32[]{:S(2)}, u32[]{:S(2)}) collective-permute-start(bf16[896,128]{1,0:T(8,128)(2,1)} %get-tuple-element.24), channel_id=1, source_target_pairs={{0,2},{1,3},{2,0},{3,1},{4,6},{5,7},{6,4},{7,5},{8,10},{9,11},{10,... | collective-permute-start | bytes 688136 | tf_op jit(solution)/shard_map/ppermute | solution.py:22
  13.3 1.5 %collective-permute-start.14 = (bf16[64,896]{1,0:T(8,128)(2,1)S(1)}, bf16[64,896]{1,0:T(8,128)(2,1)}, u32[]{:S(2)}, u32[]{:S(2)}) collective-permute-start(bf16[64,896]{1,0:T(8,128)(2,1)S(1)} %collective-permute-done.12.refs_1_), channel_id=1, source_target_pairs={{0,1},{1,0},{2,3},{3,2},{4,5},{5,4},{6,7},{7,6},{8,9},{9,8},{10,11... | collective-permute-start | bytes 344072 | tf_op jit(solution)/shard_map/ppermute | solution.py:22
  14.7 9.6 %collective-permute-start.5 = (bf16[16,3584]{1,0:T(8,128)(2,1)}, bf16[16,3584]{1,0:T(8,128)(2,1)S(1)}, u32[]{:S(2)}, u32[]{:S(2)}) collective-permute-start(bf16[16,3584]{1,0:T(8,128)(2,1)} %dynamic-slice_bitcast_fusion.5), channel_id=1, source_target_pairs={{0,2},{1,3},{2,0},{3,1},{4,6},{5,7},{6,4},{7,5},{8,10},{9,11},{10,... | collective-permute-start | bytes 344072 | tf_op jit(solution)/shard_map/ppermute | solution.py:22
  18.8 9.3 %collective-permute-start.15 = (bf16[64,128]{1,0:T(8,128)(2,1)S(1)}, bf16[64,128]{1,0:T(8,128)(2,1)S(1)}, u32[]{:S(2)}, u32[]{:S(2)}) collective-permute-start(bf16[64,128]{1,0:T(8,128)(2,1)S(1)} %shard_map.113), channel_id=1, source_target_pairs={{0,4},{4,0},{8,12},{12,8},{16,20},{20,16},{24,28},{28,24},{1,5},{5... | collective-permute-start | bytes 49160 | tf_op jit(solution)/shard_map/ppermute | solution.py:22
  24.4 9.8 %collective-permute-start.8 = (bf16[16,3584]{1,0:T(8,128)(2,1)S(1)}, bf16[16,3584]{1,0:T(8,128)(2,1)S(1)}, u32[]{:S(2)}, u32[]{:S(2)}) collective-permute-start(bf16[16,3584]{1,0:T(8,128)(2,1)S(1)} %collective-permute-done.7.refs_3_), channel_id=1, source_target_pairs={{0,8},{4,12},{8,0},{12,4},{16,24},{20,28},{24,16},{28,20},{1,9},{5... | collective-permute-start | bytes 344072 | tf_op jit(solution)/shard_map/ppermute | solution.py:22
  26.0 9.0 %collective-permute-start.6 = (bf16[16,3584]{1,0:T(8,128)(2,1)S(1)}, bf16[16,3584]{1,0:T(8,128)(2,1)S(1)}, u32[]{:S(2)}, u32[]{:S(2)}) collective-permute-start(bf16[16,3584]{1,0:T(8,128)(2,1)S(1)} %collective-permute-done.5.refs_1_), channel_id=1, source_target_pairs={{0,4},{4,0},{8,12},{12,8},{16,20},{20,16},{24,28},{28,24},{1,5},{5... | collective-permute-start | bytes 344072 | tf_op jit(solution)/shard_map/ppermute | solution.py:22
  27.3 25.7 %collective-permute-start.3 = (bf16[896,128]{1,0:T(8,128)(2,1)S(1)}, bf16[896,128]{1,0:T(8,128)(2,1)S(1)}, u32[]{:S(2)}, u32[]{:S(2)}) collective-permute-start(bf16[896,128]{1,0:T(8,128)(2,1)S(1)} %collective-permute-done.1.b_ref), channel_id=1, source_target_pairs={{0,4},{4,0},{8,12},{12,8},{16,20},{20,16},{24,28},{28,24},{1,5},{5... | collective-permute-start | bytes 688136 | tf_op jit(solution)/shard_map/ppermute | solution.py:22
  28.1 25.0 %collective-permute-start.4 = (bf16[896,128]{1,0:T(8,128)(2,1)S(1)}, bf16[896,128]{1,0:T(8,128)(2,1)S(1)}, u32[]{:S(2)}, u32[]{:S(2)}) collective-permute-start(bf16[896,128]{1,0:T(8,128)(2,1)S(1)} %collective-permute-done.2.c_ref), channel_id=1, source_target_pairs={{0,8},{4,12},{8,0},{12,4},{16,24},{20,28},{24,16},{28,20},{1,9},{5... | collective-permute-start | bytes 688136 | tf_op jit(solution)/shard_map/ppermute | solution.py:22
  28.5 12.0 %collective-permute-start.16 = (bf16[128,128]{1,0:T(8,128)(2,1)S(1)}, bf16[128,128]{1,0:T(8,128)(2,1)S(1)}, u32[]{:S(2)}, u32[]{:S(2)}) collective-permute-start(bf16[128,128]{1,0:T(8,128)(2,1)S(1)} %pad_maximum_fusion.3.refs_12_), channel_id=1, source_target_pairs={{0,8},{4,12},{8,0},{12,4},{16,24},{20,28},{24,16},{28,20},{1,9},{5... | collective-permute-start | bytes 98312 | tf_op jit(solution)/shard_map/ppermute | solution.py:22
  34.2 6.4 %collective-permute-start.17 = (bf16[128,128]{1,0:T(8,128)(2,1)S(1)}, bf16[128,128]{1,0:T(8,128)(2,1)S(1)}, u32[]{:S(2)}, u32[]{:S(2)}) collective-permute-start(bf16[128,128]{1,0:T(8,128)(2,1)S(1)} %pad_maximum_fusion.3.refs_12_), channel_id=1, source_target_pairs={{0,2},{1,3},{2,0},{3,1},{4,6},{5,7},{6,4},{7,5},{8,10},{9,11},{10,... | collective-permute-start | bytes 98312 | tf_op jit(solution)/shard_map/ppermute | solution.py:22
  39.1 6.7 %collective-permute-start.9 = (bf16[1024,128]{1,0:T(8,128)(2,1)S(1)}, bf16[1024,128]{1,0:T(8,128)(2,1)S(1)}, u32[]{:S(2)}, u32[]{:S(2)}) collective-permute-start(bf16[1024,128]{1,0:T(8,128)(2,1)S(1)} %shard_map.112.refs_8_), channel_id=1, source_target_pairs={{0,2},{1,3},{2,0},{3,1},{4,6},{5,7},{6,4},{7,5},{8,10},{9,11},{10,... | collective-permute-start | bytes 786440 | tf_op jit(solution)/shard_map/ppermute | solution.py:22
  40.6 12.5 %collective-permute-start.10 = (bf16[1024,128]{1,0:T(8,128)(2,1)S(1)}, bf16[1024,128]{1,0:T(8,128)(2,1)S(1)}, u32[]{:S(2)}, u32[]{:S(2)}) collective-permute-start(bf16[1024,128]{1,0:T(8,128)(2,1)S(1)} %shard_map.112.refs_8_), channel_id=1, source_target_pairs={{0,1},{1,0},{2,3},{3,2},{4,5},{5,4},{6,7},{7,6},{8,9},{9,8},{10,11... | collective-permute-start | bytes 786440 | tf_op jit(solution)/shard_map/ppermute | solution.py:22
  40.6 8.4 %collective-permute-start.19 = (f32[8,896]{1,0:T(8,128)S(1)}, f32[8,896]{1,0:T(8,128)S(1)}, u32[]{:S(2)}, u32[]{:S(2)}) collective-permute-start(f32[8,896]{1,0:T(8,128)S(1)} %dynamic-slice_bitcast_fusion.6), channel_id=1, source_target_pairs={{0,2},{1,3},{2,0},{3,1},{4,6},{5,7},{6,4},{7,5},{8,10},{9,11},{10,... | collective-permute-start | bytes 86024 | tf_op jit(solution)/shard_map/ppermute | solution.py:22
  45.9 7.2 %collective-permute-start.11 = (bf16[1024,128]{1,0:T(8,128)(2,1)S(1)}, bf16[1024,128]{1,0:T(8,128)(2,1)S(1)}, u32[]{:S(2)}, u32[]{:S(2)}) collective-permute-start(bf16[1024,128]{1,0:T(8,128)(2,1)S(1)} %collective-permute-done.9.refs_9_), channel_id=1, source_target_pairs={{0,1},{1,0},{2,3},{3,2},{4,5},{5,4},{6,7},{7,6},{8,9},{9,8},{10,11... | collective-permute-start | bytes 786440 | tf_op jit(solution)/shard_map/ppermute | solution.py:22
  49.0 4.0 %collective-permute-start.18 = (bf16[128,128]{1,0:T(8,128)(2,1)S(1)}, bf16[128,128]{1,0:T(8,128)(2,1)S(1)}, u32[]{:S(2)}, u32[]{:S(2)}) collective-permute-start(bf16[128,128]{1,0:T(8,128)(2,1)S(1)} %collective-permute-done.16.refs_13_), channel_id=1, source_target_pairs={{0,2},{1,3},{2,0},{3,1},{4,6},{5,7},{6,4},{7,5},{8,10},{9,11},{10,... | collective-permute-start | bytes 98312 | tf_op jit(solution)/shard_map/ppermute | solution.py:22
  59.9 3.7 %collective-permute-start.21 = (f32[8,256]{1,0:T(8,128)S(1)}, f32[8,256]{1,0:T(8,128)S(1)}, u32[]{:S(2)}, u32[]{:S(2)}) collective-permute-start(f32[8,256]{1,0:T(8,128)S(1)} %add.335), channel_id=1, source_target_pairs={{0,2},{1,3},{2,0},{3,1},{4,6},{5,7},{6,4},{7,5},{8,10},{9,11},{10,... | collective-permute-start | bytes 24584 | tf_op jit(solution)/shard_map/ppermute | solution.py:22
  63.6 3.7 %collective-permute-start.22 = (f32[8,256]{1,0:T(8,128)S(1)}, f32[8,256]{1,0:T(8,128)S(1)}, u32[]{:S(2)}, u32[]{:S(2)}) collective-permute-start(f32[8,256]{1,0:T(8,128)S(1)} %add.336), channel_id=1, source_target_pairs={{0,4},{4,0},{8,12},{12,8},{16,20},{20,16},{24,28},{28,24},{1,5},{5... | collective-permute-start | bytes 24584 | tf_op jit(solution)/shard_map/ppermute | solution.py:22
  67.2 3.7 %collective-permute-start.23 = (f32[16,256]{1,0:T(8,128)S(1)}, f32[16,256]{1,0:T(8,128)S(1)}, u32[]{:S(2)}, u32[]{:S(2)}) collective-permute-start(f32[16,256]{1,0:T(8,128)S(1)} %pad_maximum_fusion.5), channel_id=1, source_target_pairs={{0,8},{4,12},{8,0},{12,4},{16,24},{20,28},{24,16},{28,20},{1,9},{5... | collective-permute-start | bytes 49160 | tf_op jit(solution)/shard_map/ppermute | solution.py:22
  71.0 5.2 %collective-permute-start.24 = (f32[32,256]{1,0:T(8,128)S(1)}, f32[32,256]{1,0:T(8,128)S(1)}, u32[]{:S(2)}, u32[]{:S(2)}) collective-permute-start(f32[32,256]{1,0:T(8,128)S(1)} %pad_maximum_fusion.4), channel_id=1, source_target_pairs={{0,16},{4,20},{8,24},{12,28},{16,0},{20,4},{24,8},{28,12},{1,17},{... | collective-permute-start | bytes 98312 | tf_op jit(solution)/shard_map/ppermute | solution.py:22
  (12 other events, 56.4 us)

commit v4 on v3

v4 whole, which is shorter than its diff:
```python
import functools
import math

import jax
import jax.numpy as jnp
from jax import lax
from jax.experimental import pallas as pl
from jax.experimental.pallas import tpu as pltpu
from jax.sharding import PartitionSpec as P

CAP = 8
DOC_MOST = 4
OWN_DOCS = 4
F32 = jnp.float32
BF16 = jnp.bfloat16
NT = (((1,), (1,)), ((), ()))


def flipped(block, axis, mask):
    count = lax.axis_size(axis)
    return lax.ppermute(block, axis, [(i, i ^ mask) for i in range(count)])


def after(value, earlier):
    return lax.optimization_barrier((value, earlier))[0]


def cut(array, at, size, axis):
    return lax.dynamic_slice_in_dim(array, at * size, size, axis=axis)


def slot_table(seg_replica):
    replica_of = seg_replica[:, 0]
    order = jnp.arange(replica_of.shape[0], dtype=jnp.int32)
    earlier = (replica_of[None, :] == replica_of[:, None]) & (order[None, :] < order[:, None])
    return replica_of, jnp.sum(earlier.astype(jnp.int32), axis=1)


def owner_rows(doc_of_segment, doc_owner):
    owner_of = doc_owner[:, 0]
    doc_ids = jnp.arange(owner_of.shape[0], dtype=jnp.int32)
    earlier = (owner_of[None, :] == owner_of[:, None]) & (doc_ids[None, :] < doc_ids[:, None])
    doc_rank = jnp.sum(earlier.astype(jnp.int32), axis=1)
    start_of = jnp.sum((doc_of_segment[None, :] < doc_ids[:, None]).astype(jnp.int32), axis=1)
    matches = doc_of_segment[:, None] == doc_ids[None, :]
    seg_owner = jnp.sum(jnp.where(matches, owner_of[None, :], 0), axis=1)
    seg_rank = jnp.sum(jnp.where(matches, doc_rank[None, :], 0), axis=1)
    seg_start = jnp.sum(jnp.where(matches, start_of[None, :], 0), axis=1)
    position = jnp.arange(doc_of_segment.shape[0], dtype=jnp.int32) - seg_start
    return seg_owner * (OWN_DOCS * DOC_MOST) + seg_rank * DOC_MOST + position


def room(*arrays):
    total = sum(math.prod(a.shape) * jnp.dtype(a.dtype).itemsize for a in arrays)
    return pltpu.CompilerParams(vmem_limit_bytes=total * 5 // 4 + 6 * 2**20)


def lane_step(width):
    step = 512
    while width % step:
        step //= 2
    return step


def parities():
    rep = lax.axis_index("rep")
    return lax.rem(rep, 2), lax.rem(rep // 2, 2)


def token_kernel(order_ref, x_ref, gain_ref, own_ref, scale_ref, sum_ref):
    slots, count, width = x_ref.shape
    step = lane_step(width)
    for s in range(slots):
        squares = jnp.zeros((count, 128), F32)
        for at in range(0, width, step):
            x = x_ref[s, :, at:at + step].astype(F32)
            sum_ref[s:s + 1, at:at + step] = jnp.sum(x, axis=0, keepdims=True)
            x = x * x
            for i in range(0, step, 128):
                squares += x[:, i:i + 128]
        mean = jnp.sum(squares, axis=1, keepdims=True) * (1.0 / width)
        scale_ref[s * count:(s + 1) * count, :] = jnp.broadcast_to(
            lax.rsqrt(mean + 1e-06), (count, scale_ref.shape[1])
        )


def keyvalue_kernel(length, near_ref, far_ref, gain_ref, own_ref, near_scale_ref, near_sum_ref, *refs):
    half_refs, (kv_ref, near_out, far_out, scale_ref, mean_ref) = refs[:-5], refs[-5:]
    slots, count, width = near_ref.shape
    rows = slots * count
    step = lane_step(width)
    parts = [own_ref[0], own_ref[1]]
    for here, there in zip(half_refs[::2], half_refs[1::2]):
        parts += [here[0], there[0], here[1], there[1]]
    weights = jnp.concatenate(parts, axis=0)
    scale_ref[:rows, :] = near_scale_ref[...]
    for c, (x_ref, out_ref) in enumerate(((near_ref, near_out), (far_ref, far_out))):
        for s in range(slots):
            squares = jnp.zeros((count, 128), F32)
            for at in range(0, width, step):
                x = x_ref[s, :, at:at + step].astype(F32)
                out_ref[s, :, at:at + step] = (x * gain_ref[at:at + step].reshape(1, step)).astype(BF16)
                if c:
                    total = jnp.sum(x, axis=0, keepdims=True) + near_sum_ref[s:s + 1, at:at + step]
                    mean_ref[s:s + 1, at:at + step] = total * (1.0 / length)
                    x = x * x
                    for i in range(0, step, 128):
                        squares += x[:, i:i + 128]
            if c:
                mean = jnp.sum(squares, axis=1, keepdims=True) * (1.0 / width)
                at_row = c * rows + s * count
                scale_ref[at_row:at_row + count, :] = jnp.broadcast_to(
                    lax.rsqrt(mean + 1e-06), (count, scale_ref.shape[1])
                )
        kv = lax.dot_general(out_ref[...].reshape(rows, width), weights, NT, preferred_element_type=F32)
        span = slice(c * rows, (c + 1) * rows)
        kv_ref[span, :] = (kv * scale_ref[span, :1]).astype(BF16)


def half_query(x_ref, b_ref, c_ref, turn):
    slots, count, width = x_ref.shape
    part = b_ref.shape[0]
    x_bit, z_bit = parities()
    at_b = pl.multiple_of((x_bit ^ turn) * part, 128)
    at_c = pl.multiple_of((2 + (z_bit ^ turn)) * part, 128)
    rows = slots * count
    total = jnp.dot(
        x_ref[:, :, pl.ds(at_b, part)].reshape(rows, part), b_ref[...], preferred_element_type=F32
    )
    return total + jnp.dot(
        x_ref[:, :, pl.ds(at_c, part)].reshape(rows, part), c_ref[...], preferred_element_type=F32
    )


def query_kernel(near_ref, far_ref, scale_ref, query_ref, *refs):
    part_refs, (own_ref, *half_refs) = refs[:len(refs) // 3 * 2], refs[len(refs) // 3 * 2:]
    slots, count, width = near_ref.shape
    rows = slots * count
    for c, x_ref in enumerate((near_ref, far_ref)):
        span = slice(c * rows, (c + 1) * rows)
        for p, half_ref in enumerate(half_refs):
            half_ref[span, :] = half_query(x_ref, part_refs[2 * p], part_refs[2 * p + 1], 0)
        q = jnp.dot(x_ref[...].reshape(rows, width), query_ref[...], preferred_element_type=F32)
        own_ref[span, :] = (q * scale_ref[span, :]).astype(BF16)


def product_kernel(masks, order_ref, output_ref, *refs):
    proj_refs, out_ref = refs[:-1], refs[-1]
    total = jnp.zeros(out_ref.shape, F32)
    for mask, proj_ref in zip(masks, proj_refs):
        total += jnp.dot(output_ref[mask], proj_ref[...], preferred_element_type=F32)
    out_ref[...] = total.astype(BF16)


def split(value):
    high = value.astype(BF16)
    return jnp.concatenate([high, (value - high.astype(F32)).astype(BF16)], axis=0)


def joined(value):
    half = value.shape[0] // 2
    return value[:half] + value[half:]


def attention_kernel(masks, group, length, *refs):
    n = len(masks)
    at = iter(range(len(refs)))

    def take(count):
        return [refs[next(at)] for _ in range(count)]

    x_refs = take(2)
    scale_ref, query_ref = take(2)
    early_refs, b_refs, c_refs = take(n - 1), take(n - 1), take(n - 1)
    near_refs, far_refs = take(n), take(n)
    w2_refs = [take(2) for _ in range(n)]
    mean_refs = take(n)
    place_ref, proj_ref, out_ref, q_ref, kv_ref, score_ref, weight_ref, ctx_ref, w2_ref = take(9)
    slots, tokens, _ = x_refs[0].shape
    head_dim = query_ref.shape[1]
    rows = slots * tokens
    groups = sorted({m // group for m in masks})
    heads_of = [[p for p in range(n) if masks[p] // group == g] for g in groups]
    in_group = len(heads_of[0])

    x_bit, _ = parities()
    part = w2_ref.shape[2] // 2
    for p in range(n):
        for i in range(2):
            at_lane = pl.multiple_of((x_bit ^ i) * part, 128)
            w2_ref[p, :, pl.ds(at_lane, part)] = w2_refs[p][i][...]

    for p in range(n):
        for c in range(2):
            mixed = jnp.concatenate(
                [
                    near_refs[p][c * rows:(c + 1) * rows, :],
                    far_refs[p][(1 - c) * rows:(2 - c) * rows, :],
                ],
                axis=1,
            )
            kv_ref[p, c * rows:(c + 1) * rows, :] = jnp.dot(
                mixed, place_ref[p], preferred_element_type=F32
            ).astype(BF16)
    q_ref[0] = query_ref[...]
    for p in range(1, n):
        for c in range(2):
            span = slice(c * rows, (c + 1) * rows)
            q = early_refs[p - 1][span, :] + half_query(x_refs[c], b_refs[p - 1], c_refs[p - 1], 1)
            q_ref[p, span, :] = (q * scale_ref[span, :]).astype(BF16)

    def spans(s):
        return [slice(c * rows + s * tokens, c * rows + (s + 1) * tokens) for c in range(2)]

    def columns(s, first):
        return jnp.concatenate(
            [kv_ref[p, span, first:first + head_dim] for p in range(n) for span in spans(s)], axis=0
        )

    for s in range(slots):
        for g, heads in enumerate(heads_of):
            q = jnp.concatenate([q_ref[p, span, :] for p in heads for span in spans(s)], axis=0)
            keys = columns(s, g * 2 * head_dim)
            score_ref[s, g] = lax.dot_general(q, keys, NT, preferred_element_type=F32)
    for s in range(slots):
        for g in range(len(groups)):
            scores = score_ref[s, g]
            top = jnp.max(scores, axis=1, keepdims=True)
            e = jnp.exp((scores - top) * head_dim ** (-0.5))
            probs = e * (1.0 / jnp.sum(e, axis=1, keepdims=True))
            weight_ref[s, g] = jnp.sum(probs.reshape(in_group, 2 * tokens, -1), axis=1)
    for s in range(slots):
        for g, heads in enumerate(heads_of):
            values = columns(s, (g * 2 + 1) * head_dim)
            context = joined(
                jnp.dot(split(weight_ref[s, g]), values, preferred_element_type=F32)
            ) * (1.0 / length)
            for j, p in enumerate(heads):
                ctx_ref[p, s:s + 1, :] = context[j:j + 1]
    mean = mean_refs[0][...]
    for p in range(1, n):
        mean += mean_refs[p][...]
    total = joined(jnp.dot(split(mean), proj_ref[...], preferred_element_type=F32))
    for p in range(n):
        total += joined(jnp.dot(split(ctx_ref[p]), w2_ref[p], preferred_element_type=F32))
    out_ref[...] = total


def document_kernel(near_ref, far_ref, select_ref, allow_ref, fill_ref, gain_ref, qkv_ref, out_ref):
    docs, most, head = out_ref.shape
    rows = jnp.concatenate([near_ref[...], far_ref[...]], axis=0)
    high = rows.astype(BF16)
    rest = rows - high.astype(F32)
    middle = rest.astype(BF16)
    low = (rest - middle.astype(F32)).astype(BF16)
    select = select_ref[...].astype(BF16)
    first = sum(jnp.dot(select, part, preferred_element_type=F32) for part in (high, middle, low))
    scale = lax.rsqrt(jnp.mean(first * first, axis=-1, keepdims=True) + 1e-06)
    normed = (first * scale * gain_ref[...]).astype(BF16)
    q, k, v = (
        lax.dot_general(normed, qkv_ref[i], NT, preferred_element_type=F32).astype(BF16) for i in range(3)
    )
    scores = lax.dot_general(q, k, NT, preferred_element_type=F32) * head ** (-0.5)
    scores = jnp.where(allow_ref[...] > 0.5, scores, -1e30)
    e = jnp.exp(scores - jnp.max(scores, axis=1, keepdims=True))
    probs = (e / jnp.sum(e, axis=1, keepdims=True)).astype(BF16)
    context = jnp.dot(probs, v, preferred_element_type=F32) * fill_ref[...]
    for d in range(docs):
        out_ref[d] = context[d * most:(d + 1) * most].astype(BF16)


def local(
    tokens,
    seg_replica,
    doc_of_segment,
    doc_owner,
    enc_gain,
    enc_query,
    enc_keyvalue,
    enc_output,
    doc_proj,
    doc_gain,
    doc_qkv,
):
    n_rep, n_tp = lax.axis_size("rep"), lax.axis_size("tp")
    rep_index = lax.axis_index("rep")
    tp_index = lax.axis_index("tp")
    x_bit, z_bit = rep_index % 2, rep_index // 2 % 2
    slots, own_tokens, width = tokens.shape
    length = own_tokens * n_tp
    head_dim = enc_query.shape[1]
    kv_width = enc_keyvalue.shape[2]
    group = head_dim // kv_width
    block, doc_width = doc_proj.shape
    masks = list(range(0, n_tp, 2))

    kv_rows = jnp.transpose(enc_keyvalue, (1, 2, 0))
    kv_half = cut(kv_rows, x_bit, kv_width // 2, 1)
    kv_y = [flipped(kv_half, "tp", m) for m in masks[1:]]
    tokens_far = flipped(tokens, "tp", 1)
    part_q, part_doc = width // 4, doc_width // 2
    query_here = after(enc_query, kv_half)
    b_part, c_part = cut(query_here, x_bit, part_q, 0), cut(query_here, 2 + z_bit, part_q, 0)
    b_y = [flipped(b_part, "tp", m) for m in masks[1:]]
    c_y = [flipped(c_part, "tp", m) for m in masks[1:]]
    proj = cut(after(doc_proj, (b_part, c_part)), x_bit, part_doc, 1)
    proj_near = [proj] + [flipped(proj, "tp", m) for m in masks[1:]]

    weights = []
    for w in kv_y:
        weights += [w, flipped(w, "rep", 1)]

    rows = slots * own_tokens
    lanes = 2 * kv_width * len(masks)
    out = [
        jax.ShapeDtypeStruct((rows, head_dim), F32),
        jax.ShapeDtypeStruct((slots, width), F32),
    ]
    scale, sums = pl.pallas_call(
        token_kernel,
        in_specs=[pl.BlockSpec(memory_space=pl.ANY)] + [pl.BlockSpec(memory_space=pltpu.VMEM)] * 3,
        out_shape=out,
        compiler_params=room(tokens, enc_gain, kv_rows, *out),
    )(kv_y[0], tokens, enc_gain, kv_rows)
    operands = (tokens, tokens_far, enc_gain, kv_rows, scale, sums, *weights)
    out = [
        jax.ShapeDtypeStruct((2 * rows, lanes), BF16),
        jax.ShapeDtypeStruct(tokens.shape, BF16),
        jax.ShapeDtypeStruct(tokens.shape, BF16),
        jax.ShapeDtypeStruct((2 * rows, head_dim), F32),
        jax.ShapeDtypeStruct((slots, width), F32),
    ]
    kv, near, far, scale, mean = pl.pallas_call(
        functools.partial(keyvalue_kernel, length),
        out_shape=out,
        compiler_params=room(*operands, *out),
    )(*operands)
    kv_near = [kv] + [flipped(kv, "tp", m) for m in masks[1:]]
    kv_far = [flipped(k, "tp", 1) for k in kv_near]

    proj_near = [after(p, kv) for p in proj_near]
    proj_all = proj_near + [flipped(p, "tp", 1) for p in proj_near]
    origin = masks + [m + 1 for m in masks]
    output_blocks = jnp.stack([cut(after(enc_output, kv), tp_index ^ m, block, 1) for m in range(n_tp)], axis=0)
    out = jax.ShapeDtypeStruct((head_dim, part_doc), BF16)
    w2 = pl.pallas_call(
        functools.partial(product_kernel, origin),
        in_specs=[pl.BlockSpec(memory_space=pl.ANY)]
        + [pl.BlockSpec(memory_space=pltpu.VMEM)] * (1 + n_tp),
        out_shape=out,
        compiler_params=room(output_blocks, *proj_all, out),
    )(kv, output_blocks, *proj_all)
    w2_pair = [w2, flipped(w2, "rep", 1)]
    count = 2 * lanes
    column = jnp.arange(count, dtype=jnp.int32)
    core = column // lanes
    mask_of = column % lanes // (2 * kv_width) * 2
    inner = column % (2 * kv_width)
    part_kv = kv_width // 2
    quarter = inner // part_kv
    swapped = quarter // 2 * 2 + (quarter % 2 ^ x_bit)
    inner = jnp.where(mask_of == 0, inner, swapped * part_kv + inner % part_kv)
    places = []
    for m in masks:
        target = (
            (mask_of ^ m) // group * (2 * head_dim)
            + inner // kv_width * head_dim
            + (tp_index ^ m ^ mask_of ^ core) % group * kv_width
            + inner % kv_width
        )
        places.append((target[:, None] == column[None, :]).astype(BF16))
    place = jnp.stack(places, axis=0)

    parts, b_rest, c_rest = [], [], []
    for q_b, q_c in zip(b_y, c_y):
        q_b, q_c = after((q_b, q_c), kv)
        parts += [q_b, q_c]
        b_rest.append(flipped(q_b, "rep", 1))
        c_rest.append(flipped(q_c, "rep", 2))
    operands = (near, far, scale, enc_query, *parts)
    out = [jax.ShapeDtypeStruct((2 * rows, head_dim), BF16)]
    out += [jax.ShapeDtypeStruct((2 * rows, head_dim), F32) for _ in masks[1:]]
    own, *early = pl.pallas_call(
        query_kernel, out_shape=out, compiler_params=room(*operands, *out)
    )(*operands)

    mean, *w2_pair = after((mean, *w2_pair), own)
    mean = mean.reshape(slots, n_tp, block)

    def mean_of(m):
        return lax.dynamic_index_in_dim(mean, tp_index ^ m, 1, keepdims=False)

    means = [mean_of(0)] + [flipped(mean_of(m), "tp", m) for m in masks[1:]]
    w2_all = w2_pair + [flipped(w, "tp", m) for m in masks[1:] for w in w2_pair]

    n = len(masks)
    groups = n_tp // group
    operands = (
        near,
        far,
        scale,
        own,
        *early,
        *b_rest,
        *c_rest,
        *kv_near,
        *kv_far,
        *w2_all,
        *means,
        place,
        doc_proj,
    )
    scratch = [
        pltpu.VMEM((n, 2 * rows, head_dim), BF16),
        pltpu.VMEM((n, 2 * rows, 2 * lanes), BF16),
        pltpu.VMEM((slots, groups, n // groups * 2 * own_tokens, length), F32),
        pltpu.VMEM((slots, groups, n // groups, length), F32),
        pltpu.VMEM((n, slots, head_dim), F32),
        pltpu.VMEM((n, head_dim, doc_width), BF16),
    ]
    part = pl.pallas_call(
        functools.partial(attention_kernel, masks, group, length),
        out_shape=jax.ShapeDtypeStruct((slots, doc_width), F32),
        scratch_shapes=scratch,
        compiler_params=room(*operands, *scratch),
    )(*operands)

    bit = 1
    while bit < n_tp:
        part = part + flipped(part, "tp", bit)
        bit *= 2
    bit = 1
    while bit < n_rep // 2:
        part = jnp.concatenate([part, flipped(part, "rep", bit)], axis=0)
        bit *= 2
    part_far = flipped(part, "rep", bit)

    seg_replica, doc_of_segment, doc_owner = after((seg_replica, doc_of_segment, doc_owner), kv)
    replica_of, rank = slot_table(seg_replica)
    row_of = owner_rows(doc_of_segment, doc_owner)
    owned = OWN_DOCS * DOC_MOST
    wanted = rep_index * owned + jnp.arange(owned, dtype=jnp.int32)
    matches = (row_of[None, :] == wanted[:, None]).astype(F32)
    at_slot = (replica_of ^ rep_index) * CAP + rank
    holds = (at_slot[:, None] == jnp.arange(n_rep * CAP, dtype=jnp.int32)[None, :]).astype(F32)
    select = jnp.dot(matches, holds)
    filled = jnp.sum(matches, axis=1)
    row = jnp.arange(owned, dtype=jnp.int32)
    same_doc = row[:, None] // DOC_MOST == row[None, :] // DOC_MOST
    allowed = same_doc & ((filled[None, :] > 0.5) | (row[:, None] == row[None, :]))

    operands = (
        part,
        part_far,
        select,
        allowed.astype(F32),
        filled[:, None],
        doc_gain[None, :],
        jnp.transpose(doc_qkv, (1, 2, 0)),
    )
    return pl.pallas_call(
        document_kernel,
        out_shape=jax.ShapeDtypeStruct((OWN_DOCS, DOC_MOST, doc_qkv.shape[2]), BF16),
        compiler_params=room(*operands),
    )(*operands)


def solution(mesh):
    in_specs = (
        P("rep", "tp", None),
        P(),
        P(),
        P(),
        P(),
        P(None, "tp"),
        P(None, None, "tp"),
        P("tp", None),
        P("tp", None),
        P(),
        P(None, None, "tp"),
    )
    out_specs = P("rep", None, "tp")
    return jax.shard_map(local, mesh=mesh, in_specs=in_specs, out_specs=out_specs, check_vma=False)
```

time: 79.5 us -> 61.8 us (0.78)
  Pallas kernels: 22.7 us -> 13.3 us
  waiting for transfers between devices: 16.9 us -> 13.7 us
  other arithmetic: 4.23 us -> 1.23 us
  local copies, waits for them, and re-layouts: 9.07 us -> 7.7 us
    pallas_call x5 -> x4, Pallas kernels: 14.7 us -> 9.49 us  [the longest x1 4.9 us: local(): pl.pallas_call(functools.partial(keyvalue_kernel, length), out_shape=out,...]
    ppermute x25 -> x22, waiting for transfers between devices: 16.9 us -> 13.7 us  [flipped(): return lax.ppermute(block, axis, [(i, i ^ mask) for i in range(count)])]
    pallas_call x1, Pallas kernels: 5.62 us -> 2.49 us  [local(): pl.pallas_call(functools.partial(attention_kernel, masks, group, length),...]
    convert_element_type x3 -> x0, other arithmetic: 1.73 us -> none  [the longest x2 1.19 us: local(): (jnp.transpose(enc_keyvalue, (1, 2, 0)).astype(F32) * enc_gain).astype(BF16)]
    another operation x1, local copies, waits for them, and re-layouts: 1.37 us -> 0.07 us  [local(): jnp.stack([cut(after(enc_output, kv), tp_index ^ m, block, 1) for m in ra...]
    pallas_call x1, Pallas kernels: 2.38 us -> 1.37 us  [local(): pl.pallas_call(document_kernel, out_shape=jax.ShapeDtypeStruct((OWN_DOCS,...]
    unnamed x23 -> x28, local copies, waits for them, and re-layouts: 3.72 us -> 4.55 us
    dynamic_slice x4 -> x3, local copies, waits for them, and re-layouts: 3.26 us -> 2.99 us  [cut(): return lax.dynamic_slice_in_dim(array, at * size, size, axis=axis)]
  transfers between devices with their start and end apart: 25 -> 22, of which waited for: 8 -> 11; matrix products, arithmetic and copies ran while one was open for 11% -> 7% of each run, Pallas kernels for 19% -> 15%
where the time goes in v4:
time: 61.8 us; the launch traced here: 61.5 us
  starting transfers between devices  25.1 us (41%)
  waiting for transfers between devices  13.7 us (22%)
  Pallas kernels  13.3 us (22%)
  local copies, waits for them, and re-layouts  7.7 us (12%)
  other arithmetic  1.23 us (2%)
    ppermute x22, starting transfers between devices, flipped(): return lax.ppermute(block, axis, [(i, i ^ mask) for i in range(count)])  25.1 us
    ppermute x22, waiting for transfers between devices, flipped(): return lax.ppermute(block, axis, [(i, i ^ mask) for i in range(count)])  13.7 us
    pallas_call x1, Pallas kernels, local(): pl.pallas_call(functools.partial(keyvalue_kernel, length), out_shape=out,...  4.9 us
    unnamed x28, local copies, waits for them, and re-layouts  4.55 us
    pallas_call x1, Pallas kernels, local(): pl.pallas_call(query_kernel, out_shape=out, compiler_params=room(*operand...  3.03 us
    dynamic_slice x3, local copies, waits for them, and re-layouts, cut(): return lax.dynamic_slice_in_dim(array, at * size, size, axis=axis)  2.99 us
    pallas_call x1, Pallas kernels, local(): pl.pallas_call(functools.partial(attention_kernel, masks, group, length),...  2.49 us
    pallas_call x1, Pallas kernels, local(): pl.pallas_call(document_kernel, out_shape=jax.ShapeDtypeStruct((OWN_DOCS,...  1.37 us
  transfers between devices with their start and end apart: 22, of which 11 were waited for; matrix products, arithmetic and copies ran while one was open for 7% of the time, Pallas kernels for 15%

profile of v4, /device:TPU:0, one launch (start us, length us, event | category | flops | bytes accessed | tf_op | source)
XLA Modules:
  0.0 61.5 jit_solution(11435801215725705545)
XLA Ops:
  1.4 2.7 %collective-permute-start.1 = (bf16[2,16,3584]{2,1,0:T(8,128)(2,1)S(1)}, bf16[2,16,3584]{2,1,0:T(8,128)(2,1)S(1)}, u32[]{:S(2)}, u32[]{:S(2)}) collective-permute-start(bf16[2,16,3584]{2,1,0:T(8,128)(2,1)S(1)} %dynamic-slice_bitcast_fusion.4), channel_id=1, source_target_pairs={{0,2},{1,3},{2,0},{3,1},{4,6},{5,7},{6,4},{7,5},{8,10},{9,11},{10,... | collective-permute-start | bytes 688136 | tf_op jit(solution)/shard_map/ppermute | solution.py:21
  5.3 2.0 %collective-permute-start.4 = (bf16[896,128]{1,0:T(8,128)(2,1)S(1)}, bf16[896,128]{1,0:T(8,128)(2,1)S(1)}, u32[]{:S(2)}, u32[]{:S(2)}) collective-permute-start(bf16[896,128]{1,0:T(8,128)(2,1)S(1)} %get-tuple-element.56), channel_id=1, source_target_pairs={{0,2},{1,3},{2,0},{3,1},{4,6},{5,7},{6,4},{7,5},{8,10},{9,11},{10,... | collective-permute-start | bytes 688136 | tf_op jit(solution)/shard_map/ppermute | solution.py:21
  8.6 2.0 %collective-permute-done.1.order_ref.refs_0_ = bf16[2,16,3584]{2,1,0:T(8,128)(2,1)S(1)} collective-permute-done((bf16[2,16,3584]{2,1,0:T(8,128)(2,1)S(1)}, bf16[2,16,3584]{2,1,0:T(8,128)(2,1)S(1)}, u32[]{:S(2)}, u32[]{:S(2)}) %collective-permute-start.1) | collective-permute-done | bytes 229408 | tf_op jit(solution)/shard_map/ppermute | solution.py:21
  10.5 1.9 %collective-permute-start.2 = (bf16[2,16,3584]{2,1,0:T(8,128)(2,1)S(1)}, bf16[2,16,3584]{2,1,0:T(8,128)(2,1)S(1)}, u32[]{:S(2)}, u32[]{:S(2)}) collective-permute-start(bf16[2,16,3584]{2,1,0:T(8,128)(2,1)S(1)} %collective-permute-done.1.order_ref.refs_0_), channel_id=1, source_target_pairs={{0,4},{4,0},{8,12},{12,8},{16,20},{20,16},{24,28},{28,24},{1,5},{5... | collective-permute-start | bytes 688136 | tf_op jit(solution)/shard_map/ppermute | solution.py:21
  12.6 2.0 %copy-done = bf16[8,64,3584]{2,1,0:T(8,128)(2,1)S(1)} copy-done((bf16[8,64,3584]{2,1,0:T(8,128)(2,1)S(1)}, bf16[8,64,3584]{2,1,0:T(8,128)(2,1)}, u32[]{:S(2)}) %copy-start) | copy-done | bytes 3670040
  16.3 1.2 %shard_map.109 = (f32[512,128]{1,0:T(8,128)S(1)}, f32[8,3584]{1,0:T(8,128)S(1)}) custom-call(bf16[2,16,3584]{2,1,0:T(8,128)(2,1)S(1)} %collective-permute-done.1.order_ref.refs_0_, bf16[8,64,3584]{2,1,0:T(8,128)(2,1)S(1)} %copy-done, f32[3584]{0:T(1024)S(1)} %copy-done.7, bf16[2,32,3584]{2,1,0:T(8,128)(2,1)S(1)} %bitcast.27), custom_call_target="tpu_custom_call" | custom-call | tf_op jit(solution)/shard_map/pallas_call | solution.py:319
  18.4 4.9 %shard_map.110 = (bf16[1024,128]{1,0:T(8,128)(2,1)S(1)}, bf16[8,64,3584]{2,1,0:T(8,128)(2,1)S(1)}, bf16[8,64,3584]{2,1,0:T(8,128)(2,1)S(1)}, f32[1024,128]{1,0:T(8,128)S(1)}, f32[8,3584]{1,0:T(8,128)S(1)}) custom-call(bf16[8,64,3584]{2,1,0:T(8,128)(2,1)S(1)} %copy-done.1, bf16[8,64,3584]{2,1,0:T(8,128)(2,1)} %collective-permute-done.far_ref, ...), custom_call_target="tpu_custom_call" | custom-call | tf_op jit(solution)/shard_map/pallas_call | solution.py:333
  23.3 1.6 %collective-permute-start.7 = (bf16[1024,128]{1,0:T(8,128)(2,1)S(1)}, bf16[1024,128]{1,0:T(8,128)(2,1)S(1)}, u32[]{:S(2)}, u32[]{:S(2)}) collective-permute-start(bf16[1024,128]{1,0:T(8,128)(2,1)S(1)} %get-tuple-element.33.order_ref.refs_7_), channel_id=1, source_target_pairs={{0,2},{1,3},{2,0},{3,1},{4,6},{5,7},{6,4},{7,5},{8,10},{9,11},{10,... | collective-permute-start | bytes 786440 | tf_op jit(solution)/shard_map/ppermute | solution.py:21
  25.9 2.1 %collective-permute-start.5 = (bf16[896,128]{1,0:T(8,128)(2,1)S(1)}, bf16[896,128]{1,0:T(8,128)(2,1)S(1)}, u32[]{:S(2)}, u32[]{:S(2)}) collective-permute-start(bf16[896,128]{1,0:T(8,128)(2,1)S(1)} %collective-permute-done.3.refs_0_), channel_id=1, source_target_pairs={{0,4},{4,0},{8,12},{12,8},{16,20},{20,16},{24,28},{28,24},{1,5},{5... | collective-permute-start | bytes 688136 | tf_op jit(solution)/shard_map/ppermute | solution.py:21
  28.4 1.6 %collective-permute-start.6 = (bf16[896,128]{1,0:T(8,128)(2,1)S(1)}, bf16[896,128]{1,0:T(8,128)(2,1)S(1)}, u32[]{:S(2)}, u32[]{:S(2)}) collective-permute-start(bf16[896,128]{1,0:T(8,128)(2,1)S(1)} %collective-permute-done.4.refs_1_), channel_id=1, source_target_pairs={{0,8},{4,12},{8,0},{12,4},{16,24},{20,28},{24,16},{28,20},{1,9},{5... | collective-permute-start | bytes 688136 | tf_op jit(solution)/shard_map/ppermute | solution.py:21
  31.0 3.0 %shard_map.111 = (bf16[1024,128]{1,0:T(8,128)(2,1)S(1)}, f32[1024,128]{1,0:T(8,128)S(1)}) custom-call(bf16[8,64,3584]{2,1,0:T(8,128)(2,1)S(1)} %get-tuple-element.29.near_ref.refs_0_, bf16[8,64,3584]{2,1,0:T(8,128)(2,1)S(1)} %get-tuple-element.30.far_ref.refs_1_, f32[1024,128]{1,0:T(8,128)S(1)} %get-tuple-element.31.scale_ref.refs_2_, ...), custom_call_target="tpu_custom_call" | custom-call | tf_op jit(solution)/shard_map/pallas_call | solution.py:383
  34.5 1.6 %collective-permute-start.16 = (f32[8,896]{1,0:T(8,128)S(1)}, f32[8,896]{1,0:T(8,128)S(1)}, u32[]{:S(2)}, u32[]{:S(2)}) collective-permute-start(f32[8,896]{1,0:T(8,128)S(1)} %get-tuple-element.58), channel_id=1, source_target_pairs={{0,2},{1,3},{2,0},{3,1},{4,6},{5,7},{6,4},{7,5},{8,10},{9,11},{10,... | collective-permute-start | bytes 86024 | tf_op jit(solution)/shard_map/ppermute | solution.py:21
  36.6 1.6 %collective-permute-start.15 = (bf16[128,128]{1,0:T(8,128)(2,1)S(1)}, bf16[128,128]{1,0:T(8,128)(2,1)S(1)}, u32[]{:S(2)}, u32[]{:S(2)}) collective-permute-start(bf16[128,128]{1,0:T(8,128)(2,1)S(1)} %collective-permute-done.13.refs_12_), channel_id=1, source_target_pairs={{0,2},{1,3},{2,0},{3,1},{4,6},{5,7},{6,4},{7,5},{8,10},{9,11},{10,... | collective-permute-start | bytes 98312 | tf_op jit(solution)/shard_map/ppermute | solution.py:21
  38.4 1.7 %collective-permute-done.14.refs_13_ = bf16[128,128]{1,0:T(8,128)(2,1)S(1)} collective-permute-done((bf16[128,128]{1,0:T(8,128)(2,1)S(1)}, bf16[128,128]{1,0:T(8,128)(2,1)S(1)}, u32[]{:S(2)}, u32[]{:S(2)}) %collective-permute-start.14) | collective-permute-done | bytes 32800 | tf_op jit(solution)/shard_map/ppermute | solution.py:21
  40.5 2.5 %shard_map.113 = f32[8,256]{1,0:T(8,128)S(1)} custom-call(bf16[8,64,3584]{2,1,0:T(8,128)(2,1)S(1)} %get-tuple-element.29.near_ref.refs_0_, bf16[8,64,3584]{2,1,0:T(8,128)(2,1)S(1)} %get-tuple-element.30.far_ref.refs_1_, f32[1024,128]{1,0:T(8,128)S(1)} %get-tuple-element.31.scale_ref.refs_2_, bf16[1024,128]{1,0:T(8,128)(2,1)S(1)} %get-tuple-element.36.refs_3_, ...), custom_call_target="tpu_custom_call" | custom-call | tf_op jit(solution)/shard_map/pallas_call | solution.py:421
  44.2 1.6 %collective-permute-start.18 = (f32[8,256]{1,0:T(8,128)S(1)}, f32[8,256]{1,0:T(8,128)S(1)}, u32[]{:S(2)}, u32[]{:S(2)}) collective-permute-start(f32[8,256]{1,0:T(8,128)S(1)} %add.317), channel_id=1, source_target_pairs={{0,2},{1,3},{2,0},{3,1},{4,6},{5,7},{6,4},{7,5},{8,10},{9,11},{10,... | collective-permute-start | bytes 24584 | tf_op jit(solution)/shard_map/ppermute | solution.py:21
  46.1 1.8 %collective-permute-done.18 = f32[8,256]{1,0:T(8,128)S(1)} collective-permute-done((f32[8,256]{1,0:T(8,128)S(1)}, f32[8,256]{1,0:T(8,128)S(1)}, u32[]{:S(2)}, u32[]{:S(2)}) %collective-permute-start.18) | collective-permute-done | bytes 8224 | tf_op jit(solution)/shard_map/ppermute | solution.py:21
  47.9 1.7 %collective-permute-start.19 = (f32[8,256]{1,0:T(8,128)S(1)}, f32[8,256]{1,0:T(8,128)S(1)}, u32[]{:S(2)}, u32[]{:S(2)}) collective-permute-start(f32[8,256]{1,0:T(8,128)S(1)} %add.318), channel_id=1, source_target_pairs={{0,4},{4,0},{8,12},{12,8},{16,20},{20,16},{24,28},{28,24},{1,5},{5... | collective-permute-start | bytes 24584 | tf_op jit(solution)/shard_map/ppermute | solution.py:21
  49.8 1.7 %collective-permute-done.19 = f32[8,256]{1,0:T(8,128)S(1)} collective-permute-done((f32[8,256]{1,0:T(8,128)S(1)}, f32[8,256]{1,0:T(8,128)S(1)}, u32[]{:S(2)}, u32[]{:S(2)}) %collective-permute-start.19) | collective-permute-done | bytes 8224 | tf_op jit(solution)/shard_map/ppermute | solution.py:21
  51.5 1.7 %collective-permute-start.20 = (f32[16,256]{1,0:T(8,128)S(1)}, f32[16,256]{1,0:T(8,128)S(1)}, u32[]{:S(2)}, u32[]{:S(2)}) collective-permute-start(f32[16,256]{1,0:T(8,128)S(1)} %pad_maximum_fusion.2), channel_id=1, source_target_pairs={{0,8},{4,12},{8,0},{12,4},{16,24},{20,28},{24,16},{28,20},{1,9},{5... | collective-permute-start | bytes 49160 | tf_op jit(solution)/shard_map/ppermute | solution.py:21
  53.2 2.1 %collective-permute-done.20 = f32[16,256]{1,0:T(8,128)S(1)} collective-permute-done((f32[16,256]{1,0:T(8,128)S(1)}, f32[16,256]{1,0:T(8,128)S(1)}, u32[]{:S(2)}, u32[]{:S(2)}) %collective-permute-start.20) | collective-permute-done | bytes 16416 | tf_op jit(solution)/shard_map/ppermute | solution.py:21
  55.3 2.7 %collective-permute-start.21 = (f32[32,256]{1,0:T(8,128)S(1)}, f32[32,256]{1,0:T(8,128)S(1)}, u32[]{:S(2)}, u32[]{:S(2)}) collective-permute-start(f32[32,256]{1,0:T(8,128)S(1)} %pad_maximum_fusion.1.near_ref), channel_id=1, source_target_pairs={{0,16},{4,20},{8,24},{12,28},{16,0},{20,4},{24,8},{28,12},{1,17},{... | collective-permute-start | bytes 98312 | tf_op jit(solution)/shard_map/ppermute | solution.py:21
  58.1 1.9 %collective-permute-done.21.far_ref = f32[32,256]{1,0:T(8,128)S(1)} collective-permute-done((f32[32,256]{1,0:T(8,128)S(1)}, f32[32,256]{1,0:T(8,128)S(1)}, u32[]{:S(2)}, u32[]{:S(2)}) %collective-permute-start.21) | collective-permute-done | bytes 32800 | tf_op jit(solution)/shard_map/ppermute | solution.py:21
  60.1 1.4 %shard_map.114 = bf16[4,4,64]{2,1,0:T(4,128)(2,1)} custom-call(f32[32,256]{1,0:T(8,128)S(1)} %pad_maximum_fusion.1.near_ref, f32[32,256]{1,0:T(8,128)S(1)} %collective-permute-done.21.far_ref, f32[16,64]{1,0:T(8,128)S(1)} %fusion.1.select_ref, f32[16,16]{1,0:T(8,128)S(1)} %fusion.8.allow_ref, f32[16,1]{1,0:T(8,128)S(1)} %copy.13.fill_ref, ...), custom_call_target="tpu_custom_call" | custom-call | tf_op jit(solution)/shard_map/pallas_call | solution.py:461
  (81 shorter events, 12.1 us)
Async XLA Ops:
  0.0 17.6 %collective-permute-start = (bf16[8,64,3584]{2,1,0:T(8,128)(2,1)}, bf16[8,64,3584]{2,1,0:T(8,128)(2,1)}, u32[]{:S(2)}, u32[]{:S(2)}) collective-permute-start(bf16[8,64,3584]{2,1,0:T(8,128)(2,1)} %near_ref.1), channel_id=1, source_target_pairs={{0,1},{1,0},{2,3},{3,2},{4,5},{5,4},{6,7},{7,6},{8,9},{9,8},{10,11... | collective-permute-start | bytes 11010056 | tf_op jit(solution)/shard_map/ppermute | solution.py:21
  1.4 9.1 %collective-permute-start.1 = (bf16[2,16,3584]{2,1,0:T(8,128)(2,1)S(1)}, bf16[2,16,3584]{2,1,0:T(8,128)(2,1)S(1)}, u32[]{:S(2)}, u32[]{:S(2)}) collective-permute-start(bf16[2,16,3584]{2,1,0:T(8,128)(2,1)S(1)} %dynamic-slice_bitcast_fusion.4), channel_id=1, source_target_pairs={{0,2},{1,3},{2,0},{3,1},{4,6},{5,7},{6,4},{7,5},{8,10},{9,11},{10,... | collective-permute-start | bytes 688136 | tf_op jit(solution)/shard_map/ppermute | solution.py:21
  5.2 20.4 %collective-permute-start.3 = (bf16[896,128]{1,0:T(8,128)(2,1)S(1)}, bf16[896,128]{1,0:T(8,128)(2,1)S(1)}, u32[]{:S(2)}, u32[]{:S(2)}) collective-permute-start(bf16[896,128]{1,0:T(8,128)(2,1)S(1)} %get-tuple-element.57), channel_id=1, source_target_pairs={{0,2},{1,3},{2,0},{3,1},{4,6},{5,7},{6,4},{7,5},{8,10},{9,11},{10,... | collective-permute-start | bytes 688136 | tf_op jit(solution)/shard_map/ppermute | solution.py:21
  5.3 20.6 %collective-permute-start.4 = (bf16[896,128]{1,0:T(8,128)(2,1)S(1)}, bf16[896,128]{1,0:T(8,128)(2,1)S(1)}, u32[]{:S(2)}, u32[]{:S(2)}) collective-permute-start(bf16[896,128]{1,0:T(8,128)(2,1)S(1)} %get-tuple-element.56), channel_id=1, source_target_pairs={{0,2},{1,3},{2,0},{3,1},{4,6},{5,7},{6,4},{7,5},{8,10},{9,11},{10,... | collective-permute-start | bytes 688136 | tf_op jit(solution)/shard_map/ppermute | solution.py:21
  8.2 16.9 %collective-permute-start.10 = (bf16[896,128]{1,0:T(8,128)(2,1)S(1)}, bf16[896,128]{1,0:T(8,128)(2,1)S(1)}, u32[]{:S(2)}, u32[]{:S(2)}) collective-permute-start(bf16[896,128]{1,0:T(8,128)(2,1)S(1)} %constant_dynamic-slice_fusion.refs_0_), channel_id=1, source_target_pairs={{0,2},{1,3},{2,0},{3,1},{4,6},{5,7},{6,4},{7,5},{8,10},{9,11},{10,... | collective-permute-start | bytes 688136 | tf_op jit(solution)/shard_map/ppermute | solution.py:21
  10.5 7.1 %collective-permute-start.2 = (bf16[2,16,3584]{2,1,0:T(8,128)(2,1)S(1)}, bf16[2,16,3584]{2,1,0:T(8,128)(2,1)S(1)}, u32[]{:S(2)}, u32[]{:S(2)}) collective-permute-start(bf16[2,16,3584]{2,1,0:T(8,128)(2,1)S(1)} %collective-permute-done.1.order_ref.refs_0_), channel_id=1, source_target_pairs={{0,4},{4,0},{8,12},{12,8},{16,20},{20,16},{24,28},{28,24},{1,5},{5... | collective-permute-start | bytes 688136 | tf_op jit(solution)/shard_map/ppermute | solution.py:21
  23.3 7.7 %collective-permute-start.7 = (bf16[1024,128]{1,0:T(8,128)(2,1)S(1)}, bf16[1024,128]{1,0:T(8,128)(2,1)S(1)}, u32[]{:S(2)}, u32[]{:S(2)}) collective-permute-start(bf16[1024,128]{1,0:T(8,128)(2,1)S(1)} %get-tuple-element.33.order_ref.refs_7_), channel_id=1, source_target_pairs={{0,2},{1,3},{2,0},{3,1},{4,6},{5,7},{6,4},{7,5},{8,10},{9,11},{10,... | collective-permute-start | bytes 786440 | tf_op jit(solution)/shard_map/ppermute | solution.py:21
  24.9 13.5 %collective-permute-start.8 = (bf16[1024,128]{1,0:T(8,128)(2,1)S(1)}, bf16[1024,128]{1,0:T(8,128)(2,1)S(1)}, u32[]{:S(2)}, u32[]{:S(2)}) collective-permute-start(bf16[1024,128]{1,0:T(8,128)(2,1)S(1)} %get-tuple-element.33.order_ref.refs_7_), channel_id=1, source_target_pairs={{0,1},{1,0},{2,3},{3,2},{4,5},{5,4},{6,7},{7,6},{8,9},{9,8},{10,11... | collective-permute-start | bytes 786440 | tf_op jit(solution)/shard_map/ppermute | solution.py:21
  25.1 3.3 %collective-permute-start.12 = (bf16[896,128]{1,0:T(8,128)(2,1)S(1)}, bf16[896,128]{1,0:T(8,128)(2,1)S(1)}, u32[]{:S(2)}, u32[]{:S(2)}) collective-permute-start(bf16[896,128]{1,0:T(8,128)(2,1)S(1)} %collective-permute-done.10.refs_1_), channel_id=1, source_target_pairs={{0,1},{1,0},{2,3},{3,2},{4,5},{5,4},{6,7},{7,6},{8,9},{9,8},{10,11... | collective-permute-start | bytes 688136 | tf_op jit(solution)/shard_map/ppermute | solution.py:21
  25.6 4.5 %collective-permute-start.11 = (bf16[896,128]{1,0:T(8,128)(2,1)S(1)}, bf16[896,128]{1,0:T(8,128)(2,1)S(1)}, u32[]{:S(2)}, u32[]{:S(2)}) collective-permute-start(bf16[896,128]{1,0:T(8,128)(2,1)S(1)} %constant_dynamic-slice_fusion.refs_0_), channel_id=1, source_target_pairs={{0,1},{1,0},{2,3},{3,2},{4,5},{5,4},{6,7},{7,6},{8,9},{9,8},{10,11... | collective-permute-start | bytes 688136 | tf_op jit(solution)/shard_map/ppermute | solution.py:21
  25.9 10.3 %collective-permute-start.5 = (bf16[896,128]{1,0:T(8,128)(2,1)S(1)}, bf16[896,128]{1,0:T(8,128)(2,1)S(1)}, u32[]{:S(2)}, u32[]{:S(2)}) collective-permute-start(bf16[896,128]{1,0:T(8,128)(2,1)S(1)} %collective-permute-done.3.refs_0_), channel_id=1, source_target_pairs={{0,4},{4,0},{8,12},{12,8},{16,20},{20,16},{24,28},{28,24},{1,5},{5... | collective-permute-start | bytes 688136 | tf_op jit(solution)/shard_map/ppermute | solution.py:21
  28.4 8.1 %collective-permute-start.6 = (bf16[896,128]{1,0:T(8,128)(2,1)S(1)}, bf16[896,128]{1,0:T(8,128)(2,1)S(1)}, u32[]{:S(2)}, u32[]{:S(2)}) collective-permute-start(bf16[896,128]{1,0:T(8,128)(2,1)S(1)} %collective-permute-done.4.refs_1_), channel_id=1, source_target_pairs={{0,8},{4,12},{8,0},{12,4},{16,24},{20,28},{24,16},{28,20},{1,9},{5... | collective-permute-start | bytes 688136 | tf_op jit(solution)/shard_map/ppermute | solution.py:21
  30.5 4.0 %collective-permute-start.13 = (bf16[128,128]{1,0:T(8,128)(2,1)S(1)}, bf16[128,128]{1,0:T(8,128)(2,1)S(1)}, u32[]{:S(2)}, u32[]{:S(2)}) collective-permute-start(bf16[128,128]{1,0:T(8,128)(2,1)S(1)} %shard_map.112.refs_11_), channel_id=1, source_target_pairs={{0,4},{4,0},{8,12},{12,8},{16,20},{20,16},{24,28},{28,24},{1,5},{5... | collective-permute-start | bytes 98312 | tf_op jit(solution)/shard_map/ppermute | solution.py:21
  31.0 9.5 %collective-permute-start.9 = (bf16[1024,128]{1,0:T(8,128)(2,1)S(1)}, bf16[1024,128]{1,0:T(8,128)(2,1)S(1)}, u32[]{:S(2)}, u32[]{:S(2)}) collective-permute-start(bf16[1024,128]{1,0:T(8,128)(2,1)S(1)} %collective-permute-done.7.refs_8_), channel_id=1, source_target_pairs={{0,1},{1,0},{2,3},{3,2},{4,5},{5,4},{6,7},{7,6},{8,9},{9,8},{10,11... | collective-permute-start | bytes 786440 | tf_op jit(solution)/shard_map/ppermute | solution.py:21
  34.5 3.9 %collective-permute-start.16 = (f32[8,896]{1,0:T(8,128)S(1)}, f32[8,896]{1,0:T(8,128)S(1)}, u32[]{:S(2)}, u32[]{:S(2)}) collective-permute-start(f32[8,896]{1,0:T(8,128)S(1)} %get-tuple-element.58), channel_id=1, source_target_pairs={{0,2},{1,3},{2,0},{3,1},{4,6},{5,7},{6,4},{7,5},{8,10},{9,11},{10,... | collective-permute-start | bytes 86024 | tf_op jit(solution)/shard_map/ppermute | solution.py:21
  36.2 3.9 %collective-permute-start.14 = (bf16[128,128]{1,0:T(8,128)(2,1)S(1)}, bf16[128,128]{1,0:T(8,128)(2,1)S(1)}, u32[]{:S(2)}, u32[]{:S(2)}) collective-permute-start(bf16[128,128]{1,0:T(8,128)(2,1)S(1)} %shard_map.112.refs_11_), channel_id=1, source_target_pairs={{0,2},{1,3},{2,0},{3,1},{4,6},{5,7},{6,4},{7,5},{8,10},{9,11},{10,... | collective-permute-start | bytes 98312 | tf_op jit(solution)/shard_map/ppermute | solution.py:21
  36.6 3.9 %collective-permute-start.15 = (bf16[128,128]{1,0:T(8,128)(2,1)S(1)}, bf16[128,128]{1,0:T(8,128)(2,1)S(1)}, u32[]{:S(2)}, u32[]{:S(2)}) collective-permute-start(bf16[128,128]{1,0:T(8,128)(2,1)S(1)} %collective-permute-done.13.refs_12_), channel_id=1, source_target_pairs={{0,2},{1,3},{2,0},{3,1},{4,6},{5,7},{6,4},{7,5},{8,10},{9,11},{10,... | collective-permute-start | bytes 98312 | tf_op jit(solution)/shard_map/ppermute | solution.py:21
  40.5 19.6 %copy-start.6 = (bf16[256,3,64]{0,2,1:T(8,128)(2,1)S(1)}, bf16[256,3,64]{0,2,1:T(8,128)(2,1)}, u32[]{:S(2)}) copy-start(bf16[256,3,64]{0,2,1:T(8,128)(2,1)} %param.21) | copy-start | bytes 294916
  40.5 19.6 %copy-start.9 = (f32[256]{0:T(256)S(1)}, f32[256]{0:T(256)}, u32[]{:S(2)}) copy-start(f32[256]{0:T(256)} %param.20) | copy-start | bytes 3076
  43.0 1.2 %collective-permute-start.17 = (f32[8,256]{1,0:T(8,128)S(1)}, f32[8,256]{1,0:T(8,128)S(1)}, u32[]{:S(2)}, u32[]{:S(2)}) collective-permute-start(f32[8,256]{1,0:T(8,128)S(1)} %shard_map.113), channel_id=1, source_target_pairs={{0,1},{1,0},{2,3},{3,2},{4,5},{5,4},{6,7},{7,6},{8,9},{9,8},{10,11... | collective-permute-start | bytes 24584 | tf_op jit(solution)/shard_map/ppermute | solution.py:21
  44.2 3.7 %collective-permute-start.18 = (f32[8,256]{1,0:T(8,128)S(1)}, f32[8,256]{1,0:T(8,128)S(1)}, u32[]{:S(2)}, u32[]{:S(2)}) collective-permute-start(f32[8,256]{1,0:T(8,128)S(1)} %add.317), channel_id=1, source_target_pairs={{0,2},{1,3},{2,0},{3,1},{4,6},{5,7},{6,4},{7,5},{8,10},{9,11},{10,... | collective-permute-start | bytes 24584 | tf_op jit(solution)/shard_map/ppermute | solution.py:21
  47.9 3.7 %collective-permute-start.19 = (f32[8,256]{1,0:T(8,128)S(1)}, f32[8,256]{1,0:T(8,128)S(1)}, u32[]{:S(2)}, u32[]{:S(2)}) collective-permute-start(f32[8,256]{1,0:T(8,128)S(1)} %add.318), channel_id=1, source_target_pairs={{0,4},{4,0},{8,12},{12,8},{16,20},{20,16},{24,28},{28,24},{1,5},{5... | collective-permute-start | bytes 24584 | tf_op jit(solution)/shard_map/ppermute | solution.py:21
  51.5 3.7 %collective-permute-start.20 = (f32[16,256]{1,0:T(8,128)S(1)}, f32[16,256]{1,0:T(8,128)S(1)}, u32[]{:S(2)}, u32[]{:S(2)}) collective-permute-start(f32[16,256]{1,0:T(8,128)S(1)} %pad_maximum_fusion.2), channel_id=1, source_target_pairs={{0,8},{4,12},{8,0},{12,4},{16,24},{20,28},{24,16},{28,20},{1,9},{5... | collective-permute-start | bytes 49160 | tf_op jit(solution)/shard_map/ppermute | solution.py:21
  55.3 4.8 %collective-permute-start.21 = (f32[32,256]{1,0:T(8,128)S(1)}, f32[32,256]{1,0:T(8,128)S(1)}, u32[]{:S(2)}, u32[]{:S(2)}) collective-permute-start(f32[32,256]{1,0:T(8,128)S(1)} %pad_maximum_fusion.1.near_ref), channel_id=1, source_target_pairs={{0,16},{4,20},{8,24},{12,28},{16,0},{20,4},{24,8},{28,12},{1,17},{... | collective-permute-start | bytes 98312 | tf_op jit(solution)/shard_map/ppermute | solution.py:21
  (12 other events, 91.9 us)

commit v5 on v4

--- a/solution.py
+++ b/solution.py
@@ -132,7 +132,7 @@
     )
 
 
-def query_kernel(near_ref, far_ref, scale_ref, query_ref, *refs):
+def query_kernel(order_ref, near_ref, far_ref, scale_ref, query_ref, *refs):
     part_refs, (own_ref, *half_refs) = refs[:len(refs) // 3 * 2], refs[len(refs) // 3 * 2:]
     slots, count, width = near_ref.shape
     rows = slots * count
@@ -145,11 +145,23 @@
 
 
 def product_kernel(masks, order_ref, output_ref, *refs):
-    proj_refs, out_ref = refs[:-1], refs[-1]
+    n = len(masks)
+    proj_refs, mean_refs, (out_ref, *packed_refs) = refs[:n], refs[n:n * 3 // 2 - 1], refs[n * 3 // 2 - 1:]
     total = jnp.zeros(out_ref.shape, F32)
     for mask, proj_ref in zip(masks, proj_refs):
         total += jnp.dot(output_ref[mask], proj_ref[...], preferred_element_type=F32)
     out_ref[...] = total.astype(BF16)
+    height, lanes = out_ref.shape
+    for mean_ref, packed_ref in zip(mean_refs, packed_refs):
+        packed_ref[:height, :] = total.astype(BF16)
+        both = split(mean_ref[...])
+        rows, block = both.shape
+        for i in range(0, block, lanes):
+            take = min(lanes, block - i)
+            at = height + i // lanes * rows
+            if take < lanes:
+                packed_ref[at:at + rows, :] = jnp.zeros((rows, lanes), BF16)
+            packed_ref[at:at + rows, :take] = both[:, i:i + take]
 
 
 def split(value):
@@ -174,7 +186,7 @@
     early_refs, b_refs, c_refs = take(n - 1), take(n - 1), take(n - 1)
     near_refs, far_refs = take(n), take(n)
     w2_refs = [take(2) for _ in range(n)]
-    mean_refs = take(n)
+    mean_ref, = take(1)
     place_ref, proj_ref, out_ref, q_ref, kv_ref, score_ref, weight_ref, ctx_ref, w2_ref = take(9)
     slots, tokens, _ = x_refs[0].shape
     head_dim = query_ref.shape[1]
@@ -188,7 +200,7 @@
     for p in range(n):
         for i in range(2):
             at_lane = pl.multiple_of((x_bit ^ i) * part, 128)
-            w2_ref[p, :, pl.ds(at_lane, part)] = w2_refs[p][i][...]
+            w2_ref[p, :, pl.ds(at_lane, part)] = w2_refs[p][i][:head_dim, :]
 
     for p in range(n):
         for c in range(2):
@@ -237,9 +249,14 @@
             ) * (1.0 / length)
             for j, p in enumerate(heads):
                 ctx_ref[p, s:s + 1, :] = context[j:j + 1]
-    mean = mean_refs[0][...]
+    mean = mean_ref[...]
     for p in range(1, n):
-        mean += mean_refs[p][...]
+        packed = w2_refs[p][0]
+        chunks = [
+            packed[at:at + 2 * slots, :] for at in range(head_dim, packed.shape[0], 2 * slots)
+        ]
+        both = jnp.concatenate(chunks, axis=1)[:, :mean.shape[1]]
+        mean += joined(both.astype(F32))
     total = joined(jnp.dot(split(mean), proj_ref[...], preferred_element_type=F32))
     for p in range(n):
         total += joined(jnp.dot(split(ctx_ref[p]), w2_ref[p], preferred_element_type=F32))
@@ -299,12 +316,12 @@
     kv_y = [flipped(kv_half, "tp", m) for m in masks[1:]]
     tokens_far = flipped(tokens, "tp", 1)
     part_q, part_doc = width // 4, doc_width // 2
-    query_here = after(enc_query, kv_half)
+    proj = cut(after(doc_proj, kv_half), x_bit, part_doc, 1)
+    proj_near = [proj] + [flipped(proj, "tp", m) for m in masks[1:]]
+    query_here = after(enc_query, proj)
     b_part, c_part = cut(query_here, x_bit, part_q, 0), cut(query_here, 2 + z_bit, part_q, 0)
     b_y = [flipped(b_part, "tp", m) for m in masks[1:]]
     c_y = [flipped(c_part, "tp", m) for m in masks[1:]]
-    proj = cut(after(doc_proj, (b_part, c_part)), x_bit, part_doc, 1)
-    proj_near = [proj] + [flipped(proj, "tp", m) for m in masks[1:]]
 
     weights = []
     for w in kv_y:
@@ -336,21 +353,28 @@
         compiler_params=room(*operands, *out),
     )(*operands)
     kv_near = [kv] + [flipped(kv, "tp", m) for m in masks[1:]]
-    kv_far = [flipped(k, "tp", 1) for k in kv_near]
-
-    proj_near = [after(p, kv) for p in proj_near]
+    kv_far = [flipped(after(k, kv_near[1:]), "tp", 1) for k in kv_near]
+
+    proj_near = [after(p, weights[-1]) for p in proj_near]
     proj_all = proj_near + [flipped(p, "tp", 1) for p in proj_near]
     origin = masks + [m + 1 for m in masks]
-    output_blocks = jnp.stack([cut(after(enc_output, kv), tp_index ^ m, block, 1) for m in range(n_tp)], axis=0)
-    out = jax.ShapeDtypeStruct((head_dim, part_doc), BF16)
-    w2 = pl.pallas_call(
+    output_blocks = jnp.stack([cut(after(enc_output, weights[-1]), tp_index ^ m, block, 1) for m in range(n_tp)], axis=0)
+    mean = mean.reshape(slots, n_tp, block)
+    means = [lax.dynamic_index_in_dim(mean, tp_index ^ m, 1, keepdims=False) for m in masks]
+    height = head_dim + -(-block // part_doc) * 2 * slots
+    out = [jax.ShapeDtypeStruct((head_dim, part_doc), BF16)]
+    out += [jax.ShapeDtypeStruct((height, part_doc), BF16) for _ in masks[1:]]
+    w2, *packed = pl.pallas_call(
         functools.partial(product_kernel, origin),
         in_specs=[pl.BlockSpec(memory_space=pl.ANY)]
-        + [pl.BlockSpec(memory_space=pltpu.VMEM)] * (1 + n_tp),
+        + [pl.BlockSpec(memory_space=pltpu.VMEM)] * (n_tp + len(masks)),
         out_shape=out,
-        compiler_params=room(output_blocks, *proj_all, out),
-    )(kv, output_blocks, *proj_all)
-    w2_pair = [w2, flipped(w2, "rep", 1)]
+        compiler_params=room(output_blocks, *proj_all, *means, *out),
+    )(kv, output_blocks, *proj_all, *means[1:])
+    w2_all = [w2, flipped(w2, "rep", 1)]
+    for m, p in zip(masks[1:], packed):
+        w2_all += [flipped(p, "tp", m), flipped(w2_all[1], "tp", m)]
+
     count = 2 * lanes
     column = jnp.arange(count, dtype=jnp.int32)
     core = column // lanes
@@ -381,17 +405,12 @@
     out = [jax.ShapeDtypeStruct((2 * rows, head_dim), BF16)]
     out += [jax.ShapeDtypeStruct((2 * rows, head_dim), F32) for _ in masks[1:]]
     own, *early = pl.pallas_call(
-        query_kernel, out_shape=out, compiler_params=room(*operands, *out)
-    )(*operands)
-
-    mean, *w2_pair = after((mean, *w2_pair), own)
-    mean = mean.reshape(slots, n_tp, block)
-
-    def mean_of(m):
-        return lax.dynamic_index_in_dim(mean, tp_index ^ m, 1, keepdims=False)
-
-    means = [mean_of(0)] + [flipped(mean_of(m), "tp", m) for m in masks[1:]]
-    w2_all = w2_pair + [flipped(w, "tp", m) for m in masks[1:] for w in w2_pair]
+        query_kernel,
+        in_specs=[pl.BlockSpec(memory_space=pl.ANY)]
+        + [pl.BlockSpec(memory_space=pltpu.VMEM)] * len(operands),
+        out_shape=out,
+        compiler_params=room(*operands, *out),
+    )(w2_all[1], *operands)
 
     n = len(masks)
     groups = n_tp // group
@@ -406,7 +425,7 @@
         *kv_near,
         *kv_far,
         *w2_all,
-        *means,
+        means[0],
         place,
         doc_proj,
     )
@@ -425,7 +444,8 @@
         compiler_params=room(*operands, *scratch),
     )(*operands)
 
-    bit = 1
+    part = part + flipped(part, "tp", 1) + flipped(part, "tp", 2) + flipped(part, "tp", 3)
+    bit = 4
     while bit < n_tp:
         part = part + flipped(part, "tp", bit)
         bit *= 2

time: 61.8 us -> 58.9 us (0.953)
  starting transfers between devices: 25.1 us -> 23.8 us
  waiting for transfers between devices: 13.7 us -> 12.6 us
  local copies, waits for them, and re-layouts: 7.7 us -> 6.99 us
    ppermute x22, starting transfers between devices: 25.1 us -> 23.8 us  [flipped(): return lax.ppermute(block, axis, [(i, i ^ mask) for i in range(count)])]
    ppermute x22, waiting for transfers between devices: 13.7 us -> 12.6 us  [flipped(): return lax.ppermute(block, axis, [(i, i ^ mask) for i in range(count)])]
    unnamed x28, local copies, waits for them, and re-layouts: 4.55 us -> 3.83 us
  transfers between devices with their start and end apart: 22 -> 22, of which waited for: 11 -> 9; matrix products, arithmetic and copies ran while one was open for 7% -> 8% of each run, Pallas kernels for 15% -> 16%
where the time goes in v5:
time: 58.9 us; the launch traced here: 58.5 us
  starting transfers between devices  23.8 us (40%)
  Pallas kernels  13.4 us (23%)
  waiting for transfers between devices  12.6 us (21%)
  local copies, waits for them, and re-layouts  6.99 us (12%)
  other arithmetic  1.27 us (2%)
    ppermute x22, starting transfers between devices, flipped(): return lax.ppermute(block, axis, [(i, i ^ mask) for i in range(count)])  23.8 us
    ppermute x22, waiting for transfers between devices, flipped(): return lax.ppermute(block, axis, [(i, i ^ mask) for i in range(count)])  12.6 us
    pallas_call x1, Pallas kernels, local(): pl.pallas_call(functools.partial(keyvalue_kernel, length), out_shape=out,...  4.92 us
    unnamed x28, local copies, waits for them, and re-layouts  3.83 us
    pallas_call x1, Pallas kernels, local(): pl.pallas_call(query_kernel, in_specs=[pl.BlockSpec(memory_space=pl.ANY)]...  3.02 us
    dynamic_slice x3, local copies, waits for them, and re-layouts, cut(): return lax.dynamic_slice_in_dim(array, at * size, size, axis=axis)  2.99 us
    pallas_call x1, Pallas kernels, local(): pl.pallas_call(functools.partial(attention_kernel, masks, group, length),...  2.49 us
    pallas_call x1, Pallas kernels, local(): pl.pallas_call(document_kernel, out_shape=jax.ShapeDtypeStruct((OWN_DOCS,...  1.37 us
  transfers between devices with their start and end apart: 22, of which 9 were waited for; matrix products, arithmetic and copies ran while one was open for 8% of the time, Pallas kernels for 16%

profile of v5, /device:TPU:0, one launch (start us, length us, event | category | flops | bytes accessed | tf_op | source)
XLA Modules:
  0.0 58.5 jit_solution(13156145060302450335)
XLA Ops:
  1.4 2.7 %collective-permute-start.1 = (bf16[2,16,3584]{2,1,0:T(8,128)(2,1)S(1)}, bf16[2,16,3584]{2,1,0:T(8,128)(2,1)S(1)}, u32[]{:S(2)}, u32[]{:S(2)}) collective-permute-start(bf16[2,16,3584]{2,1,0:T(8,128)(2,1)S(1)} %dynamic-slice_bitcast_fusion.4), channel_id=1, source_target_pairs={{0,2},{1,3},{2,0},{3,1},{4,6},{5,7},{6,4},{7,5},{8,10},{9,11},{10,... | collective-permute-start | bytes 688136 | tf_op jit(solution)/shard_map/ppermute | solution.py:21
  5.2 1.1 %constant_dynamic-slice_fusion = (bf16[896,128]{1,0:T(8,128)(2,1)S(1)}, bf16[896,128]{1,0:T(8,128)(2,1)S(1)}) fusion(bf16[3584,128]{1,0:T(8,128)(2,1)} %query_ref.1, s32[]{:T(128)S(6)} %select_n.263, s32[]{:T(128)S(6)} %select_n.260), kind=kLoop, calls=%fused_computation.38 | loop fusion | bytes 917512 | tf_op jit(solution)/shard_map/dynamic_slice | solution.py:29
  6.2 2.0 %collective-permute-start.7 = (bf16[896,128]{1,0:T(8,128)(2,1)S(1)}, bf16[896,128]{1,0:T(8,128)(2,1)S(1)}, u32[]{:S(2)}, u32[]{:S(2)}) collective-permute-start(bf16[896,128]{1,0:T(8,128)(2,1)S(1)} %get-tuple-element.55), channel_id=1, source_target_pairs={{0,2},{1,3},{2,0},{3,1},{4,6},{5,7},{6,4},{7,5},{8,10},{9,11},{10,... | collective-permute-start | bytes 688136 | tf_op jit(solution)/shard_map/ppermute | solution.py:21
  8.7 1.9 %collective-permute-done.1.order_ref.refs_0_ = bf16[2,16,3584]{2,1,0:T(8,128)(2,1)S(1)} collective-permute-done((bf16[2,16,3584]{2,1,0:T(8,128)(2,1)S(1)}, bf16[2,16,3584]{2,1,0:T(8,128)(2,1)S(1)}, u32[]{:S(2)}, u32[]{:S(2)}) %collective-permute-start.1) | collective-permute-done | bytes 229408 | tf_op jit(solution)/shard_map/ppermute | solution.py:21
  10.5 1.9 %collective-permute-start.2 = (bf16[2,16,3584]{2,1,0:T(8,128)(2,1)S(1)}, bf16[2,16,3584]{2,1,0:T(8,128)(2,1)S(1)}, u32[]{:S(2)}, u32[]{:S(2)}) collective-permute-start(bf16[2,16,3584]{2,1,0:T(8,128)(2,1)S(1)} %collective-permute-done.1.order_ref.refs_0_), channel_id=1, source_target_pairs={{0,4},{4,0},{8,12},{12,8},{16,20},{20,16},{24,28},{28,24},{1,5},{5... | collective-permute-start | bytes 688136 | tf_op jit(solution)/shard_map/ppermute | solution.py:21
  12.5 2.0 %copy-done = bf16[8,64,3584]{2,1,0:T(8,128)(2,1)S(1)} copy-done((bf16[8,64,3584]{2,1,0:T(8,128)(2,1)S(1)}, bf16[8,64,3584]{2,1,0:T(8,128)(2,1)}, u32[]{:S(2)}) %copy-start) | copy-done | bytes 3670040
  14.5 1.0 %copy-done.2 = bf16[3584,2,32]{0,2,1:T(8,128)(2,1)S(1)} copy-done((bf16[3584,2,32]{0,2,1:T(8,128)(2,1)S(1)}, bf16[3584,2,32]{0,2,1:T(8,128)(2,1)}, u32[]{:S(2)}) %copy-start.2) | copy-done | bytes 458776
  16.3 1.2 %shard_map.109 = (f32[512,128]{1,0:T(8,128)S(1)}, f32[8,3584]{1,0:T(8,128)S(1)}) custom-call(bf16[2,16,3584]{2,1,0:T(8,128)(2,1)S(1)} %collective-permute-done.1.order_ref.refs_0_, bf16[8,64,3584]{2,1,0:T(8,128)(2,1)S(1)} %copy-done, f32[3584]{0:T(1024)S(1)} %copy-done.7, bf16[2,32,3584]{2,1,0:T(8,128)(2,1)S(1)} %bitcast.27), custom_call_target="tpu_custom_call" | custom-call | tf_op jit(solution)/shard_map/pallas_call | solution.py:336
  18.5 4.9 %shard_map.110 = (bf16[1024,128]{1,0:T(8,128)(2,1)S(1)}, bf16[8,64,3584]{2,1,0:T(8,128)(2,1)S(1)}, bf16[8,64,3584]{2,1,0:T(8,128)(2,1)S(1)}, f32[1024,128]{1,0:T(8,128)S(1)}, f32[8,3584]{1,0:T(8,128)S(1)}) custom-call(bf16[8,64,3584]{2,1,0:T(8,128)(2,1)S(1)} %copy-done.1, bf16[8,64,3584]{2,1,0:T(8,128)(2,1)} %collective-permute-done.far_ref, ...), custom_call_target="tpu_custom_call" | custom-call | tf_op jit(solution)/shard_map/pallas_call | solution.py:350
  23.4 1.6 %collective-permute-start.11 = (bf16[1024,128]{1,0:T(8,128)(2,1)S(1)}, bf16[1024,128]{1,0:T(8,128)(2,1)S(1)}, u32[]{:S(2)}, u32[]{:S(2)}) collective-permute-start(bf16[1024,128]{1,0:T(8,128)(2,1)S(1)} %get-tuple-element.45.order_ref.refs_7_), channel_id=1, source_target_pairs={{0,2},{1,3},{2,0},{3,1},{4,6},{5,7},{6,4},{7,5},{8,10},{9,11},{10,... | collective-permute-start | bytes 786440 | tf_op jit(solution)/shard_map/ppermute | solution.py:21
  25.8 1.6 %collective-permute-start.6 = (bf16[128,128]{1,0:T(8,128)(2,1)S(1)}, bf16[128,128]{1,0:T(8,128)(2,1)S(1)}, u32[]{:S(2)}, u32[]{:S(2)}) collective-permute-start(bf16[128,128]{1,0:T(8,128)(2,1)S(1)} %get-tuple-element.39.refs_11_), channel_id=1, source_target_pairs={{0,4},{4,0},{8,12},{12,8},{16,20},{20,16},{24,28},{28,24},{1,5},{5... | collective-permute-start | bytes 98312 | tf_op jit(solution)/shard_map/ppermute | solution.py:21
  27.4 1.6 %collective-permute-start.10 = (bf16[896,128]{1,0:T(8,128)(2,1)S(1)}, bf16[896,128]{1,0:T(8,128)(2,1)S(1)}, u32[]{:S(2)}, u32[]{:S(2)}) collective-permute-start(bf16[896,128]{1,0:T(8,128)(2,1)S(1)} %collective-permute-done.8.refs_1_), channel_id=1, source_target_pairs={{0,8},{4,12},{8,0},{12,4},{16,24},{20,28},{24,16},{28,20},{1,9},{5... | collective-permute-start | bytes 688136 | tf_op jit(solution)/shard_map/ppermute | solution.py:21
  29.5 1.5 %collective-permute-start.14 = (bf16[240,128]{1,0:T(8,128)(2,1)S(1)}, bf16[240,128]{1,0:T(8,128)(2,1)S(1)}, u32[]{:S(2)}, u32[]{:S(2)}) collective-permute-start(bf16[240,128]{1,0:T(8,128)(2,1)S(1)} %get-tuple-element.47), channel_id=1, source_target_pairs={{0,2},{1,3},{2,0},{3,1},{4,6},{5,7},{6,4},{7,5},{8,10},{9,11},{10,... | collective-permute-start | bytes 184328 | tf_op jit(solution)/shard_map/ppermute | solution.py:21
  31.2 1.2 %collective-permute-done.11.refs_8_ = bf16[1024,128]{1,0:T(8,128)(2,1)S(1)} collective-permute-done((bf16[1024,128]{1,0:T(8,128)(2,1)S(1)}, bf16[1024,128]{1,0:T(8,128)(2,1)S(1)}, u32[]{:S(2)}, u32[]{:S(2)}) %collective-permute-start.11) | collective-permute-done | bytes 262176 | tf_op jit(solution)/shard_map/ppermute | solution.py:21
  33.8 1.5 %collective-permute-start.15 = (bf16[128,128]{1,0:T(8,128)(2,1)S(1)}, bf16[128,128]{1,0:T(8,128)(2,1)S(1)}, u32[]{:S(2)}, u32[]{:S(2)}) collective-permute-start(bf16[128,128]{1,0:T(8,128)(2,1)S(1)} %collective-permute-done.6.order_ref.refs_12_), channel_id=1, source_target_pairs={{0,2},{1,3},{2,0},{3,1},{4,6},{5,7},{6,4},{7,5},{8,10},{9,11},{10,... | collective-permute-start | bytes 98312 | tf_op jit(solution)/shard_map/ppermute | solution.py:21
  35.3 3.0 %shard_map.112 = (bf16[1024,128]{1,0:T(8,128)(2,1)S(1)}, f32[1024,128]{1,0:T(8,128)S(1)}) custom-call(bf16[128,128]{1,0:T(8,128)(2,1)S(1)} %collective-permute-done.6.order_ref.refs_12_, bf16[8,64,3584]{2,1,0:T(8,128)(2,1)S(1)} %get-tuple-element.30.near_ref.refs_0_, bf16[8,64,3584]{2,1,0:T(8,128)(2,1)S(1)} %get-tuple-element.31.far_ref.refs_1_, ...), custom_call_target="tpu_custom_call" | custom-call | tf_op jit(solution)/shard_map/pallas_call | solution.py:407
  38.4 2.5 %shard_map.113 = f32[8,256]{1,0:T(8,128)S(1)} custom-call(bf16[8,64,3584]{2,1,0:T(8,128)(2,1)S(1)} %get-tuple-element.30.near_ref.refs_0_, bf16[8,64,3584]{2,1,0:T(8,128)(2,1)S(1)} %get-tuple-element.31.far_ref.refs_1_, f32[1024,128]{1,0:T(8,128)S(1)} %get-tuple-element.32.scale_ref.refs_2_, bf16[1024,128]{1,0:T(8,128)(2,1)S(1)} %get-tuple-element.43.refs_3_, ...), custom_call_target="tpu_custom_call" | custom-call | tf_op jit(solution)/shard_map/pallas_call | solution.py:440
  43.0 1.7 %collective-permute-done.17 = f32[8,256]{1,0:T(8,128)S(1)} collective-permute-done((f32[8,256]{1,0:T(8,128)S(1)}, f32[8,256]{1,0:T(8,128)S(1)}, u32[]{:S(2)}, u32[]{:S(2)}) %collective-permute-start.17) | collective-permute-done | bytes 8224 | tf_op jit(solution)/shard_map/ppermute | solution.py:21
  45.0 1.5 %collective-permute-start.19 = (f32[8,256]{1,0:T(8,128)S(1)}, f32[8,256]{1,0:T(8,128)S(1)}, u32[]{:S(2)}, u32[]{:S(2)}) collective-permute-start(f32[8,256]{1,0:T(8,128)S(1)} %add_add_fusion), channel_id=1, source_target_pairs={{0,4},{4,0},{8,12},{12,8},{16,20},{20,16},{24,28},{28,24},{1,5},{5... | collective-permute-start | bytes 24584 | tf_op jit(solution)/shard_map/ppermute | solution.py:21
  46.6 2.0 %collective-permute-done.19 = f32[8,256]{1,0:T(8,128)S(1)} collective-permute-done((f32[8,256]{1,0:T(8,128)S(1)}, f32[8,256]{1,0:T(8,128)S(1)}, u32[]{:S(2)}, u32[]{:S(2)}) %collective-permute-start.19) | collective-permute-done | bytes 8224 | tf_op jit(solution)/shard_map/ppermute | solution.py:21
  49.6 2.8 %collective-permute-done.20 = f32[16,256]{1,0:T(8,128)S(1)} collective-permute-done((f32[16,256]{1,0:T(8,128)S(1)}, f32[16,256]{1,0:T(8,128)S(1)}, u32[]{:S(2)}, u32[]{:S(2)}) %collective-permute-start.20) | collective-permute-done | bytes 16416 | tf_op jit(solution)/shard_map/ppermute | solution.py:21
  52.4 2.8 %collective-permute-start.21 = (f32[32,256]{1,0:T(8,128)S(1)}, f32[32,256]{1,0:T(8,128)S(1)}, u32[]{:S(2)}, u32[]{:S(2)}) collective-permute-start(f32[32,256]{1,0:T(8,128)S(1)} %pad_maximum_fusion.1.near_ref), channel_id=1, source_target_pairs={{0,16},{4,20},{8,24},{12,28},{16,0},{20,4},{24,8},{28,12},{1,17},{... | collective-permute-start | bytes 98312 | tf_op jit(solution)/shard_map/ppermute | solution.py:21
  55.3 1.9 %collective-permute-done.21.far_ref = f32[32,256]{1,0:T(8,128)S(1)} collective-permute-done((f32[32,256]{1,0:T(8,128)S(1)}, f32[32,256]{1,0:T(8,128)S(1)}, u32[]{:S(2)}, u32[]{:S(2)}) %collective-permute-start.21) | collective-permute-done | bytes 32800 | tf_op jit(solution)/shard_map/ppermute | solution.py:21
  57.2 1.4 %shard_map.114 = bf16[4,4,64]{2,1,0:T(4,128)(2,1)} custom-call(f32[32,256]{1,0:T(8,128)S(1)} %pad_maximum_fusion.1.near_ref, f32[32,256]{1,0:T(8,128)S(1)} %collective-permute-done.21.far_ref, f32[16,64]{1,0:T(8,128)S(1)} %fusion.1.select_ref, f32[16,16]{1,0:T(8,128)S(1)} %fusion.8.allow_ref, f32[16,1]{1,0:T(8,128)S(1)} %copy.13.fill_ref, ...), custom_call_target="tpu_custom_call" | custom-call | tf_op jit(solution)/shard_map/pallas_call | solution.py:481
  (80 shorter events, 11.0 us)
Async XLA Ops:
  0.0 18.4 %collective-permute-start = (bf16[8,64,3584]{2,1,0:T(8,128)(2,1)}, bf16[8,64,3584]{2,1,0:T(8,128)(2,1)}, u32[]{:S(2)}, u32[]{:S(2)}) collective-permute-start(bf16[8,64,3584]{2,1,0:T(8,128)(2,1)} %near_ref.1), channel_id=1, source_target_pairs={{0,1},{1,0},{2,3},{3,2},{4,5},{5,4},{6,7},{7,6},{8,9},{9,8},{10,11... | collective-permute-start | bytes 11010056 | tf_op jit(solution)/shard_map/ppermute | solution.py:21
  1.4 9.1 %collective-permute-start.1 = (bf16[2,16,3584]{2,1,0:T(8,128)(2,1)S(1)}, bf16[2,16,3584]{2,1,0:T(8,128)(2,1)S(1)}, u32[]{:S(2)}, u32[]{:S(2)}) collective-permute-start(bf16[2,16,3584]{2,1,0:T(8,128)(2,1)S(1)} %dynamic-slice_bitcast_fusion.4), channel_id=1, source_target_pairs={{0,2},{1,3},{2,0},{3,1},{4,6},{5,7},{6,4},{7,5},{8,10},{9,11},{10,... | collective-permute-start | bytes 688136 | tf_op jit(solution)/shard_map/ppermute | solution.py:21
  5.0 12.6 %collective-permute-start.3 = (bf16[896,128]{1,0:T(8,128)(2,1)S(1)}, bf16[896,128]{1,0:T(8,128)(2,1)S(1)}, u32[]{:S(2)}, u32[]{:S(2)}) collective-permute-start(bf16[896,128]{1,0:T(8,128)(2,1)S(1)} %constant_dynamic-slice_fusion.2.refs_0_), channel_id=1, source_target_pairs={{0,2},{1,3},{2,0},{3,1},{4,6},{5,7},{6,4},{7,5},{8,10},{9,11},{10,... | collective-permute-start | bytes 688136 | tf_op jit(solution)/shard_map/ppermute | solution.py:21
  6.2 18.9 %collective-permute-start.7 = (bf16[896,128]{1,0:T(8,128)(2,1)S(1)}, bf16[896,128]{1,0:T(8,128)(2,1)S(1)}, u32[]{:S(2)}, u32[]{:S(2)}) collective-permute-start(bf16[896,128]{1,0:T(8,128)(2,1)S(1)} %get-tuple-element.55), channel_id=1, source_target_pairs={{0,2},{1,3},{2,0},{3,1},{4,6},{5,7},{6,4},{7,5},{8,10},{9,11},{10,... | collective-permute-start | bytes 688136 | tf_op jit(solution)/shard_map/ppermute | solution.py:21
  8.3 16.9 %collective-permute-start.8 = (bf16[896,128]{1,0:T(8,128)(2,1)S(1)}, bf16[896,128]{1,0:T(8,128)(2,1)S(1)}, u32[]{:S(2)}, u32[]{:S(2)}) collective-permute-start(bf16[896,128]{1,0:T(8,128)(2,1)S(1)} %get-tuple-element.54), channel_id=1, source_target_pairs={{0,2},{1,3},{2,0},{3,1},{4,6},{5,7},{6,4},{7,5},{8,10},{9,11},{10,... | collective-permute-start | bytes 688136 | tf_op jit(solution)/shard_map/ppermute | solution.py:21
  10.5 7.1 %collective-permute-start.2 = (bf16[2,16,3584]{2,1,0:T(8,128)(2,1)S(1)}, bf16[2,16,3584]{2,1,0:T(8,128)(2,1)S(1)}, u32[]{:S(2)}, u32[]{:S(2)}) collective-permute-start(bf16[2,16,3584]{2,1,0:T(8,128)(2,1)S(1)} %collective-permute-done.1.order_ref.refs_0_), channel_id=1, source_target_pairs={{0,4},{4,0},{8,12},{12,8},{16,20},{20,16},{24,28},{28,24},{1,5},{5... | collective-permute-start | bytes 688136 | tf_op jit(solution)/shard_map/ppermute | solution.py:21
  17.6 7.7 %collective-permute-start.5 = (bf16[896,128]{1,0:T(8,128)(2,1)S(1)}, bf16[896,128]{1,0:T(8,128)(2,1)S(1)}, u32[]{:S(2)}, u32[]{:S(2)}) collective-permute-start(bf16[896,128]{1,0:T(8,128)(2,1)S(1)} %collective-permute-done.3.refs_1_), channel_id=1, source_target_pairs={{0,1},{1,0},{2,3},{3,2},{4,5},{5,4},{6,7},{7,6},{8,9},{9,8},{10,11... | collective-permute-start | bytes 688136 | tf_op jit(solution)/shard_map/ppermute | solution.py:21
  17.6 7.7 %collective-permute-start.4 = (bf16[896,128]{1,0:T(8,128)(2,1)S(1)}, bf16[896,128]{1,0:T(8,128)(2,1)S(1)}, u32[]{:S(2)}, u32[]{:S(2)}) collective-permute-start(bf16[896,128]{1,0:T(8,128)(2,1)S(1)} %constant_dynamic-slice_fusion.2.refs_0_), channel_id=1, source_target_pairs={{0,1},{1,0},{2,3},{3,2},{4,5},{5,4},{6,7},{7,6},{8,9},{9,8},{10,11... | collective-permute-start | bytes 688136 | tf_op jit(solution)/shard_map/ppermute | solution.py:21
  23.4 8.9 %collective-permute-start.11 = (bf16[1024,128]{1,0:T(8,128)(2,1)S(1)}, bf16[1024,128]{1,0:T(8,128)(2,1)S(1)}, u32[]{:S(2)}, u32[]{:S(2)}) collective-permute-start(bf16[1024,128]{1,0:T(8,128)(2,1)S(1)} %get-tuple-element.45.order_ref.refs_7_), channel_id=1, source_target_pairs={{0,2},{1,3},{2,0},{3,1},{4,6},{5,7},{6,4},{7,5},{8,10},{9,11},{10,... | collective-permute-start | bytes 786440 | tf_op jit(solution)/shard_map/ppermute | solution.py:21
  25.8 6.6 %collective-permute-start.6 = (bf16[128,128]{1,0:T(8,128)(2,1)S(1)}, bf16[128,128]{1,0:T(8,128)(2,1)S(1)}, u32[]{:S(2)}, u32[]{:S(2)}) collective-permute-start(bf16[128,128]{1,0:T(8,128)(2,1)S(1)} %get-tuple-element.39.refs_11_), channel_id=1, source_target_pairs={{0,4},{4,0},{8,12},{12,8},{16,20},{20,16},{24,28},{28,24},{1,5},{5... | collective-permute-start | bytes 98312 | tf_op jit(solution)/shard_map/ppermute | solution.py:21
  27.4 10.9 %collective-permute-start.10 = (bf16[896,128]{1,0:T(8,128)(2,1)S(1)}, bf16[896,128]{1,0:T(8,128)(2,1)S(1)}, u32[]{:S(2)}, u32[]{:S(2)}) collective-permute-start(bf16[896,128]{1,0:T(8,128)(2,1)S(1)} %collective-permute-done.8.refs_1_), channel_id=1, source_target_pairs={{0,8},{4,12},{8,0},{12,4},{16,24},{20,28},{24,16},{28,20},{1,9},{5... | collective-permute-start | bytes 688136 | tf_op jit(solution)/shard_map/ppermute | solution.py:21
  29.0 9.3 %collective-permute-start.9 = (bf16[896,128]{1,0:T(8,128)(2,1)S(1)}, bf16[896,128]{1,0:T(8,128)(2,1)S(1)}, u32[]{:S(2)}, u32[]{:S(2)}) collective-permute-start(bf16[896,128]{1,0:T(8,128)(2,1)S(1)} %collective-permute-done.7.refs_0_), channel_id=1, source_target_pairs={{0,4},{4,0},{8,12},{12,8},{16,20},{20,16},{24,28},{28,24},{1,5},{5... | collective-permute-start | bytes 688136 | tf_op jit(solution)/shard_map/ppermute | solution.py:21
  29.5 4.2 %collective-permute-start.14 = (bf16[240,128]{1,0:T(8,128)(2,1)S(1)}, bf16[240,128]{1,0:T(8,128)(2,1)S(1)}, u32[]{:S(2)}, u32[]{:S(2)}) collective-permute-start(bf16[240,128]{1,0:T(8,128)(2,1)S(1)} %get-tuple-element.47), channel_id=1, source_target_pairs={{0,2},{1,3},{2,0},{3,1},{4,6},{5,7},{6,4},{7,5},{8,10},{9,11},{10,... | collective-permute-start | bytes 184328 | tf_op jit(solution)/shard_map/ppermute | solution.py:21
  32.3 6.0 %collective-permute-start.12 = (bf16[1024,128]{1,0:T(8,128)(2,1)S(1)}, bf16[1024,128]{1,0:T(8,128)(2,1)S(1)}, u32[]{:S(2)}, u32[]{:S(2)}) collective-permute-start(bf16[1024,128]{1,0:T(8,128)(2,1)S(1)} %get-tuple-element.45.order_ref.refs_7_), channel_id=1, source_target_pairs={{0,1},{1,0},{2,3},{3,2},{4,5},{5,4},{6,7},{7,6},{8,9},{9,8},{10,11... | collective-permute-start | bytes 786440 | tf_op jit(solution)/shard_map/ppermute | solution.py:21
  32.3 6.0 %collective-permute-start.13 = (bf16[1024,128]{1,0:T(8,128)(2,1)S(1)}, bf16[1024,128]{1,0:T(8,128)(2,1)S(1)}, u32[]{:S(2)}, u32[]{:S(2)}) collective-permute-start(bf16[1024,128]{1,0:T(8,128)(2,1)S(1)} %collective-permute-done.11.refs_8_), channel_id=1, source_target_pairs={{0,1},{1,0},{2,3},{3,2},{4,5},{5,4},{6,7},{7,6},{8,9},{9,8},{10,11... | collective-permute-start | bytes 786440 | tf_op jit(solution)/shard_map/ppermute | solution.py:21
  33.8 4.6 %collective-permute-start.15 = (bf16[128,128]{1,0:T(8,128)(2,1)S(1)}, bf16[128,128]{1,0:T(8,128)(2,1)S(1)}, u32[]{:S(2)}, u32[]{:S(2)}) collective-permute-start(bf16[128,128]{1,0:T(8,128)(2,1)S(1)} %collective-permute-done.6.order_ref.refs_12_), channel_id=1, source_target_pairs={{0,2},{1,3},{2,0},{3,1},{4,6},{5,7},{6,4},{7,5},{8,10},{9,11},{10,... | collective-permute-start | bytes 98312 | tf_op jit(solution)/shard_map/ppermute | solution.py:21
  38.4 18.8 %copy-start.6 = (bf16[256,3,64]{0,2,1:T(8,128)(2,1)S(1)}, bf16[256,3,64]{0,2,1:T(8,128)(2,1)}, u32[]{:S(2)}) copy-start(bf16[256,3,64]{0,2,1:T(8,128)(2,1)} %param.21) | copy-start | bytes 294916
  38.4 18.8 %copy-start.9 = (f32[256]{0:T(256)S(1)}, f32[256]{0:T(256)}, u32[]{:S(2)}) copy-start(f32[256]{0:T(256)} %param.20) | copy-start | bytes 3076
  40.9 2.1 %collective-permute-start.16 = (f32[8,256]{1,0:T(8,128)S(1)}, f32[8,256]{1,0:T(8,128)S(1)}, u32[]{:S(2)}, u32[]{:S(2)}) collective-permute-start(f32[8,256]{1,0:T(8,128)S(1)} %shard_map.113), channel_id=1, source_target_pairs={{0,1},{1,0},{2,3},{3,2},{4,5},{5,4},{6,7},{7,6},{8,9},{9,8},{10,11... | collective-permute-start | bytes 24584 | tf_op jit(solution)/shard_map/ppermute | solution.py:21
  41.0 3.7 %collective-permute-start.17 = (f32[8,256]{1,0:T(8,128)S(1)}, f32[8,256]{1,0:T(8,128)S(1)}, u32[]{:S(2)}, u32[]{:S(2)}) collective-permute-start(f32[8,256]{1,0:T(8,128)S(1)} %shard_map.113), channel_id=1, source_target_pairs={{0,2},{1,3},{2,0},{3,1},{4,6},{5,7},{6,4},{7,5},{8,10},{9,11},{10,... | collective-permute-start | bytes 24584 | tf_op jit(solution)/shard_map/ppermute | solution.py:21
  41.9 3.1 %collective-permute-start.18 = (f32[8,256]{1,0:T(8,128)S(1)}, f32[8,256]{1,0:T(8,128)S(1)}, u32[]{:S(2)}, u32[]{:S(2)}) collective-permute-start(f32[8,256]{1,0:T(8,128)S(1)} %shard_map.113), channel_id=1, source_target_pairs={{0,3},{1,2},{2,1},{3,0},{4,7},{5,6},{6,5},{7,4},{8,11},{9,10},{10,... | collective-permute-start | bytes 24584 | tf_op jit(solution)/shard_map/ppermute | solution.py:21
  45.0 3.7 %collective-permute-start.19 = (f32[8,256]{1,0:T(8,128)S(1)}, f32[8,256]{1,0:T(8,128)S(1)}, u32[]{:S(2)}, u32[]{:S(2)}) collective-permute-start(f32[8,256]{1,0:T(8,128)S(1)} %add_add_fusion), channel_id=1, source_target_pairs={{0,4},{4,0},{8,12},{12,8},{16,20},{20,16},{24,28},{28,24},{1,5},{5... | collective-permute-start | bytes 24584 | tf_op jit(solution)/shard_map/ppermute | solution.py:21
  48.6 3.7 %collective-permute-start.20 = (f32[16,256]{1,0:T(8,128)S(1)}, f32[16,256]{1,0:T(8,128)S(1)}, u32[]{:S(2)}, u32[]{:S(2)}) collective-permute-start(f32[16,256]{1,0:T(8,128)S(1)} %pad_maximum_fusion.2), channel_id=1, source_target_pairs={{0,8},{4,12},{8,0},{12,4},{16,24},{20,28},{24,16},{28,20},{1,9},{5... | collective-permute-start | bytes 49160 | tf_op jit(solution)/shard_map/ppermute | solution.py:21
  52.4 4.8 %collective-permute-start.21 = (f32[32,256]{1,0:T(8,128)S(1)}, f32[32,256]{1,0:T(8,128)S(1)}, u32[]{:S(2)}, u32[]{:S(2)}) collective-permute-start(f32[32,256]{1,0:T(8,128)S(1)} %pad_maximum_fusion.1.near_ref), channel_id=1, source_target_pairs={{0,16},{4,20},{8,24},{12,28},{16,0},{20,4},{24,8},{28,12},{1,17},{... | collective-permute-start | bytes 98312 | tf_op jit(solution)/shard_map/ppermute | solution.py:21
  (12 other events, 75.9 us)

commit v6 on v5

--- a/solution.py
+++ b/solution.py
@@ -84,15 +84,16 @@
         )
 
 
-def keyvalue_kernel(length, near_ref, far_ref, gain_ref, own_ref, near_scale_ref, near_sum_ref, *refs):
-    half_refs, (kv_ref, near_out, far_out, scale_ref, mean_ref) = refs[:-5], refs[-5:]
+def keyvalue_kernel(length, near_ref, far_ref, gain_ref, own_ref, near_scale_ref, near_sum_ref, query_ref, *refs):
+    half_refs, (kv_ref, q_ref, near_out, far_out, scale_ref, mean_ref) = refs[:-6], refs[-6:]
     slots, count, width = near_ref.shape
     rows = slots * count
     step = lane_step(width)
     parts = [own_ref[0], own_ref[1]]
     for here, there in zip(half_refs[::2], half_refs[1::2]):
         parts += [here[0], there[0], here[1], there[1]]
-    weights = jnp.concatenate(parts, axis=0)
+    lanes = kv_ref.shape[1]
+    weights = jnp.concatenate(parts + [query_ref[...]], axis=0)
     scale_ref[:rows, :] = near_scale_ref[...]
     for c, (x_ref, out_ref) in enumerate(((near_ref, near_out), (far_ref, far_out))):
         for s in range(slots):
@@ -112,9 +113,10 @@
                 scale_ref[at_row:at_row + count, :] = jnp.broadcast_to(
                     lax.rsqrt(mean + 1e-06), (count, scale_ref.shape[1])
                 )
-        kv = lax.dot_general(out_ref[...].reshape(rows, width), weights, NT, preferred_element_type=F32)
+        both = lax.dot_general(out_ref[...].reshape(rows, width), weights, NT, preferred_element_type=F32)
         span = slice(c * rows, (c + 1) * rows)
-        kv_ref[span, :] = (kv * scale_ref[span, :1]).astype(BF16)
+        kv_ref[span, :] = (both[:, :lanes] * scale_ref[span, :1]).astype(BF16)
+        q_ref[span, :] = (both[:, lanes:] * scale_ref[span, :]).astype(BF16)
 
 
 def half_query(x_ref, b_ref, c_ref, turn):
@@ -132,16 +134,14 @@
     )
 
 
-def query_kernel(order_ref, near_ref, far_ref, scale_ref, query_ref, *refs):
-    part_refs, (own_ref, *half_refs) = refs[:len(refs) // 3 * 2], refs[len(refs) // 3 * 2:]
-    slots, count, width = near_ref.shape
+def query_kernel(order_ref, near_ref, far_ref, *refs):
+    n = len(refs) // 3
+    part_refs, half_refs = refs[:2 * n], refs[2 * n:]
+    slots, count, _ = near_ref.shape
     rows = slots * count
     for c, x_ref in enumerate((near_ref, far_ref)):
-        span = slice(c * rows, (c + 1) * rows)
         for p, half_ref in enumerate(half_refs):
-            half_ref[span, :] = half_query(x_ref, part_refs[2 * p], part_refs[2 * p + 1], 0)
-        q = jnp.dot(x_ref[...].reshape(rows, width), query_ref[...], preferred_element_type=F32)
-        own_ref[span, :] = (q * scale_ref[span, :]).astype(BF16)
+            half_ref[c * rows:(c + 1) * rows, :] = half_query(x_ref, part_refs[2 * p], part_refs[2 * p + 1], 0)
 
 
 def product_kernel(masks, order_ref, output_ref, *refs):
@@ -323,6 +323,7 @@
     b_y = [flipped(b_part, "tp", m) for m in masks[1:]]
     c_y = [flipped(c_part, "tp", m) for m in masks[1:]]
 
+    query_turned = after(enc_query, (b_part, c_part)).T
     weights = []
     for w in kv_y:
         weights += [w, flipped(w, "rep", 1)]
@@ -339,21 +340,21 @@
         out_shape=out,
         compiler_params=room(tokens, enc_gain, kv_rows, *out),
     )(kv_y[0], tokens, enc_gain, kv_rows)
-    operands = (tokens, tokens_far, enc_gain, kv_rows, scale, sums, *weights)
+    operands = (tokens, tokens_far, enc_gain, kv_rows, scale, sums, query_turned, *weights)
     out = [
         jax.ShapeDtypeStruct((2 * rows, lanes), BF16),
+        jax.ShapeDtypeStruct((2 * rows, head_dim), BF16),
         jax.ShapeDtypeStruct(tokens.shape, BF16),
         jax.ShapeDtypeStruct(tokens.shape, BF16),
         jax.ShapeDtypeStruct((2 * rows, head_dim), F32),
         jax.ShapeDtypeStruct((slots, width), F32),
     ]
-    kv, near, far, scale, mean = pl.pallas_call(
+    kv, own, near, far, scale, mean = pl.pallas_call(
         functools.partial(keyvalue_kernel, length),
         out_shape=out,
         compiler_params=room(*operands, *out),
     )(*operands)
     kv_near = [kv] + [flipped(kv, "tp", m) for m in masks[1:]]
-    kv_far = [flipped(after(k, kv_near[1:]), "tp", 1) for k in kv_near]
 
     proj_near = [after(p, weights[-1]) for p in proj_near]
     proj_all = proj_near + [flipped(p, "tp", 1) for p in proj_near]
@@ -401,10 +402,9 @@
         parts += [q_b, q_c]
         b_rest.append(flipped(q_b, "rep", 1))
         c_rest.append(flipped(q_c, "rep", 2))
-    operands = (near, far, scale, enc_query, *parts)
-    out = [jax.ShapeDtypeStruct((2 * rows, head_dim), BF16)]
-    out += [jax.ShapeDtypeStruct((2 * rows, head_dim), F32) for _ in masks[1:]]
-    own, *early = pl.pallas_call(
+    operands = (near, far, *parts)
+    out = [jax.ShapeDtypeStruct((2 * rows, head_dim), F32) for _ in masks[1:]]
+    early = pl.pallas_call(
         query_kernel,
         in_specs=[pl.BlockSpec(memory_space=pl.ANY)]
         + [pl.BlockSpec(memory_space=pltpu.VMEM)] * len(operands),
@@ -412,6 +412,7 @@
         compiler_params=room(*operands, *out),
     )(w2_all[1], *operands)
 
+    kv_far = [flipped(after(k, (kv_near[1:], early, w2_all[-1])), "tp", 1) for k in kv_near]
     n = len(masks)
     groups = n_tp // group
     operands = (

time: 58.9 us -> 58.3 us (0.990)
  Pallas kernels: 13.4 us -> 11.4 us
  local copies, waits for them, and re-layouts: 6.99 us -> 8.25 us
  waiting for transfers between devices: 12.6 us -> 13.6 us
  starting transfers between devices: 23.8 us -> 22.9 us
    pallas_call x1, Pallas kernels: 3.02 us -> 1.13 us  [local(): pl.pallas_call(query_kernel, in_specs=[pl.BlockSpec(memory_space=pl.ANY)]...]
    unnamed x28 -> x22, local copies, waits for them, and re-layouts: 3.83 us -> 2.08 us
    dynamic_slice x3, local copies, waits for them, and re-layouts: 2.99 us -> 4.54 us  [cut(): return lax.dynamic_slice_in_dim(array, at * size, size, axis=axis)]
    optimization_barrier x0 -> x1, local copies, waits for them, and re-layouts: none -> 1.46 us  [after(): return lax.optimization_barrier((value, earlier))[0]]
    ppermute x22, waiting for transfers between devices: 12.6 us -> 13.6 us  [flipped(): return lax.ppermute(block, axis, [(i, i ^ mask) for i in range(count)])]
    ppermute x22, starting transfers between devices: 23.8 us -> 22.9 us  [flipped(): return lax.ppermute(block, axis, [(i, i ^ mask) for i in range(count)])]
  transfers between devices with their start and end apart: 22 -> 22, of which waited for: 9 -> 9; matrix products, arithmetic and copies ran while one was open for 8% -> 13% of each run, Pallas kernels for 16% -> 13%
where the time goes in v6:
time: 58.3 us; the launch traced here: 58 us
  starting transfers between devices  22.9 us (39%)
  waiting for transfers between devices  13.6 us (23%)
  Pallas kernels  11.4 us (20%)
  local copies, waits for them, and re-layouts  8.25 us (14%)
  other arithmetic  1.27 us (2%)
    ppermute x22, starting transfers between devices, flipped(): return lax.ppermute(block, axis, [(i, i ^ mask) for i in range(count)])  22.9 us
    ppermute x22, waiting for transfers between devices, flipped(): return lax.ppermute(block, axis, [(i, i ^ mask) for i in range(count)])  13.6 us
    pallas_call x1, Pallas kernels, local(): pl.pallas_call(functools.partial(keyvalue_kernel, length), out_shape=out,...  4.89 us
    dynamic_slice x3, local copies, waits for them, and re-layouts, cut(): return lax.dynamic_slice_in_dim(array, at * size, size, axis=axis)  4.54 us
    pallas_call x1, Pallas kernels, local(): pl.pallas_call(functools.partial(attention_kernel, masks, group, length),...  2.49 us
    unnamed x22, local copies, waits for them, and re-layouts  2.08 us
    optimization_barrier x1, local copies, waits for them, and re-layouts, after(): return lax.optimization_barrier((value, earlier))[0]  1.46 us
    pallas_call x1, Pallas kernels, local(): pl.pallas_call(document_kernel, out_shape=jax.ShapeDtypeStruct((OWN_DOCS,...  1.37 us
  transfers between devices with their start and end apart: 22, of which 9 were waited for; matrix products, arithmetic and copies ran while one was open for 13% of the time, Pallas kernels for 13%

profile of v6, /device:TPU:0, one launch (start us, length us, event | category | flops | bytes accessed | tf_op | source)
XLA Modules:
  0.0 58.0 jit_solution(6866954860697183001)
XLA Ops:
  0.5 1.6 %dynamic-slice_bitcast_fusion.4 = bf16[2,16,3584]{2,1,0:T(8,128)(2,1)} fusion(bf16[3584,2,32]{0,2,1:T(8,128)(2,1)} %param.17, s32[]{:T(128)S(6)} %select_n.253), kind=kLoop, calls=%fused_computation.8 | loop fusion | bytes 458756 | tf_op jit(solution)/shard_map/dynamic_slice | solution.py:29
  2.1 2.6 %collective-permute-start.1 = (bf16[2,16,3584]{2,1,0:T(8,128)(2,1)}, bf16[2,16,3584]{2,1,0:T(8,128)(2,1)S(1)}, u32[]{:S(2)}, u32[]{:S(2)}) collective-permute-start(bf16[2,16,3584]{2,1,0:T(8,128)(2,1)} %dynamic-slice_bitcast_fusion.4), channel_id=1, source_target_pairs={{0,2},{1,3},{2,0},{3,1},{4,6},{5,7},{6,4},{7,5},{8,10},{9,11},{10,... | collective-permute-start | bytes 688136 | tf_op jit(solution)/shard_map/ppermute | solution.py:21
  5.8 1.9 %constant_dynamic-slice_fusion = (bf16[896,128]{1,0:T(8,128)(2,1)}, bf16[896,128]{1,0:T(8,128)(2,1)}) fusion(bf16[3584,128]{1,0:T(8,128)(2,1)} %param.16, s32[]{:T(128)S(6)} %select_n.258, s32[]{:T(128)S(6)} %select_n.255), kind=kLoop, calls=%fused_computation.38 | loop fusion | bytes 917512 | tf_op jit(solution)/shard_map/dynamic_slice | solution.py:29
  7.7 2.0 %collective-permute-start.7 = (bf16[896,128]{1,0:T(8,128)(2,1)}, bf16[896,128]{1,0:T(8,128)(2,1)S(1)}, u32[]{:S(2)}, u32[]{:S(2)}) collective-permute-start(bf16[896,128]{1,0:T(8,128)(2,1)} %get-tuple-element.59), channel_id=1, source_target_pairs={{0,2},{1,3},{2,0},{3,1},{4,6},{5,7},{6,4},{7,5},{8,10},{9,11},{10,... | collective-permute-start | bytes 688136 | tf_op jit(solution)/shard_map/ppermute | solution.py:21
  9.9 1.5 %copy.14 = bf16[3584,128]{0,1:T(8,128)(2,1)S(1)} copy(bf16[3584,128]{1,0:T(8,128)(2,1)} %param.16) | data formatting | bytes 1835008 | tf_op jit(solution)/shard_map/optimization_barrier | solution.py:25
  11.6 2.0 %collective-permute-start.2 = (bf16[2,16,3584]{2,1,0:T(8,128)(2,1)S(1)}, bf16[2,16,3584]{2,1,0:T(8,128)(2,1)S(1)}, u32[]{:S(2)}, u32[]{:S(2)}) collective-permute-start(bf16[2,16,3584]{2,1,0:T(8,128)(2,1)S(1)} %collective-permute-done.1.order_ref.refs_0_), channel_id=1, source_target_pairs={{0,4},{4,0},{8,12},{12,8},{16,20},{20,16},{24,28},{28,24},{1,5},{5... | collective-permute-start | bytes 688136 | tf_op jit(solution)/shard_map/ppermute | solution.py:21
  13.6 2.0 %copy-done = bf16[8,64,3584]{2,1,0:T(8,128)(2,1)S(1)} copy-done((bf16[8,64,3584]{2,1,0:T(8,128)(2,1)S(1)}, bf16[8,64,3584]{2,1,0:T(8,128)(2,1)}, u32[]{:S(2)}) %copy-start) | copy-done | bytes 3670040
  15.7 1.2 %shard_map.109 = (f32[512,128]{1,0:T(8,128)S(1)}, f32[8,3584]{1,0:T(8,128)S(1)}) custom-call(bf16[2,16,3584]{2,1,0:T(8,128)(2,1)S(1)} %collective-permute-done.1.order_ref.refs_0_, bf16[8,64,3584]{2,1,0:T(8,128)(2,1)S(1)} %copy-done, f32[3584]{0:T(1024)S(1)} %copy-done.5, bf16[2,32,3584]{2,1,0:T(8,128)(2,1)S(1)} %bitcast.29), custom_call_target="tpu_custom_call" | custom-call | tf_op jit(solution)/shard_map/pallas_call | solution.py:337
  16.8 1.9 %collective-permute-done.2.refs_1_ = bf16[2,16,3584]{2,1,0:T(8,128)(2,1)S(1)} collective-permute-done((bf16[2,16,3584]{2,1,0:T(8,128)(2,1)S(1)}, bf16[2,16,3584]{2,1,0:T(8,128)(2,1)S(1)}, u32[]{:S(2)}, u32[]{:S(2)}) %collective-permute-start.2) | collective-permute-done | bytes 229408 | tf_op jit(solution)/shard_map/ppermute | solution.py:21
  19.5 4.9 %shard_map.110 = (bf16[1024,128]{1,0:T(8,128)(2,1)S(1)}, bf16[1024,128]{1,0:T(8,128)(2,1)S(1)}, bf16[8,64,3584]{2,1,0:T(8,128)(2,1)S(1)}, bf16[8,64,3584]{2,1,0:...) custom-call(bf16[8,64,3584]{2,1,0:T(8,128)(2,1)S(1)} %copy-done.1, ...), custom_call_target="tpu_custom_call" | custom-call | tf_op jit(solution)/shard_map/pallas_call | solution.py:352
  24.4 1.7 %collective-permute-start.11 = (bf16[1024,128]{1,0:T(8,128)(2,1)S(1)}, bf16[1024,128]{1,0:T(8,128)(2,1)S(1)}, u32[]{:S(2)}, u32[]{:S(2)}) collective-permute-start(bf16[1024,128]{1,0:T(8,128)(2,1)S(1)} %get-tuple-element.45.order_ref.refs_7_), channel_id=1, source_target_pairs={{0,2},{1,3},{2,0},{3,1},{4,6},{5,7},{6,4},{7,5},{8,10},{9,11},{10,... | collective-permute-start | bytes 786440 | tf_op jit(solution)/shard_map/ppermute | solution.py:21
  26.9 1.6 %collective-permute-start.6 = (bf16[128,128]{1,0:T(8,128)(2,1)S(1)}, bf16[128,128]{1,0:T(8,128)(2,1)S(1)}, u32[]{:S(2)}, u32[]{:S(2)}) collective-permute-start(bf16[128,128]{1,0:T(8,128)(2,1)S(1)} %get-tuple-element.42.refs_11_), channel_id=1, source_target_pairs={{0,4},{4,0},{8,12},{12,8},{16,20},{20,16},{24,28},{28,24},{1,5},{5... | collective-permute-start | bytes 98312 | tf_op jit(solution)/shard_map/ppermute | solution.py:21
  28.5 1.6 %collective-permute-start.10 = (bf16[896,128]{1,0:T(8,128)(2,1)S(1)}, bf16[896,128]{1,0:T(8,128)(2,1)S(1)}, u32[]{:S(2)}, u32[]{:S(2)}) collective-permute-start(bf16[896,128]{1,0:T(8,128)(2,1)S(1)} %collective-permute-done.8.refs_1_), channel_id=1, source_target_pairs={{0,8},{4,12},{8,0},{12,4},{16,24},{20,28},{24,16},{28,20},{1,9},{5... | collective-permute-start | bytes 688136 | tf_op jit(solution)/shard_map/ppermute | solution.py:21
  30.6 1.3 %collective-permute-start.15 = (bf16[240,128]{1,0:T(8,128)(2,1)S(1)}, bf16[240,128]{1,0:T(8,128)(2,1)S(1)}, u32[]{:S(2)}, u32[]{:S(2)}) collective-permute-start(bf16[240,128]{1,0:T(8,128)(2,1)S(1)} %get-tuple-element.47), channel_id=1, source_target_pairs={{0,2},{1,3},{2,0},{3,1},{4,6},{5,7},{6,4},{7,5},{8,10},{9,11},{10,... | collective-permute-start | bytes 184328 | tf_op jit(solution)/shard_map/ppermute | solution.py:21
  33.9 2.0 %collective-permute-done.12.refs_14_ = bf16[128,128]{1,0:T(8,128)(2,1)S(1)} collective-permute-done((bf16[128,128]{1,0:T(8,128)(2,1)S(1)}, bf16[128,128]{1,0:T(8,128)(2,1)S(1)}, u32[]{:S(2)}, u32[]{:S(2)}) %collective-permute-start.12) | collective-permute-done | bytes 32800 | tf_op jit(solution)/shard_map/ppermute | solution.py:21
  37.9 2.5 %shard_map.113 = f32[8,256]{1,0:T(8,128)S(1)} custom-call(bf16[8,64,3584]{2,1,0:T(8,128)(2,1)S(1)} %get-tuple-element.33.near_ref.refs_0_, bf16[8,64,3584]{2,1,0:T(8,128)(2,1)S(1)} %get-tuple-element.34.far_ref.refs_1_, f32[1024,128]{1,0:T(8,128)S(1)} %get-tuple-element.35.refs_2_, bf16[1024,128]{1,0:T(8,128)(2,1)S(1)} %get-tuple-element.36.refs_3_, ...), custom_call_target="tpu_custom_call" | custom-call | tf_op jit(solution)/shard_map/pallas_call | solution.py:441
  42.5 1.7 %collective-permute-done.17 = f32[8,256]{1,0:T(8,128)S(1)} collective-permute-done((f32[8,256]{1,0:T(8,128)S(1)}, f32[8,256]{1,0:T(8,128)S(1)}, u32[]{:S(2)}, u32[]{:S(2)}) %collective-permute-start.17) | collective-permute-done | bytes 8224 | tf_op jit(solution)/shard_map/ppermute | solution.py:21
  44.4 1.5 %collective-permute-start.19 = (f32[8,256]{1,0:T(8,128)S(1)}, f32[8,256]{1,0:T(8,128)S(1)}, u32[]{:S(2)}, u32[]{:S(2)}) collective-permute-start(f32[8,256]{1,0:T(8,128)S(1)} %add_add_fusion), channel_id=1, source_target_pairs={{0,4},{4,0},{8,12},{12,8},{16,20},{20,16},{24,28},{28,24},{1,5},{5... | collective-permute-start | bytes 24584 | tf_op jit(solution)/shard_map/ppermute | solution.py:21
  46.1 2.0 %collective-permute-done.19 = f32[8,256]{1,0:T(8,128)S(1)} collective-permute-done((f32[8,256]{1,0:T(8,128)S(1)}, f32[8,256]{1,0:T(8,128)S(1)}, u32[]{:S(2)}, u32[]{:S(2)}) %collective-permute-start.19) | collective-permute-done | bytes 8224 | tf_op jit(solution)/shard_map/ppermute | solution.py:21
  48.1 1.3 %collective-permute-start.20 = (f32[16,256]{1,0:T(8,128)S(1)}, f32[16,256]{1,0:T(8,128)S(1)}, u32[]{:S(2)}, u32[]{:S(2)}) collective-permute-start(f32[16,256]{1,0:T(8,128)S(1)} %pad_maximum_fusion.2), channel_id=1, source_target_pairs={{0,8},{4,12},{8,0},{12,4},{16,24},{20,28},{24,16},{28,20},{1,9},{5... | collective-permute-start | bytes 49160 | tf_op jit(solution)/shard_map/ppermute | solution.py:21
  49.3 2.5 %collective-permute-done.20 = f32[16,256]{1,0:T(8,128)S(1)} collective-permute-done((f32[16,256]{1,0:T(8,128)S(1)}, f32[16,256]{1,0:T(8,128)S(1)}, u32[]{:S(2)}, u32[]{:S(2)}) %collective-permute-start.20) | collective-permute-done | bytes 16416 | tf_op jit(solution)/shard_map/ppermute | solution.py:21
  51.8 2.6 %collective-permute-start.21 = (f32[32,256]{1,0:T(8,128)S(1)}, f32[32,256]{1,0:T(8,128)S(1)}, u32[]{:S(2)}, u32[]{:S(2)}) collective-permute-start(f32[32,256]{1,0:T(8,128)S(1)} %pad_maximum_fusion.1.near_ref), channel_id=1, source_target_pairs={{0,16},{4,20},{8,24},{12,28},{16,0},{20,4},{24,8},{28,12},{1,17},{... | collective-permute-start | bytes 98312 | tf_op jit(solution)/shard_map/ppermute | solution.py:21
  54.6 2.1 %collective-permute-done.21.far_ref = f32[32,256]{1,0:T(8,128)S(1)} collective-permute-done((f32[32,256]{1,0:T(8,128)S(1)}, f32[32,256]{1,0:T(8,128)S(1)}, u32[]{:S(2)}, u32[]{:S(2)}) %collective-permute-start.21) | collective-permute-done | bytes 32800 | tf_op jit(solution)/shard_map/ppermute | solution.py:21
  56.6 1.4 %shard_map.114 = bf16[4,4,64]{2,1,0:T(4,128)(2,1)} custom-call(f32[32,256]{1,0:T(8,128)S(1)} %pad_maximum_fusion.1.near_ref, f32[32,256]{1,0:T(8,128)S(1)} %collective-permute-done.21.far_ref, f32[16,64]{1,0:T(8,128)S(1)} %fusion.1.select_ref, f32[16,16]{1,0:T(8,128)S(1)} %fusion.8.allow_ref, f32[16,1]{1,0:T(8,128)S(1)} %copy.15.fill_ref, ...), custom_call_target="tpu_custom_call" | custom-call | tf_op jit(solution)/shard_map/pallas_call | solution.py:482
  (75 shorter events, 10.4 us)
Async XLA Ops:
  0.0 19.5 %collective-permute-start = (bf16[8,64,3584]{2,1,0:T(8,128)(2,1)}, bf16[8,64,3584]{2,1,0:T(8,128)(2,1)}, u32[]{:S(2)}, u32[]{:S(2)}) collective-permute-start(bf16[8,64,3584]{2,1,0:T(8,128)(2,1)} %near_ref.1), channel_id=1, source_target_pairs={{0,1},{1,0},{2,3},{3,2},{4,5},{5,4},{6,7},{7,6},{8,9},{9,8},{10,11... | collective-permute-start | bytes 11010056 | tf_op jit(solution)/shard_map/ppermute | solution.py:21
  2.1 9.4 %collective-permute-start.1 = (bf16[2,16,3584]{2,1,0:T(8,128)(2,1)}, bf16[2,16,3584]{2,1,0:T(8,128)(2,1)S(1)}, u32[]{:S(2)}, u32[]{:S(2)}) collective-permute-start(bf16[2,16,3584]{2,1,0:T(8,128)(2,1)} %dynamic-slice_bitcast_fusion.4), channel_id=1, source_target_pairs={{0,2},{1,3},{2,0},{3,1},{4,6},{5,7},{6,4},{7,5},{8,10},{9,11},{10,... | collective-permute-start | bytes 688136 | tf_op jit(solution)/shard_map/ppermute | solution.py:21
  5.7 13.1 %collective-permute-start.3 = (bf16[896,128]{1,0:T(8,128)(2,1)S(1)}, bf16[896,128]{1,0:T(8,128)(2,1)S(1)}, u32[]{:S(2)}, u32[]{:S(2)}) collective-permute-start(bf16[896,128]{1,0:T(8,128)(2,1)S(1)} %constant_dynamic-slice_fusion.2.refs_0_), channel_id=1, source_target_pairs={{0,2},{1,3},{2,0},{3,1},{4,6},{5,7},{6,4},{7,5},{8,10},{9,11},{10,... | collective-permute-start | bytes 688136 | tf_op jit(solution)/shard_map/ppermute | solution.py:21
  7.7 18.5 %collective-permute-start.7 = (bf16[896,128]{1,0:T(8,128)(2,1)}, bf16[896,128]{1,0:T(8,128)(2,1)S(1)}, u32[]{:S(2)}, u32[]{:S(2)}) collective-permute-start(bf16[896,128]{1,0:T(8,128)(2,1)} %get-tuple-element.59), channel_id=1, source_target_pairs={{0,2},{1,3},{2,0},{3,1},{4,6},{5,7},{6,4},{7,5},{8,10},{9,11},{10,... | collective-permute-start | bytes 688136 | tf_op jit(solution)/shard_map/ppermute | solution.py:21
  9.7 16.6 %collective-permute-start.8 = (bf16[896,128]{1,0:T(8,128)(2,1)}, bf16[896,128]{1,0:T(8,128)(2,1)S(1)}, u32[]{:S(2)}, u32[]{:S(2)}) collective-permute-start(bf16[896,128]{1,0:T(8,128)(2,1)} %get-tuple-element.58), channel_id=1, source_target_pairs={{0,2},{1,3},{2,0},{3,1},{4,6},{5,7},{6,4},{7,5},{8,10},{9,11},{10,... | collective-permute-start | bytes 688136 | tf_op jit(solution)/shard_map/ppermute | solution.py:21
  11.6 7.2 %collective-permute-start.2 = (bf16[2,16,3584]{2,1,0:T(8,128)(2,1)S(1)}, bf16[2,16,3584]{2,1,0:T(8,128)(2,1)S(1)}, u32[]{:S(2)}, u32[]{:S(2)}) collective-permute-start(bf16[2,16,3584]{2,1,0:T(8,128)(2,1)S(1)} %collective-permute-done.1.order_ref.refs_0_), channel_id=1, source_target_pairs={{0,4},{4,0},{8,12},{12,8},{16,20},{20,16},{24,28},{28,24},{1,5},{5... | collective-permute-start | bytes 688136 | tf_op jit(solution)/shard_map/ppermute | solution.py:21
  18.7 7.8 %collective-permute-start.5 = (bf16[896,128]{1,0:T(8,128)(2,1)S(1)}, bf16[896,128]{1,0:T(8,128)(2,1)S(1)}, u32[]{:S(2)}, u32[]{:S(2)}) collective-permute-start(bf16[896,128]{1,0:T(8,128)(2,1)S(1)} %collective-permute-done.3.refs_1_), channel_id=1, source_target_pairs={{0,1},{1,0},{2,3},{3,2},{4,5},{5,4},{6,7},{7,6},{8,9},{9,8},{10,11... | collective-permute-start | bytes 688136 | tf_op jit(solution)/shard_map/ppermute | solution.py:21
  18.7 7.8 %collective-permute-start.4 = (bf16[896,128]{1,0:T(8,128)(2,1)S(1)}, bf16[896,128]{1,0:T(8,128)(2,1)S(1)}, u32[]{:S(2)}, u32[]{:S(2)}) collective-permute-start(bf16[896,128]{1,0:T(8,128)(2,1)S(1)} %constant_dynamic-slice_fusion.2.refs_0_), channel_id=1, source_target_pairs={{0,1},{1,0},{2,3},{3,2},{4,5},{5,4},{6,7},{7,6},{8,9},{9,8},{10,11... | collective-permute-start | bytes 688136 | tf_op jit(solution)/shard_map/ppermute | solution.py:21
  24.4 11.6 %collective-permute-start.11 = (bf16[1024,128]{1,0:T(8,128)(2,1)S(1)}, bf16[1024,128]{1,0:T(8,128)(2,1)S(1)}, u32[]{:S(2)}, u32[]{:S(2)}) collective-permute-start(bf16[1024,128]{1,0:T(8,128)(2,1)S(1)} %get-tuple-element.45.order_ref.refs_7_), channel_id=1, source_target_pairs={{0,2},{1,3},{2,0},{3,1},{4,6},{5,7},{6,4},{7,5},{8,10},{9,11},{10,... | collective-permute-start | bytes 786440 | tf_op jit(solution)/shard_map/ppermute | solution.py:21
  26.9 5.1 %collective-permute-start.6 = (bf16[128,128]{1,0:T(8,128)(2,1)S(1)}, bf16[128,128]{1,0:T(8,128)(2,1)S(1)}, u32[]{:S(2)}, u32[]{:S(2)}) collective-permute-start(bf16[128,128]{1,0:T(8,128)(2,1)S(1)} %get-tuple-element.42.refs_11_), channel_id=1, source_target_pairs={{0,4},{4,0},{8,12},{12,8},{16,20},{20,16},{24,28},{28,24},{1,5},{5... | collective-permute-start | bytes 98312 | tf_op jit(solution)/shard_map/ppermute | solution.py:21
  28.5 8.2 %collective-permute-start.10 = (bf16[896,128]{1,0:T(8,128)(2,1)S(1)}, bf16[896,128]{1,0:T(8,128)(2,1)S(1)}, u32[]{:S(2)}, u32[]{:S(2)}) collective-permute-start(bf16[896,128]{1,0:T(8,128)(2,1)S(1)} %collective-permute-done.8.refs_1_), channel_id=1, source_target_pairs={{0,8},{4,12},{8,0},{12,4},{16,24},{20,28},{24,16},{28,20},{1,9},{5... | collective-permute-start | bytes 688136 | tf_op jit(solution)/shard_map/ppermute | solution.py:21
  30.1 6.7 %collective-permute-start.9 = (bf16[896,128]{1,0:T(8,128)(2,1)S(1)}, bf16[896,128]{1,0:T(8,128)(2,1)S(1)}, u32[]{:S(2)}, u32[]{:S(2)}) collective-permute-start(bf16[896,128]{1,0:T(8,128)(2,1)S(1)} %collective-permute-done.7.refs_0_), channel_id=1, source_target_pairs={{0,4},{4,0},{8,12},{12,8},{16,20},{20,16},{24,28},{28,24},{1,5},{5... | collective-permute-start | bytes 688136 | tf_op jit(solution)/shard_map/ppermute | solution.py:21
  30.6 6.1 %collective-permute-start.15 = (bf16[240,128]{1,0:T(8,128)(2,1)S(1)}, bf16[240,128]{1,0:T(8,128)(2,1)S(1)}, u32[]{:S(2)}, u32[]{:S(2)}) collective-permute-start(bf16[240,128]{1,0:T(8,128)(2,1)S(1)} %get-tuple-element.47), channel_id=1, source_target_pairs={{0,2},{1,3},{2,0},{3,1},{4,6},{5,7},{6,4},{7,5},{8,10},{9,11},{10,... | collective-permute-start | bytes 184328 | tf_op jit(solution)/shard_map/ppermute | solution.py:21
  32.0 4.0 %collective-permute-start.12 = (bf16[128,128]{1,0:T(8,128)(2,1)S(1)}, bf16[128,128]{1,0:T(8,128)(2,1)S(1)}, u32[]{:S(2)}, u32[]{:S(2)}) collective-permute-start(bf16[128,128]{1,0:T(8,128)(2,1)S(1)} %collective-permute-done.6.order_ref.refs_12_), channel_id=1, source_target_pairs={{0,2},{1,3},{2,0},{3,1},{4,6},{5,7},{6,4},{7,5},{8,10},{9,11},{10,... | collective-permute-start | bytes 98312 | tf_op jit(solution)/shard_map/ppermute | solution.py:21
  36.0 1.5 %collective-permute-start.14 = (bf16[1024,128]{1,0:T(8,128)(2,1)S(1)}, bf16[1024,128]{1,0:T(8,128)(2,1)S(1)}, u32[]{:S(2)}, u32[]{:S(2)}) collective-permute-start(bf16[1024,128]{1,0:T(8,128)(2,1)S(1)} %collective-permute-done.11.refs_8_), channel_id=1, source_target_pairs={{0,1},{1,0},{2,3},{3,2},{4,5},{5,4},{6,7},{7,6},{8,9},{9,8},{10,11... | collective-permute-start | bytes 786440 | tf_op jit(solution)/shard_map/ppermute | solution.py:21
  36.0 1.9 %collective-permute-start.13 = (bf16[1024,128]{1,0:T(8,128)(2,1)S(1)}, bf16[1024,128]{1,0:T(8,128)(2,1)S(1)}, u32[]{:S(2)}, u32[]{:S(2)}) collective-permute-start(bf16[1024,128]{1,0:T(8,128)(2,1)S(1)} %get-tuple-element.45.order_ref.refs_7_), channel_id=1, source_target_pairs={{0,1},{1,0},{2,3},{3,2},{4,5},{5,4},{6,7},{7,6},{8,9},{9,8},{10,11... | collective-permute-start | bytes 786440 | tf_op jit(solution)/shard_map/ppermute | solution.py:21
  37.9 18.7 %copy-start.4 = (bf16[256,3,64]{0,2,1:T(8,128)(2,1)S(1)}, bf16[256,3,64]{0,2,1:T(8,128)(2,1)}, u32[]{:S(2)}) copy-start(bf16[256,3,64]{0,2,1:T(8,128)(2,1)} %param.21) | copy-start | bytes 294916
  37.9 18.7 %copy-start.6 = (f32[256]{0:T(256)S(1)}, f32[256]{0:T(256)}, u32[]{:S(2)}) copy-start(f32[256]{0:T(256)} %param.20) | copy-start | bytes 3076
  40.4 2.1 %collective-permute-start.16 = (f32[8,256]{1,0:T(8,128)S(1)}, f32[8,256]{1,0:T(8,128)S(1)}, u32[]{:S(2)}, u32[]{:S(2)}) collective-permute-start(f32[8,256]{1,0:T(8,128)S(1)} %shard_map.113), channel_id=1, source_target_pairs={{0,1},{1,0},{2,3},{3,2},{4,5},{5,4},{6,7},{7,6},{8,9},{9,8},{10,11... | collective-permute-start | bytes 24584 | tf_op jit(solution)/shard_map/ppermute | solution.py:21
  40.6 3.7 %collective-permute-start.17 = (f32[8,256]{1,0:T(8,128)S(1)}, f32[8,256]{1,0:T(8,128)S(1)}, u32[]{:S(2)}, u32[]{:S(2)}) collective-permute-start(f32[8,256]{1,0:T(8,128)S(1)} %shard_map.113), channel_id=1, source_target_pairs={{0,2},{1,3},{2,0},{3,1},{4,6},{5,7},{6,4},{7,5},{8,10},{9,11},{10,... | collective-permute-start | bytes 24584 | tf_op jit(solution)/shard_map/ppermute | solution.py:21
  41.3 3.1 %collective-permute-start.18 = (f32[8,256]{1,0:T(8,128)S(1)}, f32[8,256]{1,0:T(8,128)S(1)}, u32[]{:S(2)}, u32[]{:S(2)}) collective-permute-start(f32[8,256]{1,0:T(8,128)S(1)} %shard_map.113), channel_id=1, source_target_pairs={{0,3},{1,2},{2,1},{3,0},{4,7},{5,6},{6,5},{7,4},{8,11},{9,10},{10,... | collective-permute-start | bytes 24584 | tf_op jit(solution)/shard_map/ppermute | solution.py:21
  44.4 3.7 %collective-permute-start.19 = (f32[8,256]{1,0:T(8,128)S(1)}, f32[8,256]{1,0:T(8,128)S(1)}, u32[]{:S(2)}, u32[]{:S(2)}) collective-permute-start(f32[8,256]{1,0:T(8,128)S(1)} %add_add_fusion), channel_id=1, source_target_pairs={{0,4},{4,0},{8,12},{12,8},{16,20},{20,16},{24,28},{28,24},{1,5},{5... | collective-permute-start | bytes 24584 | tf_op jit(solution)/shard_map/ppermute | solution.py:21
  48.1 3.7 %collective-permute-start.20 = (f32[16,256]{1,0:T(8,128)S(1)}, f32[16,256]{1,0:T(8,128)S(1)}, u32[]{:S(2)}, u32[]{:S(2)}) collective-permute-start(f32[16,256]{1,0:T(8,128)S(1)} %pad_maximum_fusion.2), channel_id=1, source_target_pairs={{0,8},{4,12},{8,0},{12,4},{16,24},{20,28},{24,16},{28,20},{1,9},{5... | collective-permute-start | bytes 49160 | tf_op jit(solution)/shard_map/ppermute | solution.py:21
  51.8 4.8 %collective-permute-start.21 = (f32[32,256]{1,0:T(8,128)S(1)}, f32[32,256]{1,0:T(8,128)S(1)}, u32[]{:S(2)}, u32[]{:S(2)}) collective-permute-start(f32[32,256]{1,0:T(8,128)S(1)} %pad_maximum_fusion.1.near_ref), channel_id=1, source_target_pairs={{0,16},{4,20},{8,24},{12,28},{16,0},{20,4},{24,8},{28,12},{1,17},{... | collective-permute-start | bytes 98312 | tf_op jit(solution)/shard_map/ppermute | solution.py:21
  (9 other events, 68.8 us)

commit v7 on v6

--- a/solution.py
+++ b/solution.py
@@ -323,7 +323,7 @@
     b_y = [flipped(b_part, "tp", m) for m in masks[1:]]
     c_y = [flipped(c_part, "tp", m) for m in masks[1:]]
 
-    query_turned = after(enc_query, (b_part, c_part)).T
+    query_turned = after(enc_query, (b_part, c_part, kv_y[0])).T
     weights = []
     for w in kv_y:
         weights += [w, flipped(w, "rep", 1)]
@@ -339,7 +339,7 @@
         in_specs=[pl.BlockSpec(memory_space=pl.ANY)] + [pl.BlockSpec(memory_space=pltpu.VMEM)] * 3,
         out_shape=out,
         compiler_params=room(tokens, enc_gain, kv_rows, *out),
-    )(kv_y[0], tokens, enc_gain, kv_rows)
+    )(query_turned, tokens, enc_gain, kv_rows)
     operands = (tokens, tokens_far, enc_gain, kv_rows, scale, sums, query_turned, *weights)
     out = [
         jax.ShapeDtypeStruct((2 * rows, lanes), BF16),

time: 58.3 us -> 57.3 us (0.983)
  local copies, waits for them, and re-layouts: 8.25 us -> 6.7 us
    dynamic_slice x3, local copies, waits for them, and re-layouts: 4.54 us -> 2.99 us  [cut(): return lax.dynamic_slice_in_dim(array, at * size, size, axis=axis)]
  transfers between devices with their start and end apart: 22 -> 22, of which waited for: 9 -> 9; matrix products, arithmetic and copies ran while one was open for 13% -> 11% of each run, Pallas kernels for 13% -> 13%
where the time goes in v7:
time: 57.3 us; the launch traced here: 57.1 us
  starting transfers between devices  23.2 us (40%)
  waiting for transfers between devices  14 us (24%)
  Pallas kernels  11.4 us (20%)
  local copies, waits for them, and re-layouts  6.7 us (12%)
  other arithmetic  1.27 us (2%)
    ppermute x22, starting transfers between devices, flipped(): return lax.ppermute(block, axis, [(i, i ^ mask) for i in range(count)])  23.2 us
    ppermute x22, waiting for transfers between devices, flipped(): return lax.ppermute(block, axis, [(i, i ^ mask) for i in range(count)])  14 us
    pallas_call x1, Pallas kernels, local(): pl.pallas_call(functools.partial(keyvalue_kernel, length), out_shape=out,...  4.89 us
    dynamic_slice x3, local copies, waits for them, and re-layouts, cut(): return lax.dynamic_slice_in_dim(array, at * size, size, axis=axis)  2.99 us
    pallas_call x1, Pallas kernels, local(): pl.pallas_call(functools.partial(attention_kernel, masks, group, length),...  2.47 us
    unnamed x22, local copies, waits for them, and re-layouts  2.08 us
    optimization_barrier x1, local copies, waits for them, and re-layouts, after(): return lax.optimization_barrier((value, earlier))[0]  1.46 us
    pallas_call x1, Pallas kernels, local(): pl.pallas_call(document_kernel, out_shape=jax.ShapeDtypeStruct((OWN_DOCS,...  1.37 us
  transfers between devices with their start and end apart: 22, of which 9 were waited for; matrix products, arithmetic and copies ran while one was open for 11% of the time, Pallas kernels for 13%

profile of v7, /device:TPU:0, one launch (start us, length us, event | category | flops | bytes accessed | tf_op | source)
XLA Modules:
  0.0 57.1 jit_solution(11238240002204077658)
XLA Ops:
  1.4 2.7 %collective-permute-start.1 = (bf16[2,16,3584]{2,1,0:T(8,128)(2,1)S(1)}, bf16[2,16,3584]{2,1,0:T(8,128)(2,1)S(1)}, u32[]{:S(2)}, u32[]{:S(2)}) collective-permute-start(bf16[2,16,3584]{2,1,0:T(8,128)(2,1)S(1)} %dynamic-slice_bitcast_fusion.4), channel_id=1, source_target_pairs={{0,2},{1,3},{2,0},{3,1},{4,6},{5,7},{6,4},{7,5},{8,10},{9,11},{10,... | collective-permute-start | bytes 688136 | tf_op jit(solution)/shard_map/ppermute | solution.py:21
  6.2 2.0 %collective-permute-start.7 = (bf16[896,128]{1,0:T(8,128)(2,1)S(1)}, bf16[896,128]{1,0:T(8,128)(2,1)S(1)}, u32[]{:S(2)}, u32[]{:S(2)}) collective-permute-start(bf16[896,128]{1,0:T(8,128)(2,1)S(1)} %get-tuple-element.59), channel_id=1, source_target_pairs={{0,2},{1,3},{2,0},{3,1},{4,6},{5,7},{6,4},{7,5},{8,10},{9,11},{10,... | collective-permute-start | bytes 688136 | tf_op jit(solution)/shard_map/ppermute | solution.py:21
  8.7 1.9 %collective-permute-done.1.refs_0_ = bf16[2,16,3584]{2,1,0:T(8,128)(2,1)S(1)} collective-permute-done((bf16[2,16,3584]{2,1,0:T(8,128)(2,1)S(1)}, bf16[2,16,3584]{2,1,0:T(8,128)(2,1)S(1)}, u32[]{:S(2)}, u32[]{:S(2)}) %collective-permute-start.1) | collective-permute-done | bytes 229408 | tf_op jit(solution)/shard_map/ppermute | solution.py:21
  10.5 1.9 %collective-permute-start.2 = (bf16[2,16,3584]{2,1,0:T(8,128)(2,1)S(1)}, bf16[2,16,3584]{2,1,0:T(8,128)(2,1)S(1)}, u32[]{:S(2)}, u32[]{:S(2)}) collective-permute-start(bf16[2,16,3584]{2,1,0:T(8,128)(2,1)S(1)} %collective-permute-done.1.refs_0_), channel_id=1, source_target_pairs={{0,4},{4,0},{8,12},{12,8},{16,20},{20,16},{24,28},{28,24},{1,5},{5... | collective-permute-start | bytes 688136 | tf_op jit(solution)/shard_map/ppermute | solution.py:21
  12.5 1.5 %copy.14 = bf16[3584,128]{0,1:T(8,128)(2,1)S(1)} copy(bf16[3584,128]{1,0:T(8,128)(2,1)} %param.16) | data formatting | bytes 1835008 | tf_op jit(solution)/shard_map/optimization_barrier | solution.py:25
  14.0 2.0 %copy-done = bf16[8,64,3584]{2,1,0:T(8,128)(2,1)S(1)} copy-done((bf16[8,64,3584]{2,1,0:T(8,128)(2,1)S(1)}, bf16[8,64,3584]{2,1,0:T(8,128)(2,1)}, u32[]{:S(2)}) %copy-start) | copy-done | bytes 3670040
  16.0 1.2 %shard_map.109 = (f32[512,128]{1,0:T(8,128)S(1)}, f32[8,3584]{1,0:T(8,128)S(1)}) custom-call(bf16[128,3584]{1,0:T(8,128)(2,1)S(1)} %bitcast.28, bf16[8,64,3584]{2,1,0:T(8,128)(2,1)S(1)} %copy-done, f32[3584]{0:T(1024)S(1)} %copy-done.5, bf16[2,32,3584]{2,1,0:T(8,128)(2,1)S(1)} %bitcast.30), custom_call_target="tpu_custom_call" | custom-call | tf_op jit(solution)/shard_map/pallas_call | solution.py:337
  18.4 4.9 %shard_map.110 = (bf16[1024,128]{1,0:T(8,128)(2,1)S(1)}, bf16[1024,128]{1,0:T(8,128)(2,1)S(1)}, bf16[8,64,3584]{2,1,0:T(8,128)(2,1)S(1)}, bf16[8,64,3584]{2,1,0:...) custom-call(bf16[8,64,3584]{2,1,0:T(8,128)(2,1)S(1)} %copy-done.1, ...), custom_call_target="tpu_custom_call" | custom-call | tf_op jit(solution)/shard_map/pallas_call | solution.py:352
  23.3 1.6 %collective-permute-start.11 = (bf16[1024,128]{1,0:T(8,128)(2,1)S(1)}, bf16[1024,128]{1,0:T(8,128)(2,1)S(1)}, u32[]{:S(2)}, u32[]{:S(2)}) collective-permute-start(bf16[1024,128]{1,0:T(8,128)(2,1)S(1)} %get-tuple-element.45.order_ref.refs_7_), channel_id=1, source_target_pairs={{0,2},{1,3},{2,0},{3,1},{4,6},{5,7},{6,4},{7,5},{8,10},{9,11},{10,... | collective-permute-start | bytes 786440 | tf_op jit(solution)/shard_map/ppermute | solution.py:21
  25.7 1.7 %collective-permute-start.6 = (bf16[128,128]{1,0:T(8,128)(2,1)S(1)}, bf16[128,128]{1,0:T(8,128)(2,1)S(1)}, u32[]{:S(2)}, u32[]{:S(2)}) collective-permute-start(bf16[128,128]{1,0:T(8,128)(2,1)S(1)} %get-tuple-element.42.refs_11_), channel_id=1, source_target_pairs={{0,4},{4,0},{8,12},{12,8},{16,20},{20,16},{24,28},{28,24},{1,5},{5... | collective-permute-start | bytes 98312 | tf_op jit(solution)/shard_map/ppermute | solution.py:21
  27.4 1.6 %collective-permute-start.10 = (bf16[896,128]{1,0:T(8,128)(2,1)S(1)}, bf16[896,128]{1,0:T(8,128)(2,1)S(1)}, u32[]{:S(2)}, u32[]{:S(2)}) collective-permute-start(bf16[896,128]{1,0:T(8,128)(2,1)S(1)} %collective-permute-done.8.refs_1_), channel_id=1, source_target_pairs={{0,8},{4,12},{8,0},{12,4},{16,24},{20,28},{24,16},{28,20},{1,9},{5... | collective-permute-start | bytes 688136 | tf_op jit(solution)/shard_map/ppermute | solution.py:21
  29.5 1.5 %collective-permute-start.15 = (bf16[240,128]{1,0:T(8,128)(2,1)S(1)}, bf16[240,128]{1,0:T(8,128)(2,1)S(1)}, u32[]{:S(2)}, u32[]{:S(2)}) collective-permute-start(bf16[240,128]{1,0:T(8,128)(2,1)S(1)} %get-tuple-element.47), channel_id=1, source_target_pairs={{0,2},{1,3},{2,0},{3,1},{4,6},{5,7},{6,4},{7,5},{8,10},{9,11},{10,... | collective-permute-start | bytes 184328 | tf_op jit(solution)/shard_map/ppermute | solution.py:21
  31.7 1.1 %shard_map.112.refs_4_ = f32[1024,128]{1,0:T(8,128)S(1)} custom-call(bf16[128,128]{1,0:T(8,128)(2,1)S(1)} %collective-permute-done.6.order_ref.refs_12_, bf16[8,64,3584]{2,1,0:T(8,128)(2,1)S(1)} %get-tuple-element.33.near_ref.refs_0_, bf16[8,64,3584]{2,1,0:T(8,128)(2,1)S(1)} %get-tuple-element.34.far_ref.refs_1_, ...), custom_call_target="tpu_custom_call" | custom-call | tf_op jit(solution)/shard_map/pallas_call | solution.py:407
  32.9 2.3 %collective-permute-done.12.refs_14_ = bf16[128,128]{1,0:T(8,128)(2,1)S(1)} collective-permute-done((bf16[128,128]{1,0:T(8,128)(2,1)S(1)}, bf16[128,128]{1,0:T(8,128)(2,1)S(1)}, u32[]{:S(2)}, u32[]{:S(2)}) %collective-permute-start.12) | collective-permute-done | bytes 32800 | tf_op jit(solution)/shard_map/ppermute | solution.py:21
  37.1 2.5 %shard_map.113 = f32[8,256]{1,0:T(8,128)S(1)} custom-call(bf16[8,64,3584]{2,1,0:T(8,128)(2,1)S(1)} %get-tuple-element.33.near_ref.refs_0_, bf16[8,64,3584]{2,1,0:T(8,128)(2,1)S(1)} %get-tuple-element.34.far_ref.refs_1_, f32[1024,128]{1,0:T(8,128)S(1)} %get-tuple-element.35.refs_2_, bf16[1024,128]{1,0:T(8,128)(2,1)S(1)} %get-tuple-element.36.refs_3_, ...), custom_call_target="tpu_custom_call" | custom-call | tf_op jit(solution)/shard_map/pallas_call | solution.py:441
  40.3 1.2 %collective-permute-start.18 = (f32[8,256]{1,0:T(8,128)S(1)}, f32[8,256]{1,0:T(8,128)S(1)}, u32[]{:S(2)}, u32[]{:S(2)}) collective-permute-start(f32[8,256]{1,0:T(8,128)S(1)} %shard_map.113), channel_id=1, source_target_pairs={{0,3},{1,2},{2,1},{3,0},{4,7},{5,6},{6,5},{7,4},{8,11},{9,10},{10,... | collective-permute-start | bytes 24584 | tf_op jit(solution)/shard_map/ppermute | solution.py:21
  41.6 1.8 %collective-permute-done.17 = f32[8,256]{1,0:T(8,128)S(1)} collective-permute-done((f32[8,256]{1,0:T(8,128)S(1)}, f32[8,256]{1,0:T(8,128)S(1)}, u32[]{:S(2)}, u32[]{:S(2)}) %collective-permute-start.17) | collective-permute-done | bytes 8224 | tf_op jit(solution)/shard_map/ppermute | solution.py:21
  43.4 1.5 %collective-permute-start.19 = (f32[8,256]{1,0:T(8,128)S(1)}, f32[8,256]{1,0:T(8,128)S(1)}, u32[]{:S(2)}, u32[]{:S(2)}) collective-permute-start(f32[8,256]{1,0:T(8,128)S(1)} %add_add_fusion), channel_id=1, source_target_pairs={{0,4},{4,0},{8,12},{12,8},{16,20},{20,16},{24,28},{28,24},{1,5},{5... | collective-permute-start | bytes 24584 | tf_op jit(solution)/shard_map/ppermute | solution.py:21
  45.2 2.0 %collective-permute-done.19 = f32[8,256]{1,0:T(8,128)S(1)} collective-permute-done((f32[8,256]{1,0:T(8,128)S(1)}, f32[8,256]{1,0:T(8,128)S(1)}, u32[]{:S(2)}, u32[]{:S(2)}) %collective-permute-start.19) | collective-permute-done | bytes 8224 | tf_op jit(solution)/shard_map/ppermute | solution.py:21
  47.1 1.3 %collective-permute-start.20 = (f32[16,256]{1,0:T(8,128)S(1)}, f32[16,256]{1,0:T(8,128)S(1)}, u32[]{:S(2)}, u32[]{:S(2)}) collective-permute-start(f32[16,256]{1,0:T(8,128)S(1)} %pad_maximum_fusion.2), channel_id=1, source_target_pairs={{0,8},{4,12},{8,0},{12,4},{16,24},{20,28},{24,16},{28,20},{1,9},{5... | collective-permute-start | bytes 49160 | tf_op jit(solution)/shard_map/ppermute | solution.py:21
  48.5 2.4 %collective-permute-done.20 = f32[16,256]{1,0:T(8,128)S(1)} collective-permute-done((f32[16,256]{1,0:T(8,128)S(1)}, f32[16,256]{1,0:T(8,128)S(1)}, u32[]{:S(2)}, u32[]{:S(2)}) %collective-permute-start.20) | collective-permute-done | bytes 16416 | tf_op jit(solution)/shard_map/ppermute | solution.py:21
  50.9 2.6 %collective-permute-start.21 = (f32[32,256]{1,0:T(8,128)S(1)}, f32[32,256]{1,0:T(8,128)S(1)}, u32[]{:S(2)}, u32[]{:S(2)}) collective-permute-start(f32[32,256]{1,0:T(8,128)S(1)} %pad_maximum_fusion.1.near_ref), channel_id=1, source_target_pairs={{0,16},{4,20},{8,24},{12,28},{16,0},{20,4},{24,8},{28,12},{1,17},{... | collective-permute-start | bytes 98312 | tf_op jit(solution)/shard_map/ppermute | solution.py:21
  53.6 2.1 %collective-permute-done.21.far_ref = f32[32,256]{1,0:T(8,128)S(1)} collective-permute-done((f32[32,256]{1,0:T(8,128)S(1)}, f32[32,256]{1,0:T(8,128)S(1)}, u32[]{:S(2)}, u32[]{:S(2)}) %collective-permute-start.21) | collective-permute-done | bytes 32800 | tf_op jit(solution)/shard_map/ppermute | solution.py:21
  55.7 1.4 %shard_map.114 = bf16[4,4,64]{2,1,0:T(4,128)(2,1)} custom-call(f32[32,256]{1,0:T(8,128)S(1)} %pad_maximum_fusion.1.near_ref, f32[32,256]{1,0:T(8,128)S(1)} %collective-permute-done.21.far_ref, f32[16,64]{1,0:T(8,128)S(1)} %fusion.1.select_ref, f32[16,16]{1,0:T(8,128)S(1)} %fusion.8.allow_ref, f32[16,1]{1,0:T(8,128)S(1)} %copy.15.fill_ref, ...), custom_call_target="tpu_custom_call" | custom-call | tf_op jit(solution)/shard_map/pallas_call | solution.py:482
  (75 shorter events, 10.2 us)
Async XLA Ops:
  0.0 18.4 %collective-permute-start = (bf16[8,64,3584]{2,1,0:T(8,128)(2,1)}, bf16[8,64,3584]{2,1,0:T(8,128)(2,1)}, u32[]{:S(2)}, u32[]{:S(2)}) collective-permute-start(bf16[8,64,3584]{2,1,0:T(8,128)(2,1)} %near_ref.1), channel_id=1, source_target_pairs={{0,1},{1,0},{2,3},{3,2},{4,5},{5,4},{6,7},{7,6},{8,9},{9,8},{10,11... | collective-permute-start | bytes 11010056 | tf_op jit(solution)/shard_map/ppermute | solution.py:21
  1.4 9.1 %collective-permute-start.1 = (bf16[2,16,3584]{2,1,0:T(8,128)(2,1)S(1)}, bf16[2,16,3584]{2,1,0:T(8,128)(2,1)S(1)}, u32[]{:S(2)}, u32[]{:S(2)}) collective-permute-start(bf16[2,16,3584]{2,1,0:T(8,128)(2,1)S(1)} %dynamic-slice_bitcast_fusion.4), channel_id=1, source_target_pairs={{0,2},{1,3},{2,0},{3,1},{4,6},{5,7},{6,4},{7,5},{8,10},{9,11},{10,... | collective-permute-start | bytes 688136 | tf_op jit(solution)/shard_map/ppermute | solution.py:21
  5.0 12.6 %collective-permute-start.3 = (bf16[896,128]{1,0:T(8,128)(2,1)S(1)}, bf16[896,128]{1,0:T(8,128)(2,1)S(1)}, u32[]{:S(2)}, u32[]{:S(2)}) collective-permute-start(bf16[896,128]{1,0:T(8,128)(2,1)S(1)} %constant_dynamic-slice_fusion.2.refs_0_), channel_id=1, source_target_pairs={{0,2},{1,3},{2,0},{3,1},{4,6},{5,7},{6,4},{7,5},{8,10},{9,11},{10,... | collective-permute-start | bytes 688136 | tf_op jit(solution)/shard_map/ppermute | solution.py:21
  6.2 18.8 %collective-permute-start.7 = (bf16[896,128]{1,0:T(8,128)(2,1)S(1)}, bf16[896,128]{1,0:T(8,128)(2,1)S(1)}, u32[]{:S(2)}, u32[]{:S(2)}) collective-permute-start(bf16[896,128]{1,0:T(8,128)(2,1)S(1)} %get-tuple-element.59), channel_id=1, source_target_pairs={{0,2},{1,3},{2,0},{3,1},{4,6},{5,7},{6,4},{7,5},{8,10},{9,11},{10,... | collective-permute-start | bytes 688136 | tf_op jit(solution)/shard_map/ppermute | solution.py:21
  8.3 16.8 %collective-permute-start.8 = (bf16[896,128]{1,0:T(8,128)(2,1)S(1)}, bf16[896,128]{1,0:T(8,128)(2,1)S(1)}, u32[]{:S(2)}, u32[]{:S(2)}) collective-permute-start(bf16[896,128]{1,0:T(8,128)(2,1)S(1)} %get-tuple-element.58), channel_id=1, source_target_pairs={{0,2},{1,3},{2,0},{3,1},{4,6},{5,7},{6,4},{7,5},{8,10},{9,11},{10,... | collective-permute-start | bytes 688136 | tf_op jit(solution)/shard_map/ppermute | solution.py:21
  10.5 7.1 %collective-permute-start.2 = (bf16[2,16,3584]{2,1,0:T(8,128)(2,1)S(1)}, bf16[2,16,3584]{2,1,0:T(8,128)(2,1)S(1)}, u32[]{:S(2)}, u32[]{:S(2)}) collective-permute-start(bf16[2,16,3584]{2,1,0:T(8,128)(2,1)S(1)} %collective-permute-done.1.refs_0_), channel_id=1, source_target_pairs={{0,4},{4,0},{8,12},{12,8},{16,20},{20,16},{24,28},{28,24},{1,5},{5... | collective-permute-start | bytes 688136 | tf_op jit(solution)/shard_map/ppermute | solution.py:21
  17.6 7.6 %collective-permute-start.5 = (bf16[896,128]{1,0:T(8,128)(2,1)S(1)}, bf16[896,128]{1,0:T(8,128)(2,1)S(1)}, u32[]{:S(2)}, u32[]{:S(2)}) collective-permute-start(bf16[896,128]{1,0:T(8,128)(2,1)S(1)} %collective-permute-done.3.refs_1_), channel_id=1, source_target_pairs={{0,1},{1,0},{2,3},{3,2},{4,5},{5,4},{6,7},{7,6},{8,9},{9,8},{10,11... | collective-permute-start | bytes 688136 | tf_op jit(solution)/shard_map/ppermute | solution.py:21
  17.6 7.6 %collective-permute-start.4 = (bf16[896,128]{1,0:T(8,128)(2,1)S(1)}, bf16[896,128]{1,0:T(8,128)(2,1)S(1)}, u32[]{:S(2)}, u32[]{:S(2)}) collective-permute-start(bf16[896,128]{1,0:T(8,128)(2,1)S(1)} %constant_dynamic-slice_fusion.2.refs_0_), channel_id=1, source_target_pairs={{0,1},{1,0},{2,3},{3,2},{4,5},{5,4},{6,7},{7,6},{8,9},{9,8},{10,11... | collective-permute-start | bytes 688136 | tf_op jit(solution)/shard_map/ppermute | solution.py:21
  23.3 11.8 %collective-permute-start.11 = (bf16[1024,128]{1,0:T(8,128)(2,1)S(1)}, bf16[1024,128]{1,0:T(8,128)(2,1)S(1)}, u32[]{:S(2)}, u32[]{:S(2)}) collective-permute-start(bf16[1024,128]{1,0:T(8,128)(2,1)S(1)} %get-tuple-element.45.order_ref.refs_7_), channel_id=1, source_target_pairs={{0,2},{1,3},{2,0},{3,1},{4,6},{5,7},{6,4},{7,5},{8,10},{9,11},{10,... | collective-permute-start | bytes 786440 | tf_op jit(solution)/shard_map/ppermute | solution.py:21
  25.7 5.5 %collective-permute-start.6 = (bf16[128,128]{1,0:T(8,128)(2,1)S(1)}, bf16[128,128]{1,0:T(8,128)(2,1)S(1)}, u32[]{:S(2)}, u32[]{:S(2)}) collective-permute-start(bf16[128,128]{1,0:T(8,128)(2,1)S(1)} %get-tuple-element.42.refs_11_), channel_id=1, source_target_pairs={{0,4},{4,0},{8,12},{12,8},{16,20},{20,16},{24,28},{28,24},{1,5},{5... | collective-permute-start | bytes 98312 | tf_op jit(solution)/shard_map/ppermute | solution.py:21
  27.4 8.4 %collective-permute-start.10 = (bf16[896,128]{1,0:T(8,128)(2,1)S(1)}, bf16[896,128]{1,0:T(8,128)(2,1)S(1)}, u32[]{:S(2)}, u32[]{:S(2)}) collective-permute-start(bf16[896,128]{1,0:T(8,128)(2,1)S(1)} %collective-permute-done.8.refs_1_), channel_id=1, source_target_pairs={{0,8},{4,12},{8,0},{12,4},{16,24},{20,28},{24,16},{28,20},{1,9},{5... | collective-permute-start | bytes 688136 | tf_op jit(solution)/shard_map/ppermute | solution.py:21
  29.0 6.9 %collective-permute-start.9 = (bf16[896,128]{1,0:T(8,128)(2,1)S(1)}, bf16[896,128]{1,0:T(8,128)(2,1)S(1)}, u32[]{:S(2)}, u32[]{:S(2)}) collective-permute-start(bf16[896,128]{1,0:T(8,128)(2,1)S(1)} %collective-permute-done.7.refs_0_), channel_id=1, source_target_pairs={{0,4},{4,0},{8,12},{12,8},{16,20},{20,16},{24,28},{28,24},{1,5},{5... | collective-permute-start | bytes 688136 | tf_op jit(solution)/shard_map/ppermute | solution.py:21
  29.5 6.3 %collective-permute-start.15 = (bf16[240,128]{1,0:T(8,128)(2,1)S(1)}, bf16[240,128]{1,0:T(8,128)(2,1)S(1)}, u32[]{:S(2)}, u32[]{:S(2)}) collective-permute-start(bf16[240,128]{1,0:T(8,128)(2,1)S(1)} %get-tuple-element.47), channel_id=1, source_target_pairs={{0,2},{1,3},{2,0},{3,1},{4,6},{5,7},{6,4},{7,5},{8,10},{9,11},{10,... | collective-permute-start | bytes 184328 | tf_op jit(solution)/shard_map/ppermute | solution.py:21
  31.2 4.0 %collective-permute-start.12 = (bf16[128,128]{1,0:T(8,128)(2,1)S(1)}, bf16[128,128]{1,0:T(8,128)(2,1)S(1)}, u32[]{:S(2)}, u32[]{:S(2)}) collective-permute-start(bf16[128,128]{1,0:T(8,128)(2,1)S(1)} %collective-permute-done.6.order_ref.refs_12_), channel_id=1, source_target_pairs={{0,2},{1,3},{2,0},{3,1},{4,6},{5,7},{6,4},{7,5},{8,10},{9,11},{10,... | collective-permute-start | bytes 98312 | tf_op jit(solution)/shard_map/ppermute | solution.py:21
  35.1 1.5 %collective-permute-start.14 = (bf16[1024,128]{1,0:T(8,128)(2,1)S(1)}, bf16[1024,128]{1,0:T(8,128)(2,1)S(1)}, u32[]{:S(2)}, u32[]{:S(2)}) collective-permute-start(bf16[1024,128]{1,0:T(8,128)(2,1)S(1)} %collective-permute-done.11.refs_8_), channel_id=1, source_target_pairs={{0,1},{1,0},{2,3},{3,2},{4,5},{5,4},{6,7},{7,6},{8,9},{9,8},{10,11... | collective-permute-start | bytes 786440 | tf_op jit(solution)/shard_map/ppermute | solution.py:21
  35.1 1.9 %collective-permute-start.13 = (bf16[1024,128]{1,0:T(8,128)(2,1)S(1)}, bf16[1024,128]{1,0:T(8,128)(2,1)S(1)}, u32[]{:S(2)}, u32[]{:S(2)}) collective-permute-start(bf16[1024,128]{1,0:T(8,128)(2,1)S(1)} %get-tuple-element.45.order_ref.refs_7_), channel_id=1, source_target_pairs={{0,1},{1,0},{2,3},{3,2},{4,5},{5,4},{6,7},{7,6},{8,9},{9,8},{10,11... | collective-permute-start | bytes 786440 | tf_op jit(solution)/shard_map/ppermute | solution.py:21
  37.1 18.6 %copy-start.4 = (bf16[256,3,64]{0,2,1:T(8,128)(2,1)S(1)}, bf16[256,3,64]{0,2,1:T(8,128)(2,1)}, u32[]{:S(2)}) copy-start(bf16[256,3,64]{0,2,1:T(8,128)(2,1)} %param.21) | copy-start | bytes 294916
  37.1 18.6 %copy-start.6 = (f32[256]{0:T(256)S(1)}, f32[256]{0:T(256)}, u32[]{:S(2)}) copy-start(f32[256]{0:T(256)} %param.20) | copy-start | bytes 3076
  39.5 2.1 %collective-permute-start.16 = (f32[8,256]{1,0:T(8,128)S(1)}, f32[8,256]{1,0:T(8,128)S(1)}, u32[]{:S(2)}, u32[]{:S(2)}) collective-permute-start(f32[8,256]{1,0:T(8,128)S(1)} %shard_map.113), channel_id=1, source_target_pairs={{0,1},{1,0},{2,3},{3,2},{4,5},{5,4},{6,7},{7,6},{8,9},{9,8},{10,11... | collective-permute-start | bytes 24584 | tf_op jit(solution)/shard_map/ppermute | solution.py:21
  39.7 3.7 %collective-permute-start.17 = (f32[8,256]{1,0:T(8,128)S(1)}, f32[8,256]{1,0:T(8,128)S(1)}, u32[]{:S(2)}, u32[]{:S(2)}) collective-permute-start(f32[8,256]{1,0:T(8,128)S(1)} %shard_map.113), channel_id=1, source_target_pairs={{0,2},{1,3},{2,0},{3,1},{4,6},{5,7},{6,4},{7,5},{8,10},{9,11},{10,... | collective-permute-start | bytes 24584 | tf_op jit(solution)/shard_map/ppermute | solution.py:21
  40.3 3.2 %collective-permute-start.18 = (f32[8,256]{1,0:T(8,128)S(1)}, f32[8,256]{1,0:T(8,128)S(1)}, u32[]{:S(2)}, u32[]{:S(2)}) collective-permute-start(f32[8,256]{1,0:T(8,128)S(1)} %shard_map.113), channel_id=1, source_target_pairs={{0,3},{1,2},{2,1},{3,0},{4,7},{5,6},{6,5},{7,4},{8,11},{9,10},{10,... | collective-permute-start | bytes 24584 | tf_op jit(solution)/shard_map/ppermute | solution.py:21
  43.4 3.7 %collective-permute-start.19 = (f32[8,256]{1,0:T(8,128)S(1)}, f32[8,256]{1,0:T(8,128)S(1)}, u32[]{:S(2)}, u32[]{:S(2)}) collective-permute-start(f32[8,256]{1,0:T(8,128)S(1)} %add_add_fusion), channel_id=1, source_target_pairs={{0,4},{4,0},{8,12},{12,8},{16,20},{20,16},{24,28},{28,24},{1,5},{5... | collective-permute-start | bytes 24584 | tf_op jit(solution)/shard_map/ppermute | solution.py:21
  47.1 3.7 %collective-permute-start.20 = (f32[16,256]{1,0:T(8,128)S(1)}, f32[16,256]{1,0:T(8,128)S(1)}, u32[]{:S(2)}, u32[]{:S(2)}) collective-permute-start(f32[16,256]{1,0:T(8,128)S(1)} %pad_maximum_fusion.2), channel_id=1, source_target_pairs={{0,8},{4,12},{8,0},{12,4},{16,24},{20,28},{24,16},{28,20},{1,9},{5... | collective-permute-start | bytes 49160 | tf_op jit(solution)/shard_map/ppermute | solution.py:21
  50.9 4.8 %collective-permute-start.21 = (f32[32,256]{1,0:T(8,128)S(1)}, f32[32,256]{1,0:T(8,128)S(1)}, u32[]{:S(2)}, u32[]{:S(2)}) collective-permute-start(f32[32,256]{1,0:T(8,128)S(1)} %pad_maximum_fusion.1.near_ref), channel_id=1, source_target_pairs={{0,16},{4,20},{8,24},{12,28},{16,0},{20,4},{24,8},{28,12},{1,17},{... | collective-permute-start | bytes 98312 | tf_op jit(solution)/shard_map/ppermute | solution.py:21
  (9 other events, 56.9 us)

commit v8 on v7

--- a/solution.py
+++ b/solution.py
@@ -450,11 +450,11 @@
     while bit < n_tp:
         part = part + flipped(part, "tp", bit)
         bit *= 2
-    bit = 1
-    while bit < n_rep // 2:
+    bit = n_rep // 2
+    while bit > 1:
         part = jnp.concatenate([part, flipped(part, "rep", bit)], axis=0)
-        bit *= 2
-    part_far = flipped(part, "rep", bit)
+        bit //= 2
+    part_far = flipped(part, "rep", 1)
 
     seg_replica, doc_of_segment, doc_owner = after((seg_replica, doc_of_segment, doc_owner), kv)
     replica_of, rank = slot_table(seg_replica)
@@ -462,7 +462,11 @@
     owned = OWN_DOCS * DOC_MOST
     wanted = rep_index * owned + jnp.arange(owned, dtype=jnp.int32)
     matches = (row_of[None, :] == wanted[:, None]).astype(F32)
-    at_slot = (replica_of ^ rep_index) * CAP + rank
+    apart, place_of, bit = replica_of ^ rep_index, 0, 1
+    while bit < n_rep:
+        place_of = place_of + (apart // bit % 2) * (n_rep // 2 // bit)
+        bit *= 2
+    at_slot = place_of * CAP + rank
     holds = (at_slot[:, None] == jnp.arange(n_rep * CAP, dtype=jnp.int32)[None, :]).astype(F32)
     select = jnp.dot(matches, holds)
     filled = jnp.sum(matches, axis=1)

time: 57.3 us -> 57.3 us (level)
  no operation moved by 1% of the time
where the time goes in v8:
time: 57.3 us; the launch traced here: 57.1 us
  starting transfers between devices  23.3 us (41%)
  waiting for transfers between devices  13.9 us (24%)
  Pallas kernels  11.4 us (20%)
  local copies, waits for them, and re-layouts  6.7 us (12%)
  other arithmetic  1.29 us (2%)
    ppermute x22, starting transfers between devices, flipped(): return lax.ppermute(block, axis, [(i, i ^ mask) for i in range(count)])  23.3 us
    ppermute x22, waiting for transfers between devices, flipped(): return lax.ppermute(block, axis, [(i, i ^ mask) for i in range(count)])  13.9 us
    pallas_call x1, Pallas kernels, local(): pl.pallas_call(functools.partial(keyvalue_kernel, length), out_shape=out,...  4.89 us
    dynamic_slice x3, local copies, waits for them, and re-layouts, cut(): return lax.dynamic_slice_in_dim(array, at * size, size, axis=axis)  2.99 us
    pallas_call x1, Pallas kernels, local(): pl.pallas_call(functools.partial(attention_kernel, masks, group, length),...  2.47 us
    unnamed x22, local copies, waits for them, and re-layouts  2.08 us
    optimization_barrier x1, local copies, waits for them, and re-layouts, after(): return lax.optimization_barrier((value, earlier))[0]  1.46 us
    pallas_call x1, Pallas kernels, local(): pl.pallas_call(document_kernel, out_shape=jax.ShapeDtypeStruct((OWN_DOCS,...  1.37 us
  transfers between devices with their start and end apart: 22, of which 9 were waited for; matrix products, arithmetic and copies ran while one was open for 11% of the time, Pallas kernels for 13%

profile of v8, /device:TPU:0, one launch (start us, length us, event | category | flops | bytes accessed | tf_op | source)
XLA Modules:
  0.0 57.1 jit_solution(16961523631181677590)
XLA Ops:
  1.4 2.7 %collective-permute-start.1 = (bf16[2,16,3584]{2,1,0:T(8,128)(2,1)S(1)}, bf16[2,16,3584]{2,1,0:T(8,128)(2,1)S(1)}, u32[]{:S(2)}, u32[]{:S(2)}) collective-permute-start(bf16[2,16,3584]{2,1,0:T(8,128)(2,1)S(1)} %dynamic-slice_bitcast_fusion.4), channel_id=1, source_target_pairs={{0,2},{1,3},{2,0},{3,1},{4,6},{5,7},{6,4},{7,5},{8,10},{9,11},{10,... | collective-permute-start | bytes 688136 | tf_op jit(solution)/shard_map/ppermute | solution.py:21
  6.2 2.0 %collective-permute-start.7 = (bf16[896,128]{1,0:T(8,128)(2,1)S(1)}, bf16[896,128]{1,0:T(8,128)(2,1)S(1)}, u32[]{:S(2)}, u32[]{:S(2)}) collective-permute-start(bf16[896,128]{1,0:T(8,128)(2,1)S(1)} %get-tuple-element.59), channel_id=1, source_target_pairs={{0,2},{1,3},{2,0},{3,1},{4,6},{5,7},{6,4},{7,5},{8,10},{9,11},{10,... | collective-permute-start | bytes 688136 | tf_op jit(solution)/shard_map/ppermute | solution.py:21
  8.7 1.9 %collective-permute-done.1.refs_0_ = bf16[2,16,3584]{2,1,0:T(8,128)(2,1)S(1)} collective-permute-done((bf16[2,16,3584]{2,1,0:T(8,128)(2,1)S(1)}, bf16[2,16,3584]{2,1,0:T(8,128)(2,1)S(1)}, u32[]{:S(2)}, u32[]{:S(2)}) %collective-permute-start.1) | collective-permute-done | bytes 229408 | tf_op jit(solution)/shard_map/ppermute | solution.py:21
  10.5 1.9 %collective-permute-start.2 = (bf16[2,16,3584]{2,1,0:T(8,128)(2,1)S(1)}, bf16[2,16,3584]{2,1,0:T(8,128)(2,1)S(1)}, u32[]{:S(2)}, u32[]{:S(2)}) collective-permute-start(bf16[2,16,3584]{2,1,0:T(8,128)(2,1)S(1)} %collective-permute-done.1.refs_0_), channel_id=1, source_target_pairs={{0,4},{4,0},{8,12},{12,8},{16,20},{20,16},{24,28},{28,24},{1,5},{5... | collective-permute-start | bytes 688136 | tf_op jit(solution)/shard_map/ppermute | solution.py:21
  12.5 1.5 %copy.14 = bf16[3584,128]{0,1:T(8,128)(2,1)S(1)} copy(bf16[3584,128]{1,0:T(8,128)(2,1)} %param.16) | data formatting | bytes 1835008 | tf_op jit(solution)/shard_map/optimization_barrier | solution.py:25
  14.0 2.0 %copy-done = bf16[8,64,3584]{2,1,0:T(8,128)(2,1)S(1)} copy-done((bf16[8,64,3584]{2,1,0:T(8,128)(2,1)S(1)}, bf16[8,64,3584]{2,1,0:T(8,128)(2,1)}, u32[]{:S(2)}) %copy-start) | copy-done | bytes 3670040
  16.0 1.2 %shard_map.109 = (f32[512,128]{1,0:T(8,128)S(1)}, f32[8,3584]{1,0:T(8,128)S(1)}) custom-call(bf16[128,3584]{1,0:T(8,128)(2,1)S(1)} %bitcast.28, bf16[8,64,3584]{2,1,0:T(8,128)(2,1)S(1)} %copy-done, f32[3584]{0:T(1024)S(1)} %copy-done.5, bf16[2,32,3584]{2,1,0:T(8,128)(2,1)S(1)} %bitcast.30), custom_call_target="tpu_custom_call" | custom-call | tf_op jit(solution)/shard_map/pallas_call | solution.py:337
  18.4 4.9 %shard_map.110 = (bf16[1024,128]{1,0:T(8,128)(2,1)S(1)}, bf16[1024,128]{1,0:T(8,128)(2,1)S(1)}, bf16[8,64,3584]{2,1,0:T(8,128)(2,1)S(1)}, bf16[8,64,3584]{2,1,0:...) custom-call(bf16[8,64,3584]{2,1,0:T(8,128)(2,1)S(1)} %copy-done.1, ...), custom_call_target="tpu_custom_call" | custom-call | tf_op jit(solution)/shard_map/pallas_call | solution.py:352
  23.3 1.6 %collective-permute-start.11 = (bf16[1024,128]{1,0:T(8,128)(2,1)S(1)}, bf16[1024,128]{1,0:T(8,128)(2,1)S(1)}, u32[]{:S(2)}, u32[]{:S(2)}) collective-permute-start(bf16[1024,128]{1,0:T(8,128)(2,1)S(1)} %get-tuple-element.45.order_ref.refs_7_), channel_id=1, source_target_pairs={{0,2},{1,3},{2,0},{3,1},{4,6},{5,7},{6,4},{7,5},{8,10},{9,11},{10,... | collective-permute-start | bytes 786440 | tf_op jit(solution)/shard_map/ppermute | solution.py:21
  25.7 1.7 %collective-permute-start.6 = (bf16[128,128]{1,0:T(8,128)(2,1)S(1)}, bf16[128,128]{1,0:T(8,128)(2,1)S(1)}, u32[]{:S(2)}, u32[]{:S(2)}) collective-permute-start(bf16[128,128]{1,0:T(8,128)(2,1)S(1)} %get-tuple-element.42.refs_11_), channel_id=1, source_target_pairs={{0,4},{4,0},{8,12},{12,8},{16,20},{20,16},{24,28},{28,24},{1,5},{5... | collective-permute-start | bytes 98312 | tf_op jit(solution)/shard_map/ppermute | solution.py:21
  27.4 1.6 %collective-permute-start.10 = (bf16[896,128]{1,0:T(8,128)(2,1)S(1)}, bf16[896,128]{1,0:T(8,128)(2,1)S(1)}, u32[]{:S(2)}, u32[]{:S(2)}) collective-permute-start(bf16[896,128]{1,0:T(8,128)(2,1)S(1)} %collective-permute-done.8.refs_1_), channel_id=1, source_target_pairs={{0,8},{4,12},{8,0},{12,4},{16,24},{20,28},{24,16},{28,20},{1,9},{5... | collective-permute-start | bytes 688136 | tf_op jit(solution)/shard_map/ppermute | solution.py:21
  29.5 1.5 %collective-permute-start.15 = (bf16[240,128]{1,0:T(8,128)(2,1)S(1)}, bf16[240,128]{1,0:T(8,128)(2,1)S(1)}, u32[]{:S(2)}, u32[]{:S(2)}) collective-permute-start(bf16[240,128]{1,0:T(8,128)(2,1)S(1)} %get-tuple-element.47), channel_id=1, source_target_pairs={{0,2},{1,3},{2,0},{3,1},{4,6},{5,7},{6,4},{7,5},{8,10},{9,11},{10,... | collective-permute-start | bytes 184328 | tf_op jit(solution)/shard_map/ppermute | solution.py:21
  31.7 1.1 %shard_map.112.refs_4_ = f32[1024,128]{1,0:T(8,128)S(1)} custom-call(bf16[128,128]{1,0:T(8,128)(2,1)S(1)} %collective-permute-done.6.order_ref.refs_12_, bf16[8,64,3584]{2,1,0:T(8,128)(2,1)S(1)} %get-tuple-element.33.near_ref.refs_0_, bf16[8,64,3584]{2,1,0:T(8,128)(2,1)S(1)} %get-tuple-element.34.far_ref.refs_1_, ...), custom_call_target="tpu_custom_call" | custom-call | tf_op jit(solution)/shard_map/pallas_call | solution.py:407
  32.9 2.3 %collective-permute-done.12.refs_14_ = bf16[128,128]{1,0:T(8,128)(2,1)S(1)} collective-permute-done((bf16[128,128]{1,0:T(8,128)(2,1)S(1)}, bf16[128,128]{1,0:T(8,128)(2,1)S(1)}, u32[]{:S(2)}, u32[]{:S(2)}) %collective-permute-start.12) | collective-permute-done | bytes 32800 | tf_op jit(solution)/shard_map/ppermute | solution.py:21
  37.1 2.5 %shard_map.113 = f32[8,256]{1,0:T(8,128)S(1)} custom-call(bf16[8,64,3584]{2,1,0:T(8,128)(2,1)S(1)} %get-tuple-element.33.near_ref.refs_0_, bf16[8,64,3584]{2,1,0:T(8,128)(2,1)S(1)} %get-tuple-element.34.far_ref.refs_1_, f32[1024,128]{1,0:T(8,128)S(1)} %get-tuple-element.35.refs_2_, bf16[1024,128]{1,0:T(8,128)(2,1)S(1)} %get-tuple-element.36.refs_3_, ...), custom_call_target="tpu_custom_call" | custom-call | tf_op jit(solution)/shard_map/pallas_call | solution.py:441
  40.3 1.2 %collective-permute-start.18 = (f32[8,256]{1,0:T(8,128)S(1)}, f32[8,256]{1,0:T(8,128)S(1)}, u32[]{:S(2)}, u32[]{:S(2)}) collective-permute-start(f32[8,256]{1,0:T(8,128)S(1)} %shard_map.113), channel_id=1, source_target_pairs={{0,3},{1,2},{2,1},{3,0},{4,7},{5,6},{6,5},{7,4},{8,11},{9,10},{10,... | collective-permute-start | bytes 24584 | tf_op jit(solution)/shard_map/ppermute | solution.py:21
  41.6 1.8 %collective-permute-done.17 = f32[8,256]{1,0:T(8,128)S(1)} collective-permute-done((f32[8,256]{1,0:T(8,128)S(1)}, f32[8,256]{1,0:T(8,128)S(1)}, u32[]{:S(2)}, u32[]{:S(2)}) %collective-permute-start.17) | collective-permute-done | bytes 8224 | tf_op jit(solution)/shard_map/ppermute | solution.py:21
  43.4 2.7 %collective-permute-start.19 = (f32[8,256]{1,0:T(8,128)S(1)}, f32[8,256]{1,0:T(8,128)S(1)}, u32[]{:S(2)}, u32[]{:S(2)}) collective-permute-start(f32[8,256]{1,0:T(8,128)S(1)} %add_add_fusion), channel_id=1, source_target_pairs={{0,16},{4,20},{8,24},{12,28},{16,0},{20,4},{24,8},{28,12},{1,17},{... | collective-permute-start | bytes 24584 | tf_op jit(solution)/shard_map/ppermute | solution.py:21
  46.3 1.8 %collective-permute-done.19 = f32[8,256]{1,0:T(8,128)S(1)} collective-permute-done((f32[8,256]{1,0:T(8,128)S(1)}, f32[8,256]{1,0:T(8,128)S(1)}, u32[]{:S(2)}, u32[]{:S(2)}) %collective-permute-start.19) | collective-permute-done | bytes 8224 | tf_op jit(solution)/shard_map/ppermute | solution.py:21
  48.0 1.3 %collective-permute-start.20 = (f32[16,256]{1,0:T(8,128)S(1)}, f32[16,256]{1,0:T(8,128)S(1)}, u32[]{:S(2)}, u32[]{:S(2)}) collective-permute-start(f32[16,256]{1,0:T(8,128)S(1)} %pad_maximum_fusion.2), channel_id=1, source_target_pairs={{0,8},{4,12},{8,0},{12,4},{16,24},{20,28},{24,16},{28,20},{1,9},{5... | collective-permute-start | bytes 49160 | tf_op jit(solution)/shard_map/ppermute | solution.py:21
  49.4 2.4 %collective-permute-done.20 = f32[16,256]{1,0:T(8,128)S(1)} collective-permute-done((f32[16,256]{1,0:T(8,128)S(1)}, f32[16,256]{1,0:T(8,128)S(1)}, u32[]{:S(2)}, u32[]{:S(2)}) %collective-permute-start.20) | collective-permute-done | bytes 16416 | tf_op jit(solution)/shard_map/ppermute | solution.py:21
  51.8 1.5 %collective-permute-start.21 = (f32[32,256]{1,0:T(8,128)S(1)}, f32[32,256]{1,0:T(8,128)S(1)}, u32[]{:S(2)}, u32[]{:S(2)}) collective-permute-start(f32[32,256]{1,0:T(8,128)S(1)} %pad_maximum_fusion.1.near_ref), channel_id=1, source_target_pairs={{0,4},{4,0},{8,12},{12,8},{16,20},{20,16},{24,28},{28,24},{1,5},{5... | collective-permute-start | bytes 98312 | tf_op jit(solution)/shard_map/ppermute | solution.py:21
  53.5 2.2 %collective-permute-done.21.far_ref = f32[32,256]{1,0:T(8,128)S(1)} collective-permute-done((f32[32,256]{1,0:T(8,128)S(1)}, f32[32,256]{1,0:T(8,128)S(1)}, u32[]{:S(2)}, u32[]{:S(2)}) %collective-permute-start.21) | collective-permute-done | bytes 32800 | tf_op jit(solution)/shard_map/ppermute | solution.py:21
  55.7 1.4 %shard_map.114 = bf16[4,4,64]{2,1,0:T(4,128)(2,1)} custom-call(f32[32,256]{1,0:T(8,128)S(1)} %pad_maximum_fusion.1.near_ref, f32[32,256]{1,0:T(8,128)S(1)} %collective-permute-done.21.far_ref, f32[16,64]{1,0:T(8,128)S(1)} %fusion.1.select_ref, f32[16,16]{1,0:T(8,128)S(1)} %fusion.8.allow_ref, f32[16,1]{1,0:T(8,128)S(1)} %copy.15.fill_ref, ...), custom_call_target="tpu_custom_call" | custom-call | tf_op jit(solution)/shard_map/pallas_call | solution.py:486
  (75 shorter events, 10.2 us)
Async XLA Ops:
  0.0 18.4 %collective-permute-start = (bf16[8,64,3584]{2,1,0:T(8,128)(2,1)}, bf16[8,64,3584]{2,1,0:T(8,128)(2,1)}, u32[]{:S(2)}, u32[]{:S(2)}) collective-permute-start(bf16[8,64,3584]{2,1,0:T(8,128)(2,1)} %near_ref.1), channel_id=1, source_target_pairs={{0,1},{1,0},{2,3},{3,2},{4,5},{5,4},{6,7},{7,6},{8,9},{9,8},{10,11... | collective-permute-start | bytes 11010056 | tf_op jit(solution)/shard_map/ppermute | solution.py:21
  1.4 9.1 %collective-permute-start.1 = (bf16[2,16,3584]{2,1,0:T(8,128)(2,1)S(1)}, bf16[2,16,3584]{2,1,0:T(8,128)(2,1)S(1)}, u32[]{:S(2)}, u32[]{:S(2)}) collective-permute-start(bf16[2,16,3584]{2,1,0:T(8,128)(2,1)S(1)} %dynamic-slice_bitcast_fusion.4), channel_id=1, source_target_pairs={{0,2},{1,3},{2,0},{3,1},{4,6},{5,7},{6,4},{7,5},{8,10},{9,11},{10,... | collective-permute-start | bytes 688136 | tf_op jit(solution)/shard_map/ppermute | solution.py:21
  5.0 12.6 %collective-permute-start.3 = (bf16[896,128]{1,0:T(8,128)(2,1)S(1)}, bf16[896,128]{1,0:T(8,128)(2,1)S(1)}, u32[]{:S(2)}, u32[]{:S(2)}) collective-permute-start(bf16[896,128]{1,0:T(8,128)(2,1)S(1)} %constant_dynamic-slice_fusion.2.refs_0_), channel_id=1, source_target_pairs={{0,2},{1,3},{2,0},{3,1},{4,6},{5,7},{6,4},{7,5},{8,10},{9,11},{10,... | collective-permute-start | bytes 688136 | tf_op jit(solution)/shard_map/ppermute | solution.py:21
  6.2 18.8 %collective-permute-start.7 = (bf16[896,128]{1,0:T(8,128)(2,1)S(1)}, bf16[896,128]{1,0:T(8,128)(2,1)S(1)}, u32[]{:S(2)}, u32[]{:S(2)}) collective-permute-start(bf16[896,128]{1,0:T(8,128)(2,1)S(1)} %get-tuple-element.59), channel_id=1, source_target_pairs={{0,2},{1,3},{2,0},{3,1},{4,6},{5,7},{6,4},{7,5},{8,10},{9,11},{10,... | collective-permute-start | bytes 688136 | tf_op jit(solution)/shard_map/ppermute | solution.py:21
  8.3 16.8 %collective-permute-start.8 = (bf16[896,128]{1,0:T(8,128)(2,1)S(1)}, bf16[896,128]{1,0:T(8,128)(2,1)S(1)}, u32[]{:S(2)}, u32[]{:S(2)}) collective-permute-start(bf16[896,128]{1,0:T(8,128)(2,1)S(1)} %get-tuple-element.58), channel_id=1, source_target_pairs={{0,2},{1,3},{2,0},{3,1},{4,6},{5,7},{6,4},{7,5},{8,10},{9,11},{10,... | collective-permute-start | bytes 688136 | tf_op jit(solution)/shard_map/ppermute | solution.py:21
  10.5 7.1 %collective-permute-start.2 = (bf16[2,16,3584]{2,1,0:T(8,128)(2,1)S(1)}, bf16[2,16,3584]{2,1,0:T(8,128)(2,1)S(1)}, u32[]{:S(2)}, u32[]{:S(2)}) collective-permute-start(bf16[2,16,3584]{2,1,0:T(8,128)(2,1)S(1)} %collective-permute-done.1.refs_0_), channel_id=1, source_target_pairs={{0,4},{4,0},{8,12},{12,8},{16,20},{20,16},{24,28},{28,24},{1,5},{5... | collective-permute-start | bytes 688136 | tf_op jit(solution)/shard_map/ppermute | solution.py:21
  17.6 7.6 %collective-permute-start.5 = (bf16[896,128]{1,0:T(8,128)(2,1)S(1)}, bf16[896,128]{1,0:T(8,128)(2,1)S(1)}, u32[]{:S(2)}, u32[]{:S(2)}) collective-permute-start(bf16[896,128]{1,0:T(8,128)(2,1)S(1)} %collective-permute-done.3.refs_1_), channel_id=1, source_target_pairs={{0,1},{1,0},{2,3},{3,2},{4,5},{5,4},{6,7},{7,6},{8,9},{9,8},{10,11... | collective-permute-start | bytes 688136 | tf_op jit(solution)/shard_map/ppermute | solution.py:21
  17.6 7.6 %collective-permute-start.4 = (bf16[896,128]{1,0:T(8,128)(2,1)S(1)}, bf16[896,128]{1,0:T(8,128)(2,1)S(1)}, u32[]{:S(2)}, u32[]{:S(2)}) collective-permute-start(bf16[896,128]{1,0:T(8,128)(2,1)S(1)} %constant_dynamic-slice_fusion.2.refs_0_), channel_id=1, source_target_pairs={{0,1},{1,0},{2,3},{3,2},{4,5},{5,4},{6,7},{7,6},{8,9},{9,8},{10,11... | collective-permute-start | bytes 688136 | tf_op jit(solution)/shard_map/ppermute | solution.py:21
  23.3 11.8 %collective-permute-start.11 = (bf16[1024,128]{1,0:T(8,128)(2,1)S(1)}, bf16[1024,128]{1,0:T(8,128)(2,1)S(1)}, u32[]{:S(2)}, u32[]{:S(2)}) collective-permute-start(bf16[1024,128]{1,0:T(8,128)(2,1)S(1)} %get-tuple-element.45.order_ref.refs_7_), channel_id=1, source_target_pairs={{0,2},{1,3},{2,0},{3,1},{4,6},{5,7},{6,4},{7,5},{8,10},{9,11},{10,... | collective-permute-start | bytes 786440 | tf_op jit(solution)/shard_map/ppermute | solution.py:21
  25.7 5.5 %collective-permute-start.6 = (bf16[128,128]{1,0:T(8,128)(2,1)S(1)}, bf16[128,128]{1,0:T(8,128)(2,1)S(1)}, u32[]{:S(2)}, u32[]{:S(2)}) collective-permute-start(bf16[128,128]{1,0:T(8,128)(2,1)S(1)} %get-tuple-element.42.refs_11_), channel_id=1, source_target_pairs={{0,4},{4,0},{8,12},{12,8},{16,20},{20,16},{24,28},{28,24},{1,5},{5... | collective-permute-start | bytes 98312 | tf_op jit(solution)/shard_map/ppermute | solution.py:21
  27.4 8.5 %collective-permute-start.10 = (bf16[896,128]{1,0:T(8,128)(2,1)S(1)}, bf16[896,128]{1,0:T(8,128)(2,1)S(1)}, u32[]{:S(2)}, u32[]{:S(2)}) collective-permute-start(bf16[896,128]{1,0:T(8,128)(2,1)S(1)} %collective-permute-done.8.refs_1_), channel_id=1, source_target_pairs={{0,8},{4,12},{8,0},{12,4},{16,24},{20,28},{24,16},{28,20},{1,9},{5... | collective-permute-start | bytes 688136 | tf_op jit(solution)/shard_map/ppermute | solution.py:21
  29.0 6.9 %collective-permute-start.9 = (bf16[896,128]{1,0:T(8,128)(2,1)S(1)}, bf16[896,128]{1,0:T(8,128)(2,1)S(1)}, u32[]{:S(2)}, u32[]{:S(2)}) collective-permute-start(bf16[896,128]{1,0:T(8,128)(2,1)S(1)} %collective-permute-done.7.refs_0_), channel_id=1, source_target_pairs={{0,4},{4,0},{8,12},{12,8},{16,20},{20,16},{24,28},{28,24},{1,5},{5... | collective-permute-start | bytes 688136 | tf_op jit(solution)/shard_map/ppermute | solution.py:21
  29.5 6.3 %collective-permute-start.15 = (bf16[240,128]{1,0:T(8,128)(2,1)S(1)}, bf16[240,128]{1,0:T(8,128)(2,1)S(1)}, u32[]{:S(2)}, u32[]{:S(2)}) collective-permute-start(bf16[240,128]{1,0:T(8,128)(2,1)S(1)} %get-tuple-element.47), channel_id=1, source_target_pairs={{0,2},{1,3},{2,0},{3,1},{4,6},{5,7},{6,4},{7,5},{8,10},{9,11},{10,... | collective-permute-start | bytes 184328 | tf_op jit(solution)/shard_map/ppermute | solution.py:21
  31.2 4.0 %collective-permute-start.12 = (bf16[128,128]{1,0:T(8,128)(2,1)S(1)}, bf16[128,128]{1,0:T(8,128)(2,1)S(1)}, u32[]{:S(2)}, u32[]{:S(2)}) collective-permute-start(bf16[128,128]{1,0:T(8,128)(2,1)S(1)} %collective-permute-done.6.order_ref.refs_12_), channel_id=1, source_target_pairs={{0,2},{1,3},{2,0},{3,1},{4,6},{5,7},{6,4},{7,5},{8,10},{9,11},{10,... | collective-permute-start | bytes 98312 | tf_op jit(solution)/shard_map/ppermute | solution.py:21
  35.1 1.5 %collective-permute-start.14 = (bf16[1024,128]{1,0:T(8,128)(2,1)S(1)}, bf16[1024,128]{1,0:T(8,128)(2,1)S(1)}, u32[]{:S(2)}, u32[]{:S(2)}) collective-permute-start(bf16[1024,128]{1,0:T(8,128)(2,1)S(1)} %collective-permute-done.11.refs_8_), channel_id=1, source_target_pairs={{0,1},{1,0},{2,3},{3,2},{4,5},{5,4},{6,7},{7,6},{8,9},{9,8},{10,11... | collective-permute-start | bytes 786440 | tf_op jit(solution)/shard_map/ppermute | solution.py:21
  35.1 1.9 %collective-permute-start.13 = (bf16[1024,128]{1,0:T(8,128)(2,1)S(1)}, bf16[1024,128]{1,0:T(8,128)(2,1)S(1)}, u32[]{:S(2)}, u32[]{:S(2)}) collective-permute-start(bf16[1024,128]{1,0:T(8,128)(2,1)S(1)} %get-tuple-element.45.order_ref.refs_7_), channel_id=1, source_target_pairs={{0,1},{1,0},{2,3},{3,2},{4,5},{5,4},{6,7},{7,6},{8,9},{9,8},{10,11... | collective-permute-start | bytes 786440 | tf_op jit(solution)/shard_map/ppermute | solution.py:21
  37.1 18.6 %copy-start.4 = (bf16[256,3,64]{0,2,1:T(8,128)(2,1)S(1)}, bf16[256,3,64]{0,2,1:T(8,128)(2,1)}, u32[]{:S(2)}) copy-start(bf16[256,3,64]{0,2,1:T(8,128)(2,1)} %param.21) | copy-start | bytes 294916
  37.1 18.6 %copy-start.6 = (f32[256]{0:T(256)S(1)}, f32[256]{0:T(256)}, u32[]{:S(2)}) copy-start(f32[256]{0:T(256)} %param.20) | copy-start | bytes 3076
  39.5 2.1 %collective-permute-start.16 = (f32[8,256]{1,0:T(8,128)S(1)}, f32[8,256]{1,0:T(8,128)S(1)}, u32[]{:S(2)}, u32[]{:S(2)}) collective-permute-start(f32[8,256]{1,0:T(8,128)S(1)} %shard_map.113), channel_id=1, source_target_pairs={{0,1},{1,0},{2,3},{3,2},{4,5},{5,4},{6,7},{7,6},{8,9},{9,8},{10,11... | collective-permute-start | bytes 24584 | tf_op jit(solution)/shard_map/ppermute | solution.py:21
  39.7 3.7 %collective-permute-start.17 = (f32[8,256]{1,0:T(8,128)S(1)}, f32[8,256]{1,0:T(8,128)S(1)}, u32[]{:S(2)}, u32[]{:S(2)}) collective-permute-start(f32[8,256]{1,0:T(8,128)S(1)} %shard_map.113), channel_id=1, source_target_pairs={{0,2},{1,3},{2,0},{3,1},{4,6},{5,7},{6,4},{7,5},{8,10},{9,11},{10,... | collective-permute-start | bytes 24584 | tf_op jit(solution)/shard_map/ppermute | solution.py:21
  40.3 3.2 %collective-permute-start.18 = (f32[8,256]{1,0:T(8,128)S(1)}, f32[8,256]{1,0:T(8,128)S(1)}, u32[]{:S(2)}, u32[]{:S(2)}) collective-permute-start(f32[8,256]{1,0:T(8,128)S(1)} %shard_map.113), channel_id=1, source_target_pairs={{0,3},{1,2},{2,1},{3,0},{4,7},{5,6},{6,5},{7,4},{8,11},{9,10},{10,... | collective-permute-start | bytes 24584 | tf_op jit(solution)/shard_map/ppermute | solution.py:21
  43.4 4.6 %collective-permute-start.19 = (f32[8,256]{1,0:T(8,128)S(1)}, f32[8,256]{1,0:T(8,128)S(1)}, u32[]{:S(2)}, u32[]{:S(2)}) collective-permute-start(f32[8,256]{1,0:T(8,128)S(1)} %add_add_fusion), channel_id=1, source_target_pairs={{0,16},{4,20},{8,24},{12,28},{16,0},{20,4},{24,8},{28,12},{1,17},{... | collective-permute-start | bytes 24584 | tf_op jit(solution)/shard_map/ppermute | solution.py:21
  48.0 3.7 %collective-permute-start.20 = (f32[16,256]{1,0:T(8,128)S(1)}, f32[16,256]{1,0:T(8,128)S(1)}, u32[]{:S(2)}, u32[]{:S(2)}) collective-permute-start(f32[16,256]{1,0:T(8,128)S(1)} %pad_maximum_fusion.2), channel_id=1, source_target_pairs={{0,8},{4,12},{8,0},{12,4},{16,24},{20,28},{24,16},{28,20},{1,9},{5... | collective-permute-start | bytes 49160 | tf_op jit(solution)/shard_map/ppermute | solution.py:21
  51.8 3.9 %collective-permute-start.21 = (f32[32,256]{1,0:T(8,128)S(1)}, f32[32,256]{1,0:T(8,128)S(1)}, u32[]{:S(2)}, u32[]{:S(2)}) collective-permute-start(f32[32,256]{1,0:T(8,128)S(1)} %pad_maximum_fusion.1.near_ref), channel_id=1, source_target_pairs={{0,4},{4,0},{8,12},{12,8},{16,20},{20,16},{24,28},{28,24},{1,5},{5... | collective-permute-start | bytes 98312 | tf_op jit(solution)/shard_map/ppermute | solution.py:21
  (9 other events, 56.9 us)
